TPU v7x, 256 devices: a whole 4x4x8 slice. The times are simulated.
256 devices in a mesh: row: 32 (over x, y, core), col: 8 (over z).
Axes of the slice: x: 4, y: 4, z: 8, core: 2. Of those that a mesh axis runs over, the one named last changes fastest.
Arguments:
- kernel: float32 [3, 4096, 12, 1024], P(None, 'row', None, 'col'), as said below
Outputs:
- factored: float32 [3, 4096, 12, 1024], P(None, 'row', None, 'col')
Inputs may be any that keep to these rules, and one draw needn't show every extreme that they name: kernel read as an 12288 x 12288 matrix is symmetric positive definite.
All inputs are finite; a program needn't handle non-finite values.
Results may differ from a plain program's by a relative error of at most 0.0003.
Values sent between devices are 32-bit elements; how exact they have to be, the bound alone decides.
No kernel may reach another device: no remote copies, remote signals or barrier semaphores. Data moves between devices by JAX's collectives and lax.ppermute only.
A program may use at most 64 MiB of HBM per device.

v0:
```python
import jax
import jax.numpy as jnp
from jax import lax
from jax.sharding import PartitionSpec as P

PANEL = 512


HIGHEST = lax.Precision.HIGHEST


def spread_2(block, axis, source):
    block = jnp.where(lax.axis_index(axis) == source, block, jnp.zeros_like(block))
    return lax.psum(block, axis)


def factor_panel(current, column_start, row_glob):
    tile_edge = current.shape[1]
    blocks = PANEL // tile_edge
    tile_index = column_start // tile_edge
    local_col = tile_index // lax.axis_size("col")
    column_piece = current[:, :, local_col, :]
    gathered = lax.all_gather(column_piece, "col", axis=2, tiled=True)
    offset = tile_index % lax.axis_size("col") * tile_edge
    panel_rows = gathered[:, :, offset : offset + PANEL]
    local_row = tile_index // lax.axis_size("row")
    first_row = tile_index % lax.axis_size("row")
    select = (jnp.arange(blocks) == lax.axis_index("row") - first_row).astype(jnp.float32)
    placed = select[:, None, None] * panel_rows[local_row][None, :, :]
    diagonal_block = lax.psum(placed.reshape(PANEL, PANEL), "row")
    lower_factor = jnp.linalg.cholesky(diagonal_block)
    inverse_factor = lax.linalg.triangular_solve(
        lower_factor, jnp.eye(PANEL, dtype=jnp.float32), left_side=True, lower=True
    )
    flattened = panel_rows.reshape(-1, PANEL)
    solved = jnp.dot(flattened, inverse_factor.T, precision=HIGHEST)
    solved = solved.reshape(panel_rows.shape)
    own_block = jnp.sum(
        select[:, None, None] * lower_factor.reshape(blocks, tile_edge, PANEL), axis=0
    )
    factor = jnp.where((row_glob >= column_start + PANEL)[:, :, None], solved, 0.0)
    inside = jnp.sum(select) > 0.0
    return factor.at[local_row].set(jnp.where(inside, own_block, factor[local_row]))


def spread_columns(factor):
    groups = lax.axis_size("row") // lax.axis_size("col")
    col_id = lax.axis_index("col")
    received = []
    for member in range(groups):
        received.append(spread_2(factor, "row", col_id + member * lax.axis_size("col")))
    stacked = jnp.stack(received, 1)
    return stacked.reshape(-1, factor.shape[1], factor.shape[2])


def apply_update(current, row_glob, col_glob, left_rows, right_rows, bound):
    product = jnp.dot(
        left_rows.reshape(-1, left_rows.shape[-1]),
        right_rows.reshape(-1, right_rows.shape[-1]).T,
        precision=HIGHEST,
    )
    product = product.reshape(current.shape)
    row_keep = (row_glob >= bound)[:, :, None, None]
    col_keep = (col_glob >= bound)[None, None, :, :]
    return jnp.where(col_keep, jnp.where(row_keep, current - product, 0.0), current)


def place_panel(current, factor, column_start):
    tile_edge = current.shape[1]
    blocks = PANEL // tile_edge
    tile_index = column_start // tile_edge
    local_col = tile_index // lax.axis_size("col")
    first_col = tile_index % lax.axis_size("col")
    select = jnp.arange(blocks) == lax.axis_index("col") - first_col
    pieces = factor.reshape(factor.shape[0], tile_edge, blocks, tile_edge)
    chosen = jnp.sum(jnp.where(select[None, None, :, None], pieces, 0.0), axis=2)
    inside = jnp.any(select)
    return current.at[:, :, local_col, :].set(
        jnp.where(inside, chosen, current[:, :, local_col, :])
    )


def body(kernel):
    tile_rows, tile_edge, tile_cols, _ = kernel.shape
    row_glob = (
        jnp.arange(tile_rows)[:, None] * lax.axis_size("row") + lax.axis_index("row")
    ) * tile_edge + jnp.arange(tile_edge)[None, :]
    col_glob = (
        jnp.arange(tile_cols)[:, None] * lax.axis_size("col") + lax.axis_index("col")
    ) * tile_edge + jnp.arange(tile_edge)[None, :]
    current = kernel
    for number in range(2):
        column_start = number * PANEL
        factor = factor_panel(current, column_start, row_glob)
        spread = spread_columns(factor)
        current = apply_update(current, row_glob, col_glob, factor, spread, column_start + PANEL)
        current = place_panel(current, factor, column_start)
    return current


def solution(mesh):
    placed = (P(None, "row", None, "col"),)
    return jax.shard_map(
        body, mesh=mesh, in_specs=placed, out_specs=P(None, "row", None, "col"), check_vma=False
    )
```

profile of v0, /device:TPU:1, one launch (start us, length us, event | category | flops | bytes accessed | tf_op | source)
XLA Modules:
  0.0 932.8 jit_solution(10427412958186857350)
XLA Ops:
  8.3 44.4 %all-gather.6.cloned.1.call-done = f32[3,128,1,1024]{3,1,2,0:T(8,128)} async-done(((f32[3,128,1,128]{3,1,2,0:T(8,128)}), f32[3,128,1,1024]{3,1,2,0:T(8,128)}) %all-gather.6.cloned.1.call-update) | async-done | bytes 1572880 | tf_op jit(solution)/shard_map/all_gather | solution.py:23
  57.7 115.8 %all-reduce.8.cloned.1.call-done = f32[512,512]{0,1:T(8,128)} async-done(((f32[512,512]{0,1:T(8,128)}), f32[512,512]{0,1:T(8,128)}) %all-reduce.8.cloned.1.call-update) | async-done | bytes 1048592 | tf_op jit(solution)/shard_map/psum | solution.py:30
  176.4 11.7 %cholesky.286 = f32[128,128]{1,0:T(8,128)S(1)} custom-call(f32[128,128]{1,0:T(8,128)S(1)} %cholesky.426), custom_call_target="Cholesky" | custom-call | tf_op jit(solution)/shard_map/jit(cholesky)/cholesky | solution.py:31
  188.3 9.8 %custom-call.27 = f32[1,128,128]{1,2,0:T(8,128)S(1)} custom-call(f32[1,128,128]{2,1,0:T(8,128)S(1)} %get-tuple-element.130), custom_call_target="InvertDiagBlocksLowerTriangular" | custom-call | tf_op jit(solution)/shard_map/jit(cholesky)/cholesky | solution.py:31
  200.6 11.7 %cholesky.305 = f32[128,128]{1,0:T(8,128)S(1)} custom-call(f32[128,128]{1,0:T(8,128)S(1)} %cholesky.430), custom_call_target="Cholesky" | custom-call | tf_op jit(solution)/shard_map/jit(cholesky)/cholesky | solution.py:31
  212.3 10.0 %custom-call.28 = f32[1,128,128]{1,2,0:T(8,128)S(1)} custom-call(f32[1,128,128]{2,1,0:T(8,128)S(1)} %get-tuple-element.127), custom_call_target="InvertDiagBlocksLowerTriangular" | custom-call | tf_op jit(solution)/shard_map/jit(cholesky)/cholesky | solution.py:31
  224.0 11.7 %cholesky.326 = f32[128,128]{1,0:T(8,128)S(1)} custom-call(f32[128,128]{1,0:T(8,128)S(1)} %cholesky.435), custom_call_target="Cholesky" | custom-call | tf_op jit(solution)/shard_map/jit(cholesky)/cholesky | solution.py:31
  235.7 9.8 %custom-call.29 = f32[1,128,128]{1,2,0:T(8,128)S(1)} custom-call(f32[1,128,128]{2,1,0:T(8,128)S(1)} %get-tuple-element.124), custom_call_target="InvertDiagBlocksLowerTriangular" | custom-call | tf_op jit(solution)/shard_map/jit(cholesky)/cholesky | solution.py:31
  247.0 11.7 %cholesky.343 = f32[128,128]{1,0:T(8,128)S(1)} custom-call(f32[128,128]{1,0:T(8,128)S(1)} %convolution_subtract_fusion.11), custom_call_target="Cholesky" | custom-call | tf_op jit(solution)/shard_map/jit(cholesky)/cholesky | solution.py:31
  273.9 11.4 %while.8 = (s32[]{:T(128)}, f32[512,512]{1,0:T(8,128)}, s32[4,2]{0,1:T(2,128)S(1)}, f32[4,128,128]{2,1,0:T(8,128)S(1)}, s32[]{:T(128)}) while((s32[]{:T(128)}, f32[512,512]{1,0:T(8,128)}, s32[4,2]{0,1:T(2,128)S(1)}, f32[4,128,128]{2,1,0:T(8,128)S(1)}, s32[]{:T(128)}) %tuple.79), condition=%wide.while_cond.4, body=%wide.while_body.4.sunk | while | flops 2 | bytes 131189 | solution.py:32
  285.2 39.3 %custom-call.30 = f32[4,128,128]{1,2,0:T(8,128)S(1)} custom-call(f32[4,128,128]{2,1,0:T(8,128)S(1)} %get-tuple-element.69), custom_call_target="InvertDiagBlocksLowerTriangular" | custom-call | tf_op jit(solution)/shard_map/triangular_solve/custom-call.3 | solution.py:32
  335.9 118.3 %all-reduce.14.cloned.1.call-done = (f32[3,1,128,512]{3,2,0,1:T(8,128)}, f32[3,1,128,512]{3,2,0,1:T(8,128)}, f32[3,1,128,512]{3,2,0,1:T(8,128)}, f32[3,1,128,512]{3,2,0,1:T(8,128)}) async-done(((f32[3,1,128,512]{3,2,0,1:T(8,128)}, f32[3,1,128,512]{3,2,0,1:T(8,128)}, f32[3,1,128,512]{3,2,0,1:T(8,128)}, f32[3,1,128,512]{3,2,0,1:T(8,128)}), (f32[3,1,128,512]{3,2,0,1:T(8,128)}, f32[3,1,128,512]{3,2,0,1:T(8,128)}, ...) | async-done | bytes 3145744 | tf_op jit(solution)/shard_map/psum | solution.py:14
  458.0 4.2 select_select_fusion.1
  463.7 39.6 %all-gather.4.cloned.1.call-done = f32[3,128,1024]{2,1,0:T(8,128)} async-done(((f32[3,128,128]{2,1,0:T(8,128)}), f32[3,128,1024]{2,1,0:T(8,128)}) %all-gather.4.cloned.1.call-update) | async-done | bytes 1572880 | tf_op jit(solution)/shard_map/all_gather | solution.py:23
  507.3 117.0 %all-reduce.10.cloned.1.call-done = f32[512,512]{0,1:T(8,128)} async-done(((f32[512,512]{0,1:T(8,128)}), f32[512,512]{0,1:T(8,128)}) %all-reduce.10.cloned.1.call-update) | async-done | bytes 1048592 | tf_op jit(solution)/shard_map/psum | solution.py:30
  624.4 2.6 copy.13
  629.4 11.7 %cholesky.358 = f32[128,128]{1,0:T(8,128)S(1)} custom-call(f32[128,128]{1,0:T(8,128)S(1)} %cholesky.439), custom_call_target="Cholesky" | custom-call | tf_op jit(solution)/shard_map/jit(cholesky)/cholesky | solution.py:31
  642.9 9.8 %custom-call.31 = f32[1,128,128]{1,2,0:T(8,128)S(1)} custom-call(f32[1,128,128]{2,1,0:T(8,128)S(1)} %get-tuple-element.120), custom_call_target="InvertDiagBlocksLowerTriangular" | custom-call | tf_op jit(solution)/shard_map/jit(cholesky)/cholesky | solution.py:31
  655.9 11.7 %cholesky.377 = f32[128,128]{1,0:T(8,128)S(1)} custom-call(f32[128,128]{1,0:T(8,128)S(1)} %cholesky.443), custom_call_target="Cholesky" | custom-call | tf_op jit(solution)/shard_map/jit(cholesky)/cholesky | solution.py:31
  668.8 9.9 %custom-call.32 = f32[1,128,128]{1,2,0:T(8,128)S(1)} custom-call(f32[1,128,128]{2,1,0:T(8,128)S(1)} %get-tuple-element.117), custom_call_target="InvertDiagBlocksLowerTriangular" | custom-call | tf_op jit(solution)/shard_map/jit(cholesky)/cholesky | solution.py:31
  681.1 11.7 %cholesky.398 = f32[128,128]{1,0:T(8,128)S(1)} custom-call(f32[128,128]{1,0:T(8,128)S(1)} %cholesky.448), custom_call_target="Cholesky" | custom-call | tf_op jit(solution)/shard_map/jit(cholesky)/cholesky | solution.py:31
  694.0 9.8 %custom-call.33 = f32[1,128,128]{1,2,0:T(8,128)S(1)} custom-call(f32[1,128,128]{2,1,0:T(8,128)S(1)} %get-tuple-element.114), custom_call_target="InvertDiagBlocksLowerTriangular" | custom-call | tf_op jit(solution)/shard_map/jit(cholesky)/cholesky | solution.py:31
  706.2 11.7 %cholesky.415 = f32[128,128]{1,0:T(8,128)S(1)} custom-call(f32[128,128]{1,0:T(8,128)S(1)} %convolution_subtract_fusion.10), custom_call_target="Cholesky" | custom-call | tf_op jit(solution)/shard_map/jit(cholesky)/cholesky | solution.py:31
  725.8 2.8 fusion.16
  729.4 13.9 %while.9 = (s32[]{:T(128)}, f32[512,512]{1,0:T(8,128)}, s32[4,2]{0,1:T(2,128)S(1)}, f32[4,128,128]{2,1,0:T(8,128)}, s32[]{:T(128)}) while((s32[]{:T(128)}, f32[512,512]{1,0:T(8,128)}, s32[4,2]{0,1:T(2,128)S(1)}, f32[4,128,128]{2,1,0:T(8,128)}, s32[]{:T(128)}) %tuple.99), condition=%wide.while_cond.4.clone, body=%wide.while_body.4.clone.sunk | while | flops 2 | bytes 132205 | solution.py:32
  730.0 2.9 bitcast_dynamic-update-slice_fusion.5
  733.5 2.9 bitcast_dynamic-update-slice_fusion.5
  736.9 2.9 bitcast_dynamic-update-slice_fusion.5
  740.4 2.8 bitcast_dynamic-update-slice_fusion.5
  743.2 40.7 %custom-call.34 = f32[4,128,128]{1,2,0:T(8,128)} custom-call(f32[4,128,128]{2,1,0:T(8,128)} %get-tuple-element.70), custom_call_target="InvertDiagBlocksLowerTriangular" | custom-call | tf_op jit(solution)/shard_map/triangular_solve/custom-call.3 | solution.py:32
  799.9 115.5 %all-reduce.12.cloned.1.call-done = (f32[3,1,128,512]{3,2,0,1:T(8,128)}, f32[3,1,128,512]{3,2,0,1:T(8,128)}, f32[3,1,128,512]{3,2,0,1:T(8,128)}, f32[3,1,128,512]{3,2,0,1:T(8,128)}) async-done(((f32[3,1,128,512]{3,2,0,1:T(8,128)}, f32[3,1,128,512]{3,2,0,1:T(8,128)}, f32[3,1,128,512]{3,2,0,1:T(8,128)}, f32[3,1,128,512]{3,2,0,1:T(8,128)}), (f32[3,1,128,512]{3,2,0,1:T(8,128)}, f32[3,1,128,512]{3,2,0,1:T(8,128)}, ...) | async-done | bytes 3145744 | tf_op jit(solution)/shard_map/psum | solution.py:14
  917.8 5.5 select_select_fusion
  (160 shorter events, 92.5 us)
Async XLA Ops:
  6.5 46.1 %all-gather.6.cloned.1.call-start = ((), (), s32[]{:S(2)}) async-start(), calls=%async_computation.3 | async-start | bytes 1769472 | tf_op jit(solution)/shard_map/all_gather | solution.py:23
  8.2 165.3 %all-reduce.8.cloned.1.call-start = ((), (), s32[]{:S(2)}) async-start(), calls=%async_computation | async-start | bytes 2097152 | tf_op jit(solution)/shard_map/psum | solution.py:30
  54.0 2.6 copy-start.11
  55.1 399.1 %all-reduce.14.cloned.1.call-start = ((), (), s32[]{:S(2)}) async-start(), calls=%async_computation.5 | async-start | bytes 6291456 | tf_op jit(solution)/shard_map/psum | solution.py:14
  56.5 272.0 %copy-start = (f32[512,512]{1,0:T(8,128)}, f32[512,512]{1,0:T(8,128)S(1)}, u32[]{:S(2)}) copy-start(f32[512,512]{1,0:T(8,128)S(1)} %fusion.19) | copy-start | bytes 3145732
  173.5 1.7 copy-start.2
  175.4 1.0 copy-start.7
  326.6 4.0 copy-start.5
  334.1 169.2 %all-gather.4.cloned.1.call-start = ((), (), s32[]{:S(2)}) async-start(), calls=%async_computation.1 | async-start | bytes 1769472 | tf_op jit(solution)/shard_map/all_gather | solution.py:23
  335.8 126.3 %copy-start.9 = (f32[3,128,128]{2,1,0:T(8,128)}, f32[3,128,128]{2,1,0:T(8,128)S(1)}, u32[]{:S(2)}) copy-start(f32[3,128,128]{2,1,0:T(8,128)S(1)} %select_reduce_fusion.1) | copy-start | bytes 589828
  456.3 1.7 copy-start.6
  463.6 160.8 %all-reduce.10.cloned.1.call-start = ((), (), s32[]{:S(2)}) async-start(), calls=%async_computation.2 | async-start | bytes 2097152 | tf_op jit(solution)/shard_map/psum | solution.py:30
  505.7 409.6 %all-reduce.12.cloned.1.call-start = ((), (), s32[]{:S(2)}) async-start(), calls=%async_computation.4 | async-start | bytes 6291456 | tf_op jit(solution)/shard_map/psum | solution.py:14
  624.4 2.6 copy-start.3
  628.4 1.0 copy-start.8
  704.6 79.3 %copy-start.1 = (f32[512,512]{1,0:T(8,128)S(1)}, f32[512,512]{1,0:T(8,128)}, u32[]{:S(2)}) copy-start(f32[512,512]{1,0:T(8,128)} %copy-done) | copy-start | bytes 3145732
  784.0 5.4 copy-start.12
  786.5 5.3 copy-start.4
  787.9 4.1 copy-start.13
  795.3 0.9 copy-start.10
Sparse Core Ops, SparseCore 0:
  9.1 43.5 all-gather.5
  55.9 117.5 all-reduce.7
  334.3 119.8 all-reduce.13
  463.7 39.5 all-gather.3
  506.7 117.5 all-reduce.9
  795.4 119.8 all-reduce.11
where the time goes:
time: 943 us; the launch traced here: 933 us
  waiting for transfers between devices  551 us (58%)
  other arithmetic  269 us (29%)
  local copies, waits for them, and re-layouts  42.5 us (5%)
  matrix products  39.5 us (4%)
  between operations  30.1 us (3%)
    psum x2, waiting for transfers between devices, spread_2(): return lax.psum(block, axis)  234 us
    psum x2, waiting for transfers between devices, factor_panel(): diagonal_block = lax.psum(placed.reshape(PANEL, PANEL), 'row')  233 us
    another operation x29, other arithmetic, factor_panel(): lower_factor = jnp.linalg.cholesky(diagonal_block)  163 us
    another operation x5, other arithmetic, factor_panel(): lax.linalg.triangular_solve(lower_factor, jnp.eye(PANEL, dtype=jnp.float3...  84.1 us
    all_gather x2, waiting for transfers between devices, factor_panel(): gathered = lax.all_gather(column_piece, 'col', axis=2, tiled=True)  84 us
    another operation x27, local copies, waits for them, and re-layouts, factor_panel(): lax.linalg.triangular_solve(lower_factor, jnp.eye(PANEL, dtype=jnp.float3...  25.9 us
  transfers between devices with their start and end apart: 6, of which 6 were waited for; matrix products, arithmetic and copies ran while one was open for 1% of the time, Pallas kernels for 0%

commit v1 on v0

v1 whole, which is shorter than its diff:
```python
import jax
import jax.numpy as jnp
from jax import lax
from jax.experimental import pallas as pl
from jax.experimental.pallas import tpu as pltpu
from jax.sharding import Mesh
from jax.sharding import PartitionSpec as P

TILE = 128
TILES = 8
WIDTH = TILE * TILES
HIGHEST = lax.Precision.HIGHEST
ROW = ("x", "y", "k")


def factor_tile(a_ref, v_ref):
    sub = lax.broadcasted_iota(jnp.int32, (8, TILE), 0)
    lane = lax.broadcasted_iota(jnp.int32, (8, TILE), 1)
    for t in range(TILE // 8):
        n = TILE // 8 - t
        rows = [slice(8 * (t + q), 8 * (t + q) + 8) for q in range(n)]
        a = [a_ref[s, :] for s in rows]
        if t == 0:
            v = [jnp.where(lane == sub + 8 * q, 1.0, 0.0) for q in range(n)]
        else:
            v = [v_ref[s, :] for s in rows]
        cols = [
            [jnp.broadcast_to(a[q][:, 8 * t + l : 8 * t + l + 1], (8, TILE)) for q in range(n)]
            for l in range(8)
        ]
        for j in range(8):
            pivot = jnp.broadcast_to(cols[j][0][j : j + 1, :], (8, TILE))
            inverse = 1.0 / pivot
            m = [cols[j][q] * inverse for q in range(n)]
            m[0] = jnp.where(sub > j, m[0], 0.0)
            for l in range(j + 1, 8):
                e = jnp.broadcast_to(cols[l][0][j : j + 1, :], (8, TILE))
                cols[l] = [cols[l][q] - m[q] * e for q in range(n)]
            ra = jnp.broadcast_to(a[0][j : j + 1, :], (8, TILE))
            a = [a[q] - m[q] * ra for q in range(n)]
            rv = jnp.broadcast_to(v[0][j : j + 1, :], (8, TILE))
            v = [v[q] - m[q] * rv for q in range(n)]
        pivots = cols[0][0]
        for j in range(1, 8):
            pivots = jnp.where(sub == j, cols[j][0], pivots)
        scale = lax.rsqrt(pivots)
        a[0] = jnp.where(lane >= sub + 8 * t, a[0] * scale, 0.0)
        v[0] = v[0] * scale
        for q in range(n):
            a_ref[rows[q], :] = a[q]
            v_ref[rows[q], :] = v[q]


def factor_kernel(x_ref, w_ref, u_ref, a_ref, v_ref):
    w_ref[...] = x_ref[...]

    def step(k, _):
        ks = pl.ds(pl.multiple_of(k * TILE, TILE), TILE)
        a_ref[...] = w_ref[ks, ks]
        factor_tile(a_ref, v_ref)
        u_ref[k] = a_ref[...]
        w_ref[ks, :] = jnp.dot(
            v_ref[...], w_ref[ks, :], precision=HIGHEST, preferred_element_type=jnp.float32
        )
        w_ref[ks, ks] = v_ref[...]

        def update(i, _):
            rows = pl.ds(pl.multiple_of(i * TILE, TILE), TILE)
            w_ref[rows, ks] = jnp.zeros((TILE, TILE), jnp.float32)
            w_ref[rows, :] -= lax.dot_general(
                w_ref[ks, rows],
                w_ref[ks, :],
                (((0,), (0,)), ((), ())),
                precision=HIGHEST,
                preferred_element_type=jnp.float32,
            )
            return 0

        lax.fori_loop(k + 1, TILES, update, 0)
        return 0

    lax.fori_loop(0, TILES, step, 0)


def factor(block):
    return pl.pallas_call(
        factor_kernel,
        out_shape=[
            jax.ShapeDtypeStruct((WIDTH, WIDTH), jnp.float32),
            jax.ShapeDtypeStruct((TILES, TILE, TILE), jnp.float32),
        ],
        scratch_shapes=[pltpu.VMEM((TILE, TILE), jnp.float32)] * 2,
        compiler_params=pltpu.CompilerParams(vmem_limit_bytes=40 << 20),
    )(block)


def spread_x(block):
    x = lax.axis_index("x")
    out = block
    for d in (1, 3, 2):
        out = jnp.where(x == d, lax.ppermute(block, "x", [(0, d)]), out)
    return out


def gather_z(block):
    n = lax.axis_size("z")
    me = lax.axis_index("z")
    parts = [block] + [
        lax.ppermute(block, "z", [((i + d) % n, i) for i in range(n)]) for d in range(1, n)
    ]
    rolled = jnp.concatenate(parts + parts, 0)
    return lax.dynamic_slice_in_dim(rolled, ((n - me) % n) * TILE, n * TILE, 0)


def body(kernel):
    row = lax.axis_index(ROW)
    col = lax.axis_index("z")
    strip = gather_z(spread_x(kernel[0, :, 0, :]).T)
    block = lax.all_gather(strip, ("y", "k"), axis=1, tiled=True)
    own = lax.all_gather(kernel[:, :, 0, :], "z", axis=2, tiled=True)
    head = spread_x(kernel[0, :, 1:, :].reshape(TILE, -1))
    right = lax.all_gather(head, ("y", "k"), axis=0, tiled=True)

    w, u = factor(block)
    tile = jnp.arange(WIDTH) // TILE
    linv = jnp.where(tile[:, None] >= tile[None, :], w, 0.0)
    solved = jnp.dot(own.reshape(-1, WIDTH), linv.T, precision=HIGHEST)
    twice = jnp.dot(solved, linv, precision=HIGHEST)
    product = jnp.dot(twice, right, precision=HIGHEST)
    product = product.reshape(3, TILE, 11, TILE)
    inside = row < TILES
    dead = (inside & (jnp.arange(3) == 0))[:, None, None, None]
    rest = jnp.where(dead, 0.0, kernel[:, :, 1:, :] - product)

    column = lax.dynamic_index_in_dim(solved.reshape(3, TILE, TILES, TILE), col, 2, False)
    low = lax.dynamic_slice(w, (col * TILE, row * TILE), (TILE, TILE))
    low = jnp.where(col == row, lax.dynamic_index_in_dim(u, col, 0, False), low).T
    low = jnp.where(col <= row, low, 0.0)
    column = jnp.where(dead[:, :, :, 0], low[None], column)
    return jnp.concatenate([column[:, :, None, :], rest], 2)


def solution(mesh):
    fine = Mesh(mesh.devices.reshape(4, 4, 2, 8), ("x", "y", "k", "z"))
    spec = P(None, ROW, None, "z")
    return jax.shard_map(body, mesh=fine, in_specs=(spec,), out_specs=spec, check_vma=False)
```

time: 943 us -> 200 us (0.21); the launches traced: 933 us -> 200 us
  waiting for transfers between devices: 551 us -> 47.4 us
  other arithmetic: 269 us -> 5.67 us
  Pallas kernels: 0 us -> 55.2 us
  starting transfers between devices: 0.62 us -> 28.5 us
  local copies, waits for them, and re-layouts: 42.5 us -> 19.3 us
  between operations: 30.1 us -> 13.4 us
    psum x4 -> x0, waiting for transfers between devices: 467 us -> none  [the longest x2 234 us: spread_2(): return lax.psum(block, axis)]
    another operation x38 -> x0, other arithmetic: 255 us -> none  [the longest x29 163 us: factor_panel(): lower_factor = jnp.linalg.cholesky(diagonal_block)]
    all_gather x2 -> x3, waiting for transfers between devices: 84 us -> 12.4 us  [the longest x1 12.4 us: body(): right = lax.all_gather(head, ('y', 'k'), axis=0, tiled=True)]
    pallas_call x0 -> x1, Pallas kernels: none -> 55.2 us  [factor(): pl.pallas_call(factor_kernel, out_shape=[jax.ShapeDtypeStruct((WIDTH, WID...]
    ppermute x0 -> x13, waiting for transfers between devices: none -> 34.9 us  [the longest x6 26 us: spread_x(): out = jnp.where(x == d, lax.ppermute(block, 'x', [(0, d)]), out)]
    ppermute x0 -> x13, starting transfers between devices: none -> 28.5 us  [the longest x7 15.4 us: gather_z(): lax.ppermute(block, 'z', [((i + d) % n, i) for i in range(n)])]
    another operation x37 -> x0, local copies, waits for them, and re-layouts: 27.7 us -> none  [the longest x27 25.9 us: factor_panel(): lax.linalg.triangular_solve(lower_factor, jnp.eye(PANEL, dtype=jnp.float3...]
    another operation x26 -> x0, matrix products: 26.9 us -> none  [the longest x14 13.6 us: factor_panel(): lax.linalg.triangular_solve(lower_factor, jnp.eye(PANEL, dtype=jnp.float3...]
  transfers between devices with their start and end apart: 6 -> 16, of which waited for: 6 -> 8; matrix products, arithmetic and copies ran while one was open for 1% -> 14% of each run, Pallas kernels for 0% -> 28%
where the time goes in v1:
time: 200 us
  Pallas kernels  55.2 us (28%)
  waiting for transfers between devices  47.4 us (24%)
  matrix products  30.3 us (15%)
  starting transfers between devices  28.5 us (14%)
  local copies, waits for them, and re-layouts  19.3 us (10%)
  between operations  13.4 us (7%)
  other arithmetic  5.67 us (3%)
    pallas_call x1, Pallas kernels, factor(): pl.pallas_call(factor_kernel, out_shape=[jax.ShapeDtypeStruct((WIDTH, WID...  55.2 us
    ppermute x6, waiting for transfers between devices, spread_x(): out = jnp.where(x == d, lax.ppermute(block, 'x', [(0, d)]), out)  26 us
    ppermute x7, starting transfers between devices, gather_z(): lax.ppermute(block, 'z', [((i + d) % n, i) for i in range(n)])  15.4 us
    ppermute x6, starting transfers between devices, spread_x(): out = jnp.where(x == d, lax.ppermute(block, 'x', [(0, d)]), out)  13.1 us
    all_gather x1, waiting for transfers between devices, body(): right = lax.all_gather(head, ('y', 'k'), axis=0, tiled=True)  12.4 us
    dot_general x1, matrix products, body(): product = jnp.dot(twice, right, precision=HIGHEST)  11.6 us
    dot_general x1, matrix products, body(): solved = jnp.dot(own.reshape(-1, WIDTH), linv.T, precision=HIGHEST)  9.35 us
    dot_general x1, matrix products, body(): twice = jnp.dot(solved, linv, precision=HIGHEST)  9.33 us
  transfers between devices with their start and end apart: 16, of which 8 were waited for; matrix products, arithmetic and copies ran while one was open for 14% of the time, Pallas kernels for 28%

profile of v1, /device:TPU:1, one launch (start us, length us, event | category | flops | bytes accessed | tf_op | source)
XLA Modules:
  0.0 199.9 jit_solution(12911021448730334150)
XLA Ops:
  7.5 5.5 %collective-permute-start = (f32[128,128]{0,1:T(8,128)S(1)}, f32[128,128]{0,1:T(8,128)S(1)}, u32[]{:S(2)}, u32[]{:S(2)}) collective-permute-start(f32[128,128]{0,1:T(8,128)S(1)} %bitcast.34), channel_id=1, source_target_pairs={{0,128},{1,129},{2,130},{3,131},{4,132},{5,133},{6,134},{7,135},{8... | collective-permute-start | bytes 196616 | tf_op jit(solution)/shard_map/ppermute | solution.py:101
  13.0 1.3 collective-permute-start.1
  14.3 1.3 collective-permute-start.2
  15.6 1.3 collective-permute-done.2
  16.9 5.7 %collective-permute-start.3 = (f32[128,128]{1,0:T(8,128)S(1)}, f32[128,128]{1,0:T(8,128)S(1)}, u32[]{:S(2)}, u32[]{:S(2)}) collective-permute-start(f32[128,128]{1,0:T(8,128)S(1)} %get-tuple-element.10), channel_id=1, source_target_pairs={{1,0},{2,1},{3,2},{4,3},{5,4},{6,5},{7,6},{0,7},{9,8},{10,9},{11,1... | collective-permute-start | bytes 196616 | tf_op jit(solution)/shard_map/ppermute | solution.py:109
  22.6 1.2 collective-permute-start.4
  24.2 4.5 %collective-permute-start.6 = (f32[128,128]{1,0:T(8,128)S(1)}, f32[128,128]{1,0:T(8,128)S(1)}, u32[]{:S(2)}, u32[]{:S(2)}) collective-permute-start(f32[128,128]{1,0:T(8,128)S(1)} %get-tuple-element.10), channel_id=1, source_target_pairs={{4,0},{5,1},{6,2},{7,3},{0,4},{1,5},{2,6},{3,7},{12,8},{13,9},{14,... | collective-permute-start | bytes 196616 | tf_op jit(solution)/shard_map/ppermute | solution.py:109
  28.7 2.2 %collective-permute-start.8 = (f32[128,128]{1,0:T(8,128)S(1)}, f32[128,128]{1,0:T(8,128)S(1)}, u32[]{:S(2)}, u32[]{:S(2)}) collective-permute-start(f32[128,128]{1,0:T(8,128)S(1)} %get-tuple-element.10), channel_id=1, source_target_pairs={{6,0},{7,1},{0,2},{1,3},{2,4},{3,5},{4,6},{5,7},{14,8},{15,9},{8,1... | collective-permute-start | bytes 196616 | tf_op jit(solution)/shard_map/ppermute | solution.py:109
  30.9 1.4 collective-permute-start.9
  32.3 3.7 %collective-permute-done.7 = f32[128,128]{1,0:T(8,128)S(1)} collective-permute-done((f32[128,128]{1,0:T(8,128)S(1)}, f32[128,128]{1,0:T(8,128)S(1)}, u32[]{:S(2)}, u32[]{:S(2)}) %collective-permute-start.7) | collective-permute-done | bytes 65568 | tf_op jit(solution)/shard_map/ppermute | solution.py:109
  36.0 5.1 %collective-permute-done.8 = f32[128,128]{1,0:T(8,128)S(1)} collective-permute-done((f32[128,128]{1,0:T(8,128)S(1)}, f32[128,128]{1,0:T(8,128)S(1)}, u32[]{:S(2)}, u32[]{:S(2)}) %collective-permute-start.8) | collective-permute-done | bytes 65568 | tf_op jit(solution)/shard_map/ppermute | solution.py:109
  42.3 1.6 slice.13
  44.0 1.2 slice.15
  45.5 1.8 collective-permute-start.10
  47.3 1.7 collective-permute-start.11
  49.0 1.5 collective-permute-start.12
  50.5 9.2 %collective-permute-done.10 = f32[128,1408]{0,1:T(8,128)S(1)} collective-permute-done((f32[128,1408]{0,1:T(8,128)S(1)}, f32[128,1408]{0,1:T(8,128)S(1)}, u32[]{:S(2)}, u32[]{:S(2)}) %collective-permute-start.10) | collective-permute-done | bytes 720928 | tf_op jit(solution)/shard_map/ppermute | solution.py:101
  59.7 1.7 collective-permute-done.11
  61.5 13.7 %collective-permute-done.12 = f32[128,1408]{0,1:T(8,128)S(1)} collective-permute-done((f32[128,1408]{0,1:T(8,128)S(1)}, f32[128,1408]{0,1:T(8,128)S(1)}, u32[]{:S(2)}, u32[]{:S(2)}) %collective-permute-start.12) | collective-permute-done | bytes 720928 | tf_op jit(solution)/shard_map/ppermute | solution.py:101
  75.2 1.0 select_select_fusion
  76.2 1.8 slice.14
  78.1 2.9 %copy.16 = f32[3,128,11,128]{1,0,3,2:T(4,128)} copy(f32[3,128,11,128]{3,1,2,0:T(8,128)S(1)} %slice.14) | data formatting | bytes 4325376
  81.0 2.2 %copy-done.1 = f32[1024,1024]{1,0:T(8,128)S(1)} copy-done((f32[1024,1024]{1,0:T(8,128)S(1)}, f32[1024,1024]{1,0:T(8,128)}, u32[]{:S(2)}) %copy-start.1) | copy-done | bytes 4194328
  83.2 55.2 %shard_map.17 = (f32[1024,1024]{1,0:T(8,128)S(1)}, f32[8,128,128]{2,1,0:T(8,128)S(1)}) custom-call(f32[1024,1024]{1,0:T(8,128)S(1)} %copy-done.1), custom_call_target="tpu_custom_call" | custom-call | tf_op jit(solution)/shard_map/pallas_call | solution.py:86
  138.4 2.0 %copy-done = f32[1024,1024]{1,0:T(8,128)} copy-done((f32[1024,1024]{1,0:T(8,128)}, f32[1024,1024]{1,0:T(8,128)S(1)}, u32[]{:S(2)}) %copy-start) | copy-done | bytes 4194328
  140.6 9.3 %fusion.1 = f32[1024,384]{1,0:T(8,128)S(1)} fusion(f32[384,1024]{1,0:T(8,128)} %bitcast.33, f32[1024,1024]{1,0:T(8,128)} %copy-done, s32[1024]{0:T(1024)S(1)} %add_select_fusion), kind=kOutput, calls=%fused_computation.2 | convolution fusion | flops 4833935360 | bytes 7344128 | tf_op jit(solution)/shard_map/dot_general | solution.py:127
  151.1 9.3 %fusion = f32[384,1024]{1,0:T(8,128)} fusion(f32[1024,384]{1,0:T(8,128)S(1)} %fusion.1, f32[1024,1024]{1,0:T(8,128)} %copy-done, s32[1024]{0:T(1024)S(1)} %add_select_fusion), kind=kOutput, calls=%fused_computation.1 | convolution fusion | flops 4833935360 | bytes 7344128 | tf_op jit(solution)/shard_map/dot_general | solution.py:128
  160.5 12.4 %all-gather.7.cloned.1.call-done = f32[1024,1408]{0,1:T(8,128)} async-done(((f32[128,1408]{0,1:T(8,128)}), f32[1024,1408]{0,1:T(8,128)}) %all-gather.7.cloned.1.call-update) | async-done | bytes 5767184 | tf_op jit(solution)/shard_map/all_gather | solution.py:122
  172.8 11.6 %fusion.15 = f32[384,1408]{0,1:T(8,128)S(1)} fusion(f32[384,1024]{1,0:T(8,128)} %fusion, f32[1024,1408]{0,1:T(8,128)} %all-gather.7.cloned.1.call-done), kind=kOutput, calls=%fused_computation.44 | convolution fusion | flops 6643777536 | bytes 9502720 | tf_op jit(solution)/shard_map/dot_general | solution.py:129
  184.4 2.0 %reshape.48 = f32[3,128,11,128]{1,0,3,2:T(4,128)} reshape(f32[384,1408]{0,1:T(8,128)S(1)} %fusion.15) | data formatting | bytes 4325376 | tf_op jit(solution)/shard_map/reshape | solution.py:130
  186.5 3.7 %subtract_select_fusion = f32[3,128,11,128]{1,0,3,2:T(4,128)S(1)} fusion(f32[3,128,11,128]{1,0,3,2:T(4,128)} %copy.16, f32[3,128,11,128]{1,0,3,2:T(4,128)} %reshape.48, pred[3]{0:T(512)(128)(4,1)S(1)} %compare_and_fusion), kind=kLoop, calls=%fused_computation.4 | loop fusion | flops 1081344 | bytes 6488067 | tf_op jit(solution)/shard_map/jit(_where)/select_n | solution.py:133
  190.9 2.5 %copy.13 = f32[3,128,12,128]{3,1,2,0:T(8,128)} copy(f32[3,128,12,128]{1,0,3,2:T(4,128)S(1)} %pad_maximum_fusion) | data formatting | bytes 4718592 | tf_op jit(solution)/shard_map/concatenate | solution.py:140
  (48 shorter events, 5.0 us)
Async XLA Ops:
  6.5 74.5 %all-gather.5.cloned.1.call-start = ((), (), s32[]{:S(2)}) async-start(), calls=%async_computation | async-start | bytes 4718592 | tf_op jit(solution)/shard_map/all_gather | solution.py:119
  7.5 8.1 %collective-permute-start = (f32[128,128]{0,1:T(8,128)S(1)}, f32[128,128]{0,1:T(8,128)S(1)}, u32[]{:S(2)}, u32[]{:S(2)}) collective-permute-start(f32[128,128]{0,1:T(8,128)S(1)} %bitcast.34), channel_id=1, source_target_pairs={{0,128},{1,129},{2,130},{3,131},{4,132},{5,133},{6,134},{7,135},{8... | collective-permute-start | bytes 196616 | tf_op jit(solution)/shard_map/ppermute | solution.py:101
  13.0 2.6 %collective-permute-start.1 = (f32[128,128]{0,1:T(8,128)S(1)}, f32[128,128]{0,1:T(8,128)S(1)}, u32[]{:S(2)}, u32[]{:S(2)}) collective-permute-start(f32[128,128]{0,1:T(8,128)S(1)} %bitcast.35), channel_id=1, source_target_pairs={{0,192},{1,193},{2,194},{3,195},{4,196},{5,197},{6,198},{7,199},{8... | collective-permute-start | bytes 196616 | tf_op jit(solution)/shard_map/ppermute | solution.py:101
  14.3 2.6 %collective-permute-start.2 = (f32[128,128]{0,1:T(8,128)S(1)}, f32[128,128]{0,1:T(8,128)S(1)}, u32[]{:S(2)}, u32[]{:S(2)}) collective-permute-start(f32[128,128]{0,1:T(8,128)S(1)} %bitcast.36), channel_id=1, source_target_pairs={{0,64},{1,65},{2,66},{3,67},{4,68},{5,69},{6,70},{7,71},{8,72},{9,... | collective-permute-start | bytes 196616 | tf_op jit(solution)/shard_map/ppermute | solution.py:101
  16.9 11.8 %collective-permute-start.3 = (f32[128,128]{1,0:T(8,128)S(1)}, f32[128,128]{1,0:T(8,128)S(1)}, u32[]{:S(2)}, u32[]{:S(2)}) collective-permute-start(f32[128,128]{1,0:T(8,128)S(1)} %get-tuple-element.10), channel_id=1, source_target_pairs={{1,0},{2,1},{3,2},{4,3},{5,4},{6,5},{7,6},{0,7},{9,8},{10,9},{11,1... | collective-permute-start | bytes 196616 | tf_op jit(solution)/shard_map/ppermute | solution.py:109
  22.6 8.3 %collective-permute-start.4 = (f32[128,128]{1,0:T(8,128)S(1)}, f32[128,128]{1,0:T(8,128)S(1)}, u32[]{:S(2)}, u32[]{:S(2)}) collective-permute-start(f32[128,128]{1,0:T(8,128)S(1)} %get-tuple-element.10), channel_id=1, source_target_pairs={{2,0},{3,1},{4,2},{5,3},{6,4},{7,5},{0,6},{1,7},{10,8},{11,9},{12,... | collective-permute-start | bytes 196616 | tf_op jit(solution)/shard_map/ppermute | solution.py:109
  23.7 8.6 %collective-permute-start.5 = (f32[128,128]{1,0:T(8,128)S(1)}, f32[128,128]{1,0:T(8,128)S(1)}, u32[]{:S(2)}, u32[]{:S(2)}) collective-permute-start(f32[128,128]{1,0:T(8,128)S(1)} %get-tuple-element.10), channel_id=1, source_target_pairs={{3,0},{4,1},{5,2},{6,3},{7,4},{0,5},{1,6},{2,7},{11,8},{12,9},{13,... | collective-permute-start | bytes 196616 | tf_op jit(solution)/shard_map/ppermute | solution.py:109
  24.2 8.1 %collective-permute-start.6 = (f32[128,128]{1,0:T(8,128)S(1)}, f32[128,128]{1,0:T(8,128)S(1)}, u32[]{:S(2)}, u32[]{:S(2)}) collective-permute-start(f32[128,128]{1,0:T(8,128)S(1)} %get-tuple-element.10), channel_id=1, source_target_pairs={{4,0},{5,1},{6,2},{7,3},{0,4},{1,5},{2,6},{3,7},{12,8},{13,9},{14,... | collective-permute-start | bytes 196616 | tf_op jit(solution)/shard_map/ppermute | solution.py:109
  28.7 7.3 %collective-permute-start.7 = (f32[128,128]{1,0:T(8,128)S(1)}, f32[128,128]{1,0:T(8,128)S(1)}, u32[]{:S(2)}, u32[]{:S(2)}) collective-permute-start(f32[128,128]{1,0:T(8,128)S(1)} %get-tuple-element.10), channel_id=1, source_target_pairs={{5,0},{6,1},{7,2},{0,3},{1,4},{2,5},{3,6},{4,7},{13,8},{14,9},{15,... | collective-permute-start | bytes 196616 | tf_op jit(solution)/shard_map/ppermute | solution.py:109
  28.7 12.4 %collective-permute-start.8 = (f32[128,128]{1,0:T(8,128)S(1)}, f32[128,128]{1,0:T(8,128)S(1)}, u32[]{:S(2)}, u32[]{:S(2)}) collective-permute-start(f32[128,128]{1,0:T(8,128)S(1)} %get-tuple-element.10), channel_id=1, source_target_pairs={{6,0},{7,1},{0,2},{1,3},{2,4},{3,5},{4,6},{5,7},{14,8},{15,9},{8,1... | collective-permute-start | bytes 196616 | tf_op jit(solution)/shard_map/ppermute | solution.py:109
  30.9 10.4 %collective-permute-start.9 = (f32[128,128]{1,0:T(8,128)S(1)}, f32[128,128]{1,0:T(8,128)S(1)}, u32[]{:S(2)}, u32[]{:S(2)}) collective-permute-start(f32[128,128]{1,0:T(8,128)S(1)} %get-tuple-element.10), channel_id=1, source_target_pairs={{7,0},{0,1},{1,2},{2,3},{3,4},{4,5},{5,6},{6,7},{15,8},{8,9},{9,10... | collective-permute-start | bytes 196616 | tf_op jit(solution)/shard_map/ppermute | solution.py:109
  42.3 98.3 %all-gather.9.cloned.1.call-start = ((), (), s32[]{:S(2)}) async-start(), calls=%async_computation.2 | async-start | bytes 1769472 | tf_op jit(solution)/shard_map/all_gather | solution.py:120
  44.0 128.9 %all-gather.7.cloned.1.call-start = ((), (), s32[]{:S(2)}) async-start(), calls=%async_computation.1 | async-start | bytes 6488064 | tf_op jit(solution)/shard_map/all_gather | solution.py:122
  45.5 14.3 %collective-permute-start.10 = (f32[128,1408]{0,1:T(8,128)S(1)}, f32[128,1408]{0,1:T(8,128)S(1)}, u32[]{:S(2)}, u32[]{:S(2)}) collective-permute-start(f32[128,1408]{0,1:T(8,128)S(1)} %bitcast.29), channel_id=1, source_target_pairs={{0,128},{1,129},{2,130},{3,131},{4,132},{5,133},{6,134},{7,135},{8... | collective-permute-start | bytes 2162696 | tf_op jit(solution)/shard_map/ppermute | solution.py:101
  47.3 14.2 %collective-permute-start.11 = (f32[128,1408]{0,1:T(8,128)S(1)}, f32[128,1408]{0,1:T(8,128)S(1)}, u32[]{:S(2)}, u32[]{:S(2)}) collective-permute-start(f32[128,1408]{0,1:T(8,128)S(1)} %bitcast.30), channel_id=1, source_target_pairs={{0,192},{1,193},{2,194},{3,195},{4,196},{5,197},{6,198},{7,199},{8... | collective-permute-start | bytes 2162696 | tf_op jit(solution)/shard_map/ppermute | solution.py:101
  49.0 26.2 %collective-permute-start.12 = (f32[128,1408]{0,1:T(8,128)S(1)}, f32[128,1408]{0,1:T(8,128)S(1)}, u32[]{:S(2)}, u32[]{:S(2)}) collective-permute-start(f32[128,1408]{0,1:T(8,128)S(1)} %bitcast.31), channel_id=1, source_target_pairs={{0,64},{1,65},{2,66},{3,67},{4,68},{5,69},{6,70},{7,71},{8,72},{9,... | collective-permute-start | bytes 2162696 | tf_op jit(solution)/shard_map/ppermute | solution.py:101
  81.0 2.2 %copy-start.1 = (f32[1024,1024]{1,0:T(8,128)S(1)}, f32[1024,1024]{1,0:T(8,128)}, u32[]{:S(2)}) copy-start(f32[1024,1024]{1,0:T(8,128)} %all-gather.5.cloned.1.call-done.x_ref) | copy-start | bytes 12582916
  138.4 2.0 %copy-start = (f32[1024,1024]{1,0:T(8,128)}, f32[1024,1024]{1,0:T(8,128)S(1)}, u32[]{:S(2)}) copy-start(f32[1024,1024]{1,0:T(8,128)S(1)} %get-tuple-element.8) | copy-start | bytes 12582916
Sparse Core Ops, SparseCore 0:
  42.4 37.8 all-gather.4
  82.0 40.2 all-gather.8
  124.1 48.7 all-gather.6

commit v2 on v1

v2 whole, which is shorter than its diff:
```python
import jax
import jax.numpy as jnp
from jax import lax
from jax.experimental import pallas as pl
from jax.experimental.pallas import tpu as pltpu
from jax.sharding import Mesh
from jax.sharding import PartitionSpec as P

TILE = 128
TILES = 8
WIDTH = TILE * TILES
GROUP = 16
ROW = ("x", "y", "k")
VMEM = pl.BlockSpec(memory_space=pltpu.VMEM)


def split(x):
    high = x.astype(jnp.bfloat16)
    rest = x - high.astype(jnp.float32)
    middle = rest.astype(jnp.bfloat16)
    return high, middle, (rest - middle.astype(jnp.float32)).astype(jnp.bfloat16)


def left_terms(parts, axis):
    h, m, l = parts
    return jnp.concatenate([h, h, m, h, l, m], axis)


def right_terms(parts, axis):
    h, m, l = parts
    return jnp.concatenate([h, m, h, l, h, m], axis)


def contract(a, b, da, db):
    return lax.dot_general(a, b, (((da,), (db,)), ((), ())), preferred_element_type=jnp.float32)


def spread_row(x, i):
    return jnp.broadcast_to(x[i : i + 1, :], (8, TILE))


def spread_col(x, i):
    return jnp.broadcast_to(x[:, i : i + 1], (8, TILE))


def factor_tile(a_ref, v_ref, hook):
    sub = lax.broadcasted_iota(jnp.int32, (8, TILE), 0)
    lane = lax.broadcasted_iota(jnp.int32, (8, TILE), 1)
    for t in range(TILE // GROUP):
        base = GROUP * t
        total = TILE // 8 - 2 * t
        n = min(4, total)
        rows = [slice(base + 8 * q, base + 8 * q + 8) for q in range(n)]
        a = [a_ref[s, :] for s in rows]
        if t == 0:
            v = [jnp.where(lane == sub + 8 * q, 1.0, 0.0) for q in range(n)]
        else:
            v = [v_ref[s, :] for s in rows]
        cols = [[spread_col(a[q], base + l) for q in range(n)] for l in range(GROUP)]

        def eliminate(j, inverse):
            q0, i = j // 8, j % 8
            m = [
                (cols[j][q] if q > q0 else jnp.where(sub > i, cols[j][q], 0.0)) * inverse
                for q in range(q0, n)
            ]
            for l in range(j + 1, GROUP):
                e = spread_row(cols[l][q0], i)
                for q in range(q0, n):
                    cols[l][q] = cols[l][q] - m[q - q0] * e
            ra, rv = spread_row(a[q0], i), spread_row(v[q0], i)
            for q in range(q0, n):
                a[q] = a[q] - m[q - q0] * ra
                v[q] = v[q] - m[q - q0] * rv

        for j in range(0, GROUP, 2):
            q0, i = j // 8, j % 8
            p = spread_row(cols[j][q0], i)
            g = spread_row(cols[j + 1][q0], i)
            d = spread_row(cols[j + 1][q0], i + 1)
            first = 1.0 / p
            second = p * (1.0 / (p * d - g * g))
            eliminate(j, first)
            eliminate(j + 1, second)
        for q in range(2):
            pivots = cols[8 * q][q]
            for i in range(1, 8):
                pivots = jnp.where(sub == i, cols[8 * q + i][q], pivots)
            scale = lax.rsqrt(pivots)
            a[q] = jnp.where(lane >= sub + base + 8 * q, a[q] * scale, 0.0)
            v[q] = v[q] * scale
        for q in range(n):
            a_ref[rows[q], :] = a[q]
            v_ref[rows[q], :] = v[q]
        if total > n:
            start = base + 8 * n
            done = jnp.concatenate(
                [jnp.concatenate(a[:2], 0), jnp.concatenate(v[:2], 0)], 1
            )
            parts = split(done)
            change = contract(
                left_terms(parts, 0)[:, :TILE], right_terms(parts, 0), 0, 0
            )[start:, :]
            if t == 0:
                shape = (TILE - start, TILE)
                diagonal = lax.broadcasted_iota(jnp.int32, shape, 0) + start
                diagonal = diagonal == lax.broadcasted_iota(jnp.int32, shape, 1)
                v_ref[start:, :] = jnp.where(diagonal, 1.0, 0.0) - change[:, TILE:]
            else:
                v_ref[start:, :] -= change[:, TILE:]
            a_ref[start:, :] -= change[:, :TILE]
        hook(t)


def factor_kernel(
    x_ref, w_ref, u_ref, a_ref, v_ref, vp_ref, vs_ref, h_ref, m_ref, l_ref, r_ref
):
    for i in range(TILES):
        for j in range(TILES):
            w_ref[i * TILE : (i + 1) * TILE, j * TILE : (j + 1) * TILE] = x_ref[i, j]
    w_ref[WIDTH:, :] = jnp.zeros((TILE, WIDTH), jnp.float32)
    a_ref[...] = x_ref[0, 0]
    vs_ref[...] = jnp.zeros_like(vs_ref)
    vp_ref[...] = jnp.zeros_like(vp_ref)

    def tile(i):
        return pl.ds(pl.multiple_of(i * TILE, TILE), TILE)

    def panel(row, column):
        w_ref[row, :] = contract(vs_ref[...], right_terms(split(w_ref[row, :]), 0), 1, 0)
        w_ref[row, column] = vp_ref[...]

    def steps(first, last, slots):
        def step(k, _):
            old = tile(jnp.where(k == 0, TILES, k - 1))
            column = tile(jnp.maximum(k - 1, 0))

            def hook(t):
                if t == 0:
                    panel(old, column)
                    parts = split(w_ref[old, :])
                    h_ref[...], m_ref[...], l_ref[...] = parts
                    r_ref[...] = right_terms(parts, 0)
                elif t <= slots:
                    i = k + t - 1
                    row = tile(jnp.minimum(i, TILES))
                    c = tile(jnp.minimum(i, TILES - 1))
                    w_ref[row, column] = jnp.zeros((TILE, TILE), jnp.float32)
                    left = left_terms((h_ref[:, c], m_ref[:, c], l_ref[:, c]), 0)
                    w_ref[row, :] -= contract(left, r_ref[...], 0, 0)

            factor_tile(a_ref, v_ref, hook)
            u_ref[k] = a_ref[...]
            vp_ref[...] = v_ref[...]
            vs_ref[...] = left_terms(split(v_ref[...]), 1)
            after = tile(jnp.minimum(k + 1, TILES - 1))
            ahead = contract(vs_ref[...], right_terms(split(w_ref[tile(k), after]), 0), 1, 0)
            parts = split(ahead)
            a_ref[...] = w_ref[after, after] - contract(
                left_terms(parts, 0), right_terms(parts, 0), 0, 0
            )
            return 0

        lax.fori_loop(first, last, step, 0)

    steps(0, 4, 7)
    steps(4, 8, 4)
    panel(tile(7), tile(7))


def factor(block):
    tile = pltpu.VMEM((TILE, TILE), jnp.float32)
    part = pltpu.VMEM((TILE, WIDTH), jnp.bfloat16)
    return pl.pallas_call(
        factor_kernel,
        out_shape=[
            jax.ShapeDtypeStruct((WIDTH + TILE, WIDTH), jnp.float32),
            jax.ShapeDtypeStruct((TILES, TILE, TILE), jnp.float32),
        ],
        in_specs=[VMEM],
        out_specs=[VMEM, VMEM],
        scratch_shapes=[tile, tile, tile, pltpu.VMEM((TILE, 6 * TILE), jnp.bfloat16)]
        + [part, part, part, pltpu.VMEM((6 * TILE, WIDTH), jnp.bfloat16)],
        compiler_params=pltpu.CompilerParams(vmem_limit_bytes=40 << 20),
        cost_estimate=pl.CostEstimate(flops=8 << 30, bytes_accessed=9 << 20, transcendentals=0),
        name="factor",
    )(block)


def solve_kernel(ids_ref, own_ref, w_ref, u_ref, t_ref, c_ref, s_ref, hl_ref):
    row, col = ids_ref[0], ids_ref[1]
    rows = own_ref.shape[1] * TILE
    own = split(
        jnp.concatenate([own_ref[z].reshape(rows, TILE) for z in range(TILES)], 1)
    )
    half = 2 * TILE
    lower = lax.broadcasted_iota(jnp.int32, (half, half), 0) // TILE
    lower = lower >= lax.broadcasted_iota(jnp.int32, (half, half), 1) // TILE
    for b in range(0, WIDTH, half):
        n = b + half
        block = w_ref[b:n, :n]
        edge = jnp.where(lower, block[:, b:n], 0.0)
        block = edge if b == 0 else jnp.concatenate([block[:, :b], edge], 1)
        parts = split(block)
        for i in range(3):
            hl_ref[i, b:n, :n] = parts[i]
        s_ref[:, b:n] = contract(
            left_terms([x[:, :n] for x in own], 1), right_terms(parts, 1), 1, 1
        )
    solved = split(s_ref[...])
    for b in range(0, WIDTH, half):
        right = right_terms([hl_ref[i, b:, b : b + half] for i in range(3)], 0)
        twice = contract(left_terms([x[:, b:] for x in solved], 1), right, 1, 0)
        high = twice.astype(jnp.bfloat16)
        t_ref[0, :, b : b + half] = high
        t_ref[1, :, b : b + half] = (twice - high.astype(jnp.float32)).astype(jnp.bfloat16)
    here = pl.ds(pl.multiple_of(col * TILE, TILE), TILE)
    c_ref[...] = s_ref[:, here].reshape(c_ref.shape)

    @pl.when(row < TILES)
    def _():
        there = pl.ds(pl.multiple_of(jnp.minimum(row, TILES - 1) * TILE, TILE), TILE)
        upper = jnp.where(col == row, u_ref[col], w_ref[here, there])
        c_ref[0] = jnp.where(col <= row, upper.T, 0.0)


def solve(ids, own, w, u):
    rows = own.shape[1] * TILE
    return pl.pallas_call(
        solve_kernel,
        out_shape=[
            jax.ShapeDtypeStruct((2, rows, WIDTH), jnp.bfloat16),
            jax.ShapeDtypeStruct((own.shape[1], TILE, TILE), jnp.float32),
        ],
        in_specs=[pl.BlockSpec(memory_space=pltpu.SMEM), VMEM, VMEM, VMEM],
        out_specs=[VMEM, VMEM],
        scratch_shapes=[
            pltpu.VMEM((rows, WIDTH), jnp.float32),
            pltpu.VMEM((3, WIDTH, WIDTH), jnp.bfloat16),
        ],
        compiler_params=pltpu.CompilerParams(vmem_limit_bytes=40 << 20),
        name="solve",
    )(ids, own, w, u)


def update_kernel(ids_ref, t_ref, c_ref, right_ref, k_ref, o_ref):
    step = pl.program_id(0)
    tiles, _, _ = c_ref.shape
    rows = tiles * TILE
    right = jnp.concatenate([right_ref[:, i].reshape(WIDTH, TILE) for i in range(2)], 1)
    high = right.astype(jnp.bfloat16)
    low = (right - high.astype(jnp.float32)).astype(jnp.bfloat16)
    left = jnp.concatenate([t_ref[0], t_ref[0], t_ref[1]], 1)
    product = contract(left, jnp.concatenate([high, low, high], 0), 1, 0)
    product = product.reshape(tiles, TILE, 2 * TILE)
    for i in range(2):
        o_ref[:, i] = k_ref[:, i] - product[:, :, i * TILE : (i + 1) * TILE]

    @pl.when(ids_ref[0] < TILES)
    def _():
        o_ref[0] = jnp.zeros(o_ref.shape[1:], jnp.float32)

    @pl.when(step == 0)
    def _():
        o_ref[:, 0] = c_ref[...]


def update(ids, t, c, right, kernel):
    tiles, columns = kernel.shape[:2]
    block = pl.BlockSpec((tiles, 2, TILE, TILE), lambda j: (0, j, 0, 0))
    return pl.pallas_call(
        update_kernel,
        grid=(columns // 2,),
        out_shape=jax.ShapeDtypeStruct(kernel.shape, jnp.float32),
        in_specs=[
            pl.BlockSpec(memory_space=pltpu.SMEM),
            VMEM,
            VMEM,
            pl.BlockSpec((TILES, 2, TILE, TILE), lambda j: (0, j, 0, 0)),
            block,
        ],
        out_specs=block,
        compiler_params=pltpu.CompilerParams(vmem_limit_bytes=40 << 20),
        name="update",
    )(ids, t, c, right, kernel)


def spread_x(block):
    x = lax.axis_index("x")
    out = block
    for d in (1, 3, 2):
        out = jnp.where(x == d, lax.ppermute(block, "x", [(0, d)]), out)
    return out


def gather_z(block):
    n = lax.axis_size("z")
    me = lax.axis_index("z")
    parts = [block] + [
        lax.ppermute(block, "z", [((i + d) % n, i) for i in range(n)]) for d in range(1, n)
    ]
    rolled = jnp.stack(parts + parts)
    return lax.dynamic_slice_in_dim(rolled, (n - me) % n, n, 0)


def body(kernel):
    kernel = kernel.transpose(0, 2, 1, 3)
    ids = jnp.stack([lax.axis_index(ROW), lax.axis_index("z")]).astype(jnp.int32)
    strip = gather_z(spread_x(kernel[0, 0]))
    block = lax.all_gather(strip, ("y", "k"))
    own = lax.all_gather(kernel[:, 0], "z")
    right = lax.all_gather(spread_x(kernel[0]), ("y", "k"))
    w, u = factor(block)
    t, c = solve(ids, own, w, u)
    out = update(ids, t, c, right, kernel)
    return out.transpose(0, 2, 1, 3)


def solution(mesh):
    fine = Mesh(mesh.devices.reshape(4, 4, 2, 8), ("x", "y", "k", "z"))
    spec = P(None, ROW, None, "z")
    return jax.shard_map(body, mesh=fine, in_specs=(spec,), out_specs=spec, check_vma=False)
```

time: 200 us -> 181 us (0.905)
  matrix products: 30.3 us -> 0 us
  waiting for transfers between devices: 47.4 us -> 70.7 us
  Pallas kernels: 55.2 us -> 48.2 us
  other arithmetic: 5.67 us -> 2.05 us
  local copies, waits for them, and re-layouts: 19.3 us -> 16.8 us
    dot_general x3 -> x0, matrix products: 30.3 us -> none  [the longest x1 11.6 us: body(): product = jnp.dot(twice, right, precision=HIGHEST)]
    all_gather x3, waiting for transfers between devices: 12.4 us -> 34.2 us  [the longest x1 34.2 us: body(): right = lax.all_gather(spread_x(kernel[0]), ('y', 'k'))]
    pallas_call x1 -> x3, Pallas kernels: 55.2 us -> 48.2 us  [the longest x1 33.5 us: factor(): pl.pallas_call(factor_kernel, out_shape=[jax.ShapeDtypeStruct((WIDTH + TI...]
    unnamed x22 -> x32, local copies, waits for them, and re-layouts: 7.85 us -> 14.2 us
    slice x4 -> x1, local copies, waits for them, and re-layouts: 5.48 us -> 0.67 us  [body(): own = lax.all_gather(kernel[:, 0], 'z')]
    select_n x4 -> x0, other arithmetic: 3.9 us -> none  [the longest x1 3.66 us: body(): rest = jnp.where(dead, 0.0, kernel[:, :, 1:, :] - product)]
    concatenate x2 -> x0, local copies, waits for them, and re-layouts: 2.46 us -> none  [the longest x1 2.46 us: body(): return jnp.concatenate([column[:, :, None, :], rest], 2)]
    reshape x1 -> x0, local copies, waits for them, and re-layouts: 2.01 us -> none  [body(): product = product.reshape(3, TILE, 11, TILE)]
  transfers between devices with their start and end apart: 16 -> 16, of which waited for: 8 -> 8; matrix products, arithmetic and copies ran while one was open for 14% -> 1% of each run, Pallas kernels for 28% -> 23%
where the time goes in v2:
time: 181 us
  waiting for transfers between devices  70.7 us (39%)
  Pallas kernels  48.2 us (27%)
  starting transfers between devices  29.8 us (16%)
  local copies, waits for them, and re-layouts  16.8 us (9%)
  between operations  13.3 us (7%)
  other arithmetic  2.05 us (1%)
    all_gather x1, waiting for transfers between devices, body(): right = lax.all_gather(spread_x(kernel[0]), ('y', 'k'))  34.2 us
    pallas_call x1, Pallas kernels, factor(): pl.pallas_call(factor_kernel, out_shape=[jax.ShapeDtypeStruct((WIDTH + TI...  33.5 us
    ppermute x6, waiting for transfers between devices, spread_x(): out = jnp.where(x == d, lax.ppermute(block, 'x', [(0, d)]), out)  27.5 us
    ppermute x7, starting transfers between devices, gather_z(): lax.ppermute(block, 'z', [((i + d) % n, i) for i in range(n)])  15.4 us
    ppermute x6, starting transfers between devices, spread_x(): out = jnp.where(x == d, lax.ppermute(block, 'x', [(0, d)]), out)  14.4 us
    unnamed x32, local copies, waits for them, and re-layouts  14.2 us
    ppermute x7, waiting for transfers between devices, gather_z(): lax.ppermute(block, 'z', [((i + d) % n, i) for i in range(n)])  8.96 us
    pallas_call x1, Pallas kernels, solve(): pl.pallas_call(solve_kernel, out_shape=[jax.ShapeDtypeStruct((2, rows, WI...  7.96 us
  transfers between devices with their start and end apart: 16, of which 8 were waited for; matrix products, arithmetic and copies ran while one was open for 1% of the time, Pallas kernels for 23%

profile of v2, /device:TPU:1, one launch (start us, length us, event | category | flops | bytes accessed | tf_op | source)
XLA Modules:
  0.0 180.9 jit_solution(901651300160275634)
XLA Ops:
  6.5 1.0 slice_bitcast_fusion.1
  7.5 5.5 %collective-permute-start = (f32[128,128]{1,0:T(8,128)S(1)}, f32[128,128]{1,0:T(8,128)S(1)}, u32[]{:S(2)}, u32[]{:S(2)}) collective-permute-start(f32[128,128]{1,0:T(8,128)S(1)} %slice_bitcast_fusion.1), channel_id=1, source_target_pairs={{0,128},{1,129},{2,130},{3,131},{4,132},{5,133},{6,134},{7,135},{8... | collective-permute-start | bytes 196616 | tf_op jit(solution)/shard_map/ppermute | solution.py:292
  13.0 1.3 collective-permute-start.1
  14.3 1.9 %collective-permute-start.2 = (f32[128,128]{1,0:T(8,128)S(1)}, f32[128,128]{1,0:T(8,128)}, u32[]{:S(2)}, u32[]{:S(2)}) collective-permute-start(f32[128,128]{1,0:T(8,128)S(1)} %slice_bitcast_fusion.1), channel_id=1, source_target_pairs={{0,64},{1,65},{2,66},{3,67},{4,68},{5,69},{6,70},{7,71},{8,72},{9,... | collective-permute-start | bytes 196616 | tf_op jit(solution)/shard_map/ppermute | solution.py:292
  16.9 0.9 bitcast_dynamic-update-slice_fusion.14
  17.8 5.7 %collective-permute-start.3 = (f32[128,128]{1,0:T(8,128)S(1)}, f32[128,128]{1,0:T(8,128)S(1)}, u32[]{:S(2)}, u32[]{:S(2)}) collective-permute-start(f32[128,128]{1,0:T(8,128)S(1)} %get-tuple-element.14), channel_id=1, source_target_pairs={{1,0},{2,1},{3,2},{4,3},{5,4},{6,5},{7,6},{0,7},{9,8},{10,9},{11,1... | collective-permute-start | bytes 196616 | tf_op jit(solution)/shard_map/ppermute | solution.py:300
  23.4 1.2 collective-permute-start.4
  25.1 4.5 %collective-permute-start.6 = (f32[128,128]{1,0:T(8,128)S(1)}, f32[128,128]{1,0:T(8,128)S(1)}, u32[]{:S(2)}, u32[]{:S(2)}) collective-permute-start(f32[128,128]{1,0:T(8,128)S(1)} %get-tuple-element.14), channel_id=1, source_target_pairs={{4,0},{5,1},{6,2},{7,3},{0,4},{1,5},{2,6},{3,7},{12,8},{13,9},{14,... | collective-permute-start | bytes 196616 | tf_op jit(solution)/shard_map/ppermute | solution.py:300
  29.5 2.2 %collective-permute-start.8 = (f32[128,128]{1,0:T(8,128)S(1)}, f32[128,128]{1,0:T(8,128)S(1)}, u32[]{:S(2)}, u32[]{:S(2)}) collective-permute-start(f32[128,128]{1,0:T(8,128)S(1)} %get-tuple-element.14), channel_id=1, source_target_pairs={{6,0},{7,1},{0,2},{1,3},{2,4},{3,5},{4,6},{5,7},{14,8},{15,9},{8,1... | collective-permute-start | bytes 196616 | tf_op jit(solution)/shard_map/ppermute | solution.py:300
  31.7 1.4 collective-permute-start.9
  33.2 3.7 %collective-permute-done.7 = f32[128,128]{1,0:T(8,128)S(1)} collective-permute-done((f32[128,128]{1,0:T(8,128)S(1)}, f32[128,128]{1,0:T(8,128)S(1)}, u32[]{:S(2)}, u32[]{:S(2)}) %collective-permute-start.7) | collective-permute-done | bytes 65568 | tf_op jit(solution)/shard_map/ppermute | solution.py:300
  36.9 5.1 %collective-permute-done.8 = f32[128,128]{1,0:T(8,128)S(1)} collective-permute-done((f32[128,128]{1,0:T(8,128)S(1)}, f32[128,128]{1,0:T(8,128)S(1)}, u32[]{:S(2)}, u32[]{:S(2)}) %collective-permute-start.8) | collective-permute-done | bytes 65568 | tf_op jit(solution)/shard_map/ppermute | solution.py:300
  42.3 0.8 constant_dynamic-slice_fusion
  43.2 0.7 slice.12
  44.0 2.4 %collective-permute-start.10 = (f32[12,128,128]{2,1,0:T(8,128)S(1)}, f32[12,128,128]{2,1,0:T(8,128)S(1)}, u32[]{:S(2)}, u32[]{:S(2)}) collective-permute-start(f32[12,128,128]{2,1,0:T(8,128)S(1)} %slice_bitcast_fusion), channel_id=1, source_target_pairs={{0,128},{1,129},{2,130},{3,131},{4,132},{5,133},{6,134},{7,135},{8... | collective-permute-start | bytes 2359304 | tf_op jit(solution)/shard_map/ppermute | solution.py:292
  46.5 1.7 collective-permute-start.11
  48.2 1.5 collective-permute-start.12
  49.8 10.6 %collective-permute-done.10 = f32[12,128,128]{2,1,0:T(8,128)S(1)} collective-permute-done((f32[12,128,128]{2,1,0:T(8,128)S(1)}, f32[12,128,128]{2,1,0:T(8,128)S(1)}, u32[]{:S(2)}, u32[]{:S(2)}) %collective-permute-start.10) | collective-permute-done | bytes 786464 | tf_op jit(solution)/shard_map/ppermute | solution.py:292
  60.4 1.8 collective-permute-done.11
  62.1 15.1 %collective-permute-done.12 = f32[12,128,128]{2,1,0:T(8,128)S(1)} collective-permute-done((f32[12,128,128]{2,1,0:T(8,128)S(1)}, f32[12,128,128]{2,1,0:T(8,128)S(1)}, u32[]{:S(2)}, u32[]{:S(2)}) %collective-permute-start.12) | collective-permute-done | bytes 786464 | tf_op jit(solution)/shard_map/ppermute | solution.py:292
  77.2 1.1 select_select_fusion
  78.4 2.2 %copy-done.7 = f32[64,128,128]{2,1,0:T(8,128)S(1)} copy-done((f32[64,128,128]{2,1,0:T(8,128)S(1)}, f32[64,128,128]{2,1,0:T(8,128)}, u32[]{:S(2)}) %copy-start.7) | copy-done | bytes 4194328
  80.6 33.5 %factor.1 = (f32[1152,1024]{1,0:T(8,128)S(1)}, f32[8,128,128]{2,1,0:T(8,128)S(1)}) custom-call(f32[8,8,128,128]{3,2,1,0:T(8,128)S(1)} %bitcast.48), custom_call_target="tpu_custom_call" | custom-call | flops 8589934592 | bytes 9437184 | tf_op jit(solution)/shard_map/factor/pallas_call | solution.py:174
  114.2 2.2 %copy-done.2 = f32[1152,1024]{1,0:T(8,128)} copy-done((f32[1152,1024]{1,0:T(8,128)}, f32[1152,1024]{1,0:T(8,128)S(1)}, u32[]{:S(2)}) %copy-start.2) | copy-done | bytes 4718616
  116.4 2.3 %copy-done.3 = f32[1152,1024]{1,0:T(8,128)S(1)} copy-done((f32[1152,1024]{1,0:T(8,128)S(1)}, f32[1152,1024]{1,0:T(8,128)}, u32[]{:S(2)}) %copy-start.3) | copy-done | bytes 4718616
  118.8 1.4 copy-done.6
  120.2 8.0 %solve.1 = (bf16[2,384,1024]{2,1,0:T(8,128)(2,1)S(1)}, f32[3,128,128]{2,1,0:T(8,128)S(1)}) custom-call(s32[2]{0:T(128)S(1)} %pad_add_fusion.ids_ref, f32[8,3,128,128]{3,2,1,0:T(8,128)S(1)} %bitcast.47, f32[1152,1024]{1,0:T(8,128)S(1)} %copy-done.3, f32[8,128,128]{2,1,0:T(8,128)S(1)} %get-tuple-element.10.u_ref), custom_call_target="tpu_custom_call" | custom-call | tf_op jit(solution)/shard_map/solve/pallas_call | solution.py:229
  128.2 1.1 copy-done.4
  129.3 34.2 %all-gather.11.cloned.1.call-done = f32[96,128,128]{2,1,0:T(8,128)} async-done(((f32[12,128,128]{2,1,0:T(8,128)}), f32[96,128,128]{2,1,0:T(8,128)}) %all-gather.11.cloned.1.call-update) | async-done | bytes 6291472 | tf_op jit(solution)/shard_map/all_gather | solution.py:312
  163.5 2.8 %copy-done.1 = f32[96,128,128]{2,1,0:T(8,128)S(1)} copy-done((f32[96,128,128]{2,1,0:T(8,128)S(1)}, f32[96,128,128]{2,1,0:T(8,128)}, u32[]{:S(2)}) %copy-start.1) | copy-done | bytes 6291480
  166.3 1.4 copy-done.5
  167.7 6.7 %update.1 = f32[3,12,128,128]{3,2,1,0:T(8,128)} custom-call(s32[2]{0:T(128)S(1)} %pad_add_fusion.ids_ref, bf16[2,384,1024]{2,1,0:T(8,128)(2,1)S(1)} %copy-done.5, f32[3,128,128]{2,1,0:T(8,128)S(1)} %get-tuple-element.12.c_ref, f32[8,12,128,128]{3,2,1,0:T(8,128)S(1)} %bitcast.46, f32[3,12,128,128]{3,2,1,0:T(8,128)S(1)} %bitcast.45), custom_call_target="tpu_custom_call" | custom-call | tf_op jit(solution)/shard_map/update/pallas_call | solution.py:271
  (46 shorter events, 1.7 us)
Async XLA Ops:
  6.5 36.7 %copy-start = (f32[3,128,12,128]{3,1,2,0:T(8,128)S(1)}, f32[3,128,12,128]{3,1,2,0:T(8,128)}, u32[]{:S(2)}) copy-start(f32[3,128,12,128]{3,1,2,0:T(8,128)} %param.1) | copy-start | bytes 7077892
  6.5 71.9 %all-gather.9.cloned.1.call-start = ((), (), s32[]{:S(2)}) async-start(), calls=%async_computation.1 | async-start | bytes 4718592 | tf_op jit(solution)/shard_map/all_gather | solution.py:310
  7.5 8.7 %collective-permute-start = (f32[128,128]{1,0:T(8,128)S(1)}, f32[128,128]{1,0:T(8,128)S(1)}, u32[]{:S(2)}, u32[]{:S(2)}) collective-permute-start(f32[128,128]{1,0:T(8,128)S(1)} %slice_bitcast_fusion.1), channel_id=1, source_target_pairs={{0,128},{1,129},{2,130},{3,131},{4,132},{5,133},{6,134},{7,135},{8... | collective-permute-start | bytes 196616 | tf_op jit(solution)/shard_map/ppermute | solution.py:292
  13.0 3.2 %collective-permute-start.1 = (f32[128,128]{1,0:T(8,128)S(1)}, f32[128,128]{1,0:T(8,128)S(1)}, u32[]{:S(2)}, u32[]{:S(2)}) collective-permute-start(f32[128,128]{1,0:T(8,128)S(1)} %slice_bitcast_fusion.1), channel_id=1, source_target_pairs={{0,192},{1,193},{2,194},{3,195},{4,196},{5,197},{6,198},{7,199},{8... | collective-permute-start | bytes 196616 | tf_op jit(solution)/shard_map/ppermute | solution.py:292
  14.3 2.6 %collective-permute-start.2 = (f32[128,128]{1,0:T(8,128)S(1)}, f32[128,128]{1,0:T(8,128)}, u32[]{:S(2)}, u32[]{:S(2)}) collective-permute-start(f32[128,128]{1,0:T(8,128)S(1)} %slice_bitcast_fusion.1), channel_id=1, source_target_pairs={{0,64},{1,65},{2,66},{3,67},{4,68},{5,69},{6,70},{7,71},{8,72},{9,... | collective-permute-start | bytes 196616 | tf_op jit(solution)/shard_map/ppermute | solution.py:292
  16.2 0.6 copy-start.8
  17.8 11.8 %collective-permute-start.3 = (f32[128,128]{1,0:T(8,128)S(1)}, f32[128,128]{1,0:T(8,128)S(1)}, u32[]{:S(2)}, u32[]{:S(2)}) collective-permute-start(f32[128,128]{1,0:T(8,128)S(1)} %get-tuple-element.14), channel_id=1, source_target_pairs={{1,0},{2,1},{3,2},{4,3},{5,4},{6,5},{7,6},{0,7},{9,8},{10,9},{11,1... | collective-permute-start | bytes 196616 | tf_op jit(solution)/shard_map/ppermute | solution.py:300
  23.4 8.3 %collective-permute-start.4 = (f32[128,128]{1,0:T(8,128)S(1)}, f32[128,128]{1,0:T(8,128)S(1)}, u32[]{:S(2)}, u32[]{:S(2)}) collective-permute-start(f32[128,128]{1,0:T(8,128)S(1)} %get-tuple-element.14), channel_id=1, source_target_pairs={{2,0},{3,1},{4,2},{5,3},{6,4},{7,5},{0,6},{1,7},{10,8},{11,9},{12,... | collective-permute-start | bytes 196616 | tf_op jit(solution)/shard_map/ppermute | solution.py:300
  24.6 8.6 %collective-permute-start.5 = (f32[128,128]{1,0:T(8,128)S(1)}, f32[128,128]{1,0:T(8,128)S(1)}, u32[]{:S(2)}, u32[]{:S(2)}) collective-permute-start(f32[128,128]{1,0:T(8,128)S(1)} %get-tuple-element.14), channel_id=1, source_target_pairs={{3,0},{4,1},{5,2},{6,3},{7,4},{0,5},{1,6},{2,7},{11,8},{12,9},{13,... | collective-permute-start | bytes 196616 | tf_op jit(solution)/shard_map/ppermute | solution.py:300
  25.1 8.1 %collective-permute-start.6 = (f32[128,128]{1,0:T(8,128)S(1)}, f32[128,128]{1,0:T(8,128)S(1)}, u32[]{:S(2)}, u32[]{:S(2)}) collective-permute-start(f32[128,128]{1,0:T(8,128)S(1)} %get-tuple-element.14), channel_id=1, source_target_pairs={{4,0},{5,1},{6,2},{7,3},{0,4},{1,5},{2,6},{3,7},{12,8},{13,9},{14,... | collective-permute-start | bytes 196616 | tf_op jit(solution)/shard_map/ppermute | solution.py:300
  29.5 7.3 %collective-permute-start.7 = (f32[128,128]{1,0:T(8,128)S(1)}, f32[128,128]{1,0:T(8,128)S(1)}, u32[]{:S(2)}, u32[]{:S(2)}) collective-permute-start(f32[128,128]{1,0:T(8,128)S(1)} %get-tuple-element.14), channel_id=1, source_target_pairs={{5,0},{6,1},{7,2},{0,3},{1,4},{2,5},{3,6},{4,7},{13,8},{14,9},{15,... | collective-permute-start | bytes 196616 | tf_op jit(solution)/shard_map/ppermute | solution.py:300
  29.5 12.4 %collective-permute-start.8 = (f32[128,128]{1,0:T(8,128)S(1)}, f32[128,128]{1,0:T(8,128)S(1)}, u32[]{:S(2)}, u32[]{:S(2)}) collective-permute-start(f32[128,128]{1,0:T(8,128)S(1)} %get-tuple-element.14), channel_id=1, source_target_pairs={{6,0},{7,1},{0,2},{1,3},{2,4},{3,5},{4,6},{5,7},{14,8},{15,9},{8,1... | collective-permute-start | bytes 196616 | tf_op jit(solution)/shard_map/ppermute | solution.py:300
  31.7 10.5 %collective-permute-start.9 = (f32[128,128]{1,0:T(8,128)S(1)}, f32[128,128]{1,0:T(8,128)S(1)}, u32[]{:S(2)}, u32[]{:S(2)}) collective-permute-start(f32[128,128]{1,0:T(8,128)S(1)} %get-tuple-element.14), channel_id=1, source_target_pairs={{7,0},{0,1},{1,2},{2,3},{3,4},{4,5},{5,6},{6,7},{15,8},{8,9},{9,10... | collective-permute-start | bytes 196616 | tf_op jit(solution)/shard_map/ppermute | solution.py:300
  43.2 73.3 %all-gather.7.cloned.1.call-start = ((), (), s32[]{:S(2)}) async-start(), calls=%async_computation | async-start | bytes 1769472 | tf_op jit(solution)/shard_map/all_gather | solution.py:311
  43.9 119.6 %all-gather.11.cloned.1.call-start = ((), (), s32[]{:S(2)}) async-start(), calls=%async_computation.2 | async-start | bytes 7077888 | tf_op jit(solution)/shard_map/all_gather | solution.py:312
  44.0 16.3 %collective-permute-start.10 = (f32[12,128,128]{2,1,0:T(8,128)S(1)}, f32[12,128,128]{2,1,0:T(8,128)S(1)}, u32[]{:S(2)}, u32[]{:S(2)}) collective-permute-start(f32[12,128,128]{2,1,0:T(8,128)S(1)} %slice_bitcast_fusion), channel_id=1, source_target_pairs={{0,128},{1,129},{2,130},{3,131},{4,132},{5,133},{6,134},{7,135},{8... | collective-permute-start | bytes 2359304 | tf_op jit(solution)/shard_map/ppermute | solution.py:292
  46.5 15.6 %collective-permute-start.11 = (f32[12,128,128]{2,1,0:T(8,128)S(1)}, f32[12,128,128]{2,1,0:T(8,128)S(1)}, u32[]{:S(2)}, u32[]{:S(2)}) collective-permute-start(f32[12,128,128]{2,1,0:T(8,128)S(1)} %slice_bitcast_fusion), channel_id=1, source_target_pairs={{0,192},{1,193},{2,194},{3,195},{4,196},{5,197},{6,198},{7,199},{8... | collective-permute-start | bytes 2359304 | tf_op jit(solution)/shard_map/ppermute | solution.py:292
  48.2 29.0 %collective-permute-start.12 = (f32[12,128,128]{2,1,0:T(8,128)S(1)}, f32[12,128,128]{2,1,0:T(8,128)S(1)}, u32[]{:S(2)}, u32[]{:S(2)}) collective-permute-start(f32[12,128,128]{2,1,0:T(8,128)S(1)} %slice_bitcast_fusion), channel_id=1, source_target_pairs={{0,64},{1,65},{2,66},{3,67},{4,68},{5,69},{6,70},{7,71},{8,72},{9,... | collective-permute-start | bytes 2359304 | tf_op jit(solution)/shard_map/ppermute | solution.py:292
  78.4 2.2 %copy-start.7 = (f32[64,128,128]{2,1,0:T(8,128)S(1)}, f32[64,128,128]{2,1,0:T(8,128)}, u32[]{:S(2)}) copy-start(f32[64,128,128]{2,1,0:T(8,128)} %all-gather.9.cloned.1.call-done) | copy-start | bytes 12582916
  114.2 2.3 %copy-start.2 = (f32[1152,1024]{1,0:T(8,128)}, f32[1152,1024]{1,0:T(8,128)S(1)}, u32[]{:S(2)}) copy-start(f32[1152,1024]{1,0:T(8,128)S(1)} %get-tuple-element.9.w_ref) | copy-start | bytes 14155780
  116.4 2.3 %copy-start.3 = (f32[1152,1024]{1,0:T(8,128)S(1)}, f32[1152,1024]{1,0:T(8,128)}, u32[]{:S(2)}) copy-start(f32[1152,1024]{1,0:T(8,128)} %copy-done.2) | copy-start | bytes 14155780
  118.8 1.4 copy-start.6
  128.2 1.1 copy-start.4
  163.5 2.8 %copy-start.1 = (f32[96,128,128]{2,1,0:T(8,128)S(1)}, f32[96,128,128]{2,1,0:T(8,128)}, u32[]{:S(2)}) copy-start(f32[96,128,128]{2,1,0:T(8,128)} %all-gather.11.cloned.1.call-done) | copy-start | bytes 18874372
  166.3 1.4 copy-start.5
Sparse Core Ops, SparseCore 0:
  43.3 34.4 all-gather.8
  79.6 35.7 all-gather.6
  117.2 46.2 all-gather.10

commit v3 on v2

v3 whole, which is shorter than its diff:
```python
import jax
import jax.numpy as jnp
from jax import lax
from jax.experimental import pallas as pl
from jax.experimental.pallas import tpu as pltpu
from jax.sharding import Mesh
from jax.sharding import PartitionSpec as P

TILE = 128
TILES = 8
HALF = TILES // 2
WIDTH = TILE * TILES
PANEL = TILE * HALF
GROUP = 16
ROW = ("x", "y", "k")
VMEM = pl.BlockSpec(memory_space=pltpu.VMEM)
SMEM = pl.BlockSpec(memory_space=pltpu.SMEM)


def split(x):
    high = x.astype(jnp.bfloat16)
    rest = x - high.astype(jnp.float32)
    middle = rest.astype(jnp.bfloat16)
    return high, middle, (rest - middle.astype(jnp.float32)).astype(jnp.bfloat16)


def left_terms(parts, axis):
    h, m, l = parts
    return jnp.concatenate([h, h, m, h, l, m], axis)


def right_terms(parts, axis):
    h, m, l = parts
    return jnp.concatenate([h, m, h, l, h, m], axis)


def contract(a, b, da, db):
    return lax.dot_general(a, b, (((da,), (db,)), ((), ())), preferred_element_type=jnp.float32)


def tile(i):
    return pl.ds(pl.multiple_of(i * TILE, TILE), TILE)


def spread_row(x, i):
    return jnp.broadcast_to(x[i : i + 1, :], (8, TILE))


def spread_col(x, i):
    return jnp.broadcast_to(x[:, i : i + 1], (8, TILE))


def factor_tile(a_ref, v_ref, hook):
    sub = lax.broadcasted_iota(jnp.int32, (8, TILE), 0)
    lane = lax.broadcasted_iota(jnp.int32, (8, TILE), 1)
    for t in range(TILE // GROUP):
        base = GROUP * t
        total = TILE // 8 - 2 * t
        n = min(4, total)
        rows = [slice(base + 8 * q, base + 8 * q + 8) for q in range(n)]
        a = [a_ref[s, :] for s in rows]
        if t == 0:
            v = [jnp.where(lane == sub + 8 * q, 1.0, 0.0) for q in range(n)]
        else:
            v = [v_ref[s, :] for s in rows]
        cols = [[spread_col(a[q], base + l) for q in range(n)] for l in range(GROUP)]

        def eliminate(j, inverse):
            q0, i = j // 8, j % 8
            m = [
                (cols[j][q] if q > q0 else jnp.where(sub > i, cols[j][q], 0.0)) * inverse
                for q in range(q0, n)
            ]
            for l in range(j + 1, GROUP):
                e = spread_row(cols[l][q0], i)
                for q in range(q0, n):
                    cols[l][q] = cols[l][q] - m[q - q0] * e
            ra, rv = spread_row(a[q0], i), spread_row(v[q0], i)
            for q in range(q0, n):
                a[q] = a[q] - m[q - q0] * ra
                v[q] = v[q] - m[q - q0] * rv

        for j in range(0, GROUP, 2):
            q0, i = j // 8, j % 8
            p = spread_row(cols[j][q0], i)
            g = spread_row(cols[j + 1][q0], i)
            d = spread_row(cols[j + 1][q0], i + 1)
            first = 1.0 / p
            second = p * (1.0 / (p * d - g * g))
            eliminate(j, first)
            eliminate(j + 1, second)
        for q in range(2):
            pivots = cols[8 * q][q]
            for i in range(1, 8):
                pivots = jnp.where(sub == i, cols[8 * q + i][q], pivots)
            scale = lax.rsqrt(pivots)
            a[q] = jnp.where(lane >= sub + base + 8 * q, a[q] * scale, 0.0)
            v[q] = v[q] * scale
        for q in range(n):
            a_ref[rows[q], :] = a[q]
            v_ref[rows[q], :] = v[q]
        if total > n:
            start = base + 8 * n
            done = jnp.concatenate(
                [jnp.concatenate(a[:2], 0), jnp.concatenate(v[:2], 0)], 1
            )
            parts = split(done)
            change = contract(
                left_terms(parts, 0)[:, :TILE], right_terms(parts, 0), 0, 0
            )[start:, :]
            if t == 0:
                shape = (TILE - start, TILE)
                diagonal = lax.broadcasted_iota(jnp.int32, shape, 0) + start
                diagonal = diagonal == lax.broadcasted_iota(jnp.int32, shape, 1)
                v_ref[start:, :] = jnp.where(diagonal, 1.0, 0.0) - change[:, TILE:]
            else:
                v_ref[start:, :] -= change[:, TILE:]
            a_ref[start:, :] -= change[:, :TILE]
        hook(t)


def factor_panel(w_ref, a_ref, v_ref, vp_ref, vs_ref, h_ref, m_ref, l_ref, r_ref):
    w_ref[PANEL : PANEL + TILE, :] = jnp.zeros((TILE, PANEL), jnp.float32)
    a_ref[...] = w_ref[0:TILE, 0:TILE]
    vs_ref[...] = jnp.zeros_like(vs_ref)
    vp_ref[...] = jnp.zeros_like(vp_ref)

    def panel(row, column):
        w_ref[row, :] = contract(vs_ref[...], right_terms(split(w_ref[row, :]), 0), 1, 0)
        w_ref[row, column] = vp_ref[...]

    def step(k, _):
        old = tile(jnp.where(k == 0, HALF, k - 1))
        column = tile(jnp.maximum(k - 1, 0))

        def hook(t):
            if t == 0:
                panel(old, column)
                parts = split(w_ref[old, :])
                h_ref[...], m_ref[...], l_ref[...] = parts
                r_ref[...] = right_terms(parts, 0)
            elif t < HALF:
                i = k + t - 1
                row = tile(jnp.minimum(i, HALF))
                c = tile(jnp.minimum(i, HALF - 1))
                w_ref[row, column] = jnp.zeros((TILE, TILE), jnp.float32)
                left = left_terms((h_ref[:, c], m_ref[:, c], l_ref[:, c]), 0)
                w_ref[row, :] -= contract(left, r_ref[...], 0, 0)

        factor_tile(a_ref, v_ref, hook)
        w_ref[PANEL + TILE :, tile(k)] = a_ref[...]
        vp_ref[...] = v_ref[...]
        vs_ref[...] = left_terms(split(v_ref[...]), 1)
        after = tile(jnp.minimum(k + 1, HALF - 1))
        ahead = contract(vs_ref[...], right_terms(split(w_ref[tile(k), after]), 0), 1, 0)
        parts = split(ahead)
        a_ref[...] = w_ref[after, after] - contract(
            left_terms(parts, 0), right_terms(parts, 0), 0, 0
        )
        return 0

    lax.fori_loop(0, HALF, step, 0)
    panel(tile(HALF - 1), tile(HALF - 1))


def panel_scratch():
    square = pltpu.VMEM((TILE, TILE), jnp.float32)
    part = pltpu.VMEM((TILE, PANEL), jnp.bfloat16)
    return [square, square, square, pltpu.VMEM((TILE, 6 * TILE), jnp.bfloat16)] + [
        part,
        part,
        part,
        pltpu.VMEM((6 * TILE, PANEL), jnp.bfloat16),
    ]


FACTOR = (PANEL + 2 * TILE, PANEL)


def first_kernel(ids_ref, near_ref, far_ref, w_ref, *scratch):
    k = ids_ref[3]
    for ref, side in ((near_ref, k), (far_ref, 1 - k)):
        for y in range(2):
            for j in range(HALF):
                w_ref[tile(2 * y + side), j * TILE : (j + 1) * TILE] = ref[y, j]
    factor_panel(w_ref, *scratch)


def first(ids, near, far):
    return pl.pallas_call(
        first_kernel,
        out_shape=jax.ShapeDtypeStruct(FACTOR, jnp.float32),
        in_specs=[SMEM, VMEM, VMEM],
        out_specs=VMEM,
        scratch_shapes=panel_scratch(),
        compiler_params=pltpu.CompilerParams(vmem_limit_bytes=24 << 20),
        cost_estimate=pl.CostEstimate(flops=8 << 30, bytes_accessed=4 << 20, transcendentals=0),
        name="first",
    )(ids, near, far)


def factor_second(ids_ref, w0_ref, near_ref, far_ref, x_ref, w_ref, b_ref, *scratch):
    y, k = ids_ref[2], ids_ref[3]
    for ref, side in ((near_ref, k), (far_ref, 1 - k)):
        for d in range(4):
            row = tile(2 * lax.rem(y + 4 - d, 4) + side)
            for j in range(HALF):
                b_ref[row, j * TILE : (j + 1) * TILE] = ref[d, j]
    parts = split(b_ref[0:PANEL, :])
    for i in range(HALF):
        n = (i + 1) * TILE
        left = left_terms(split(w0_ref[n - TILE : n, :n]), 1)
        x_ref[n - TILE : n, :] = contract(left, right_terms([p[:n] for p in parts], 0), 1, 0)
    parts = split(x_ref[...])
    right = right_terms(parts, 0)
    for i in range(HALF):
        n = (i + 1) * TILE
        left = left_terms([p[:, n - TILE : n] for p in parts], 0)
        w_ref[n - TILE : n, :] = b_ref[PANEL + n - TILE : PANEL + n, :] - contract(
            left, right, 0, 0
        )
    factor_panel(w_ref, *scratch)


def apply_inverse(ids_ref, own_ref, w0_ref, x_ref, w1_ref, t_ref, c_ref, s_ref):
    row, col = ids_ref[0], ids_ref[1]
    rows = own_ref.shape[1] * TILE
    wide = 2 * TILE
    lower = lax.broadcasted_iota(jnp.int32, (wide, wide), 0) // TILE
    lower = lower >= lax.broadcasted_iota(jnp.int32, (wide, wide), 1) // TILE

    def inverse(w_ref):
        top = jnp.where(lower, w_ref[0:wide, 0:wide], 0.0)
        edge = jnp.where(lower, w_ref[wide:PANEL, wide:PANEL], 0.0)
        bottom = jnp.concatenate([w_ref[wide:PANEL, 0:wide], edge], 1)
        return split(top), split(bottom)

    def times_transpose(a, inv):
        a, (top, bottom) = split(a), inv
        return jnp.concatenate(
            [
                contract(left_terms([p[:, :wide] for p in a], 1), right_terms(top, 1), 1, 1),
                contract(left_terms(a, 1), right_terms(bottom, 1), 1, 1),
            ],
            1,
        )

    def times(a, inv):
        a, (top, bottom) = split(a), inv
        below = [p[:, wide:] for p in a]
        left = [jnp.concatenate([b[:, :wide]], 1) for b in bottom]
        both = [jnp.concatenate([t, l], 0) for t, l in zip(top, left)]
        right = [b[:, wide:] for b in bottom]
        return jnp.concatenate(
            [
                contract(left_terms(a, 1), right_terms(both, 0), 1, 0),
                contract(left_terms(below, 1), right_terms(right, 0), 1, 0),
            ],
            1,
        )

    def own(first):
        return jnp.concatenate(
            [own_ref[z].reshape(rows, TILE) for z in range(first, first + HALF)], 1
        )

    inv0, inv1 = inverse(w0_ref), inverse(w1_ref)
    x = split(x_ref[...])
    s0 = times_transpose(own(0), inv0)
    s_ref[:, :PANEL] = s0
    rest = own(HALF) - contract(left_terms(split(s0), 1), right_terms(x, 0), 1, 0)
    s1 = times_transpose(rest, inv1)
    s_ref[:, PANEL:] = s1
    t1 = times(s1, inv1)
    t0 = times(s0 - contract(left_terms(split(t1), 1), right_terms(x, 1), 1, 1), inv0)
    for start, t in ((0, t0), (PANEL, t1)):
        high = t.astype(jnp.bfloat16)
        t_ref[0, :, start : start + PANEL] = high
        t_ref[1, :, start : start + PANEL] = (t - high.astype(jnp.float32)).astype(jnp.bfloat16)
    c_ref[...] = s_ref[:, tile(col)].reshape(c_ref.shape)

    @pl.when(row < TILES)
    def _():
        c_ref[0] = jnp.zeros((TILE, TILE), jnp.float32)

    for first, w_ref in ((0, w0_ref), (HALF, w1_ref)):

        @pl.when((row >= first) & (row < first + HALF) & (col >= first) & (col <= row))
        def _(first=first, w_ref=w_ref):
            i, j = jnp.clip(col - first, 0, HALF - 1), jnp.clip(row - first, 0, HALF - 1)
            c_ref[0] = w_ref[tile(jnp.where(col == row, HALF + 1, i)), tile(j)].T

    @pl.when((row >= HALF) & (row < TILES) & (col < HALF))
    def _():
        i, j = jnp.clip(col, 0, HALF - 1), jnp.clip(row - HALF, 0, HALF - 1)
        c_ref[0] = x_ref[tile(i), tile(j)].T


def second_kernel(
    ids_ref, w0_ref, near_ref, far_ref, own_hbm, t_ref, c_ref,
    own_ref, arrived, x_ref, w1_ref, s_ref, b_ref, *scratch
):
    copy = pltpu.make_async_copy(own_hbm, own_ref, arrived)
    copy.start()
    factor_second(ids_ref, w0_ref, near_ref, far_ref, x_ref, w1_ref, b_ref, *scratch)
    copy.wait()
    apply_inverse(ids_ref, own_ref, w0_ref, x_ref, w1_ref, t_ref, c_ref, s_ref)


def second(ids, w0, near, far, own):
    rows = own.shape[1] * TILE
    return pl.pallas_call(
        second_kernel,
        out_shape=[
            jax.ShapeDtypeStruct((2, rows, WIDTH), jnp.bfloat16),
            jax.ShapeDtypeStruct((own.shape[1], TILE, TILE), jnp.float32),
        ],
        in_specs=[SMEM, VMEM, VMEM, VMEM, pl.BlockSpec(memory_space=pl.ANY)],
        out_specs=[VMEM, VMEM],
        scratch_shapes=[
            pltpu.VMEM(own.shape, jnp.float32),
            pltpu.SemaphoreType.DMA,
            pltpu.VMEM((PANEL, PANEL), jnp.float32),
            pltpu.VMEM(FACTOR, jnp.float32),
            pltpu.VMEM((rows, WIDTH), jnp.float32),
            pltpu.VMEM((WIDTH, PANEL), jnp.float32),
        ]
        + panel_scratch(),
        compiler_params=pltpu.CompilerParams(vmem_limit_bytes=40 << 20),
        cost_estimate=pl.CostEstimate(flops=16 << 30, bytes_accessed=8 << 20, transcendentals=0),
        name="second",
    )(ids, w0, near, far, own)


def update_kernel(ids_ref, t_ref, c_ref, right_ref, k_ref, o_ref):
    step = pl.program_id(0)
    tiles, _, _ = c_ref.shape
    rows = tiles * TILE
    quarters = [
        jnp.concatenate([right_ref[x, r, i] for r in range(TILES) for x in range(4)], 0)
        for i in range(2)
    ]
    right = jnp.concatenate(quarters, 1)
    high = right.astype(jnp.bfloat16)
    low = (right - high.astype(jnp.float32)).astype(jnp.bfloat16)
    left = jnp.concatenate([t_ref[0], t_ref[0], t_ref[1]], 1)
    product = contract(left, jnp.concatenate([high, low, high], 0), 1, 0)
    product = product.reshape(tiles, TILE, 2 * TILE)
    for i in range(2):
        o_ref[:, i] = k_ref[:, i] - product[:, :, i * TILE : (i + 1) * TILE]

    @pl.when(ids_ref[0] < TILES)
    def _():
        o_ref[0] = jnp.zeros(o_ref.shape[1:], jnp.float32)

    @pl.when(step == 0)
    def _():
        o_ref[:, 0] = c_ref[...]


def update(ids, t, c, right, kernel):
    tiles, columns = kernel.shape[:2]
    block = pl.BlockSpec((tiles, 2, TILE, TILE), lambda j: (0, j, 0, 0))
    return pl.pallas_call(
        update_kernel,
        grid=(columns // 2,),
        out_shape=jax.ShapeDtypeStruct(kernel.shape, jnp.float32),
        in_specs=[
            SMEM,
            VMEM,
            VMEM,
            pl.BlockSpec((4, TILES, 2, TILE // 4, TILE), lambda j: (0, 0, j, 0, 0)),
            block,
        ],
        out_specs=block,
        compiler_params=pltpu.CompilerParams(vmem_limit_bytes=44 << 20),
        name="update",
    )(ids, t, c, right, kernel)


def swap(x):
    return lax.ppermute(x, "k", [(0, 1), (1, 0)])


def send(x, axis, pairs):
    return lax.ppermute(x, axis, pairs)


def gather_first(strip):
    y = lax.axis_index("y")
    one = send(strip, "y", [(0, 1), (1, 0)])
    two = send(strip, "y", [(0, 3), (1, 2)])
    three = send(strip, "y", [(0, 2), (1, 3)])
    upper = jnp.where(y == 0, strip, jnp.where(y == 1, one, jnp.where(y == 2, three, two)))
    lower = jnp.where(y == 1, strip, jnp.where(y == 0, one, jnp.where(y == 2, two, three)))
    near = jnp.stack([upper, lower])
    return near, swap(near)


def gather_second(strip):
    n = lax.axis_size("y")
    return [strip] + [send(strip, "y", [(i, (i + d) % n) for i in range(n)]) for d in range(1, n)]


def body(kernel):
    kernel = kernel.transpose(0, 2, 1, 3)
    x = lax.axis_index("x")
    ids = jnp.stack([lax.axis_index(a) for a in (ROW, "z", "y", "k")]).astype(jnp.int32)
    own = lax.all_gather(kernel[:, 0], "z")

    corner = kernel[0, 0]
    for d in (1, 3, 2):
        corner = jnp.where(x == d, send(kernel[0, 0], "x", [(0, d)]), corner)
    corner, head = lax.optimization_barrier((corner, kernel[0]))
    spread = jnp.broadcast_to(corner, (TILES, TILE, TILE))
    strip = lax.all_to_all(spread, "z", 0, 0)
    quarters = head.reshape(-1, 4, TILE // 4, TILE)
    quarter = quarters[:, 0]
    for d in (1, 3, 2):
        quarter = jnp.where(x == d, send(quarters[:, d], "x", [(0, d)]), quarter)
    right = lax.all_gather(quarter, ROW)
    right = right.reshape(4, TILES, -1, TILE // 4, TILE)

    near, far = gather_first(strip[:HALF])
    near, far, rest = lax.optimization_barrier((near, far, strip[HALF:]))
    parts = gather_second(rest)
    w0 = first(ids, near, far)
    w0, parts = lax.optimization_barrier((w0, parts))
    more = jnp.stack(parts)
    t, c = second(ids, w0, more, swap(more), own)
    out = update(ids, t, c, right, kernel)
    return out.transpose(0, 2, 1, 3)


def solution(mesh):
    fine = Mesh(mesh.devices.reshape(4, 4, 2, 8), ("x", "y", "k", "z"))
    spec = P(None, ROW, None, "z")
    return jax.shard_map(body, mesh=fine, in_specs=(spec,), out_specs=spec, check_vma=False)
```

time: 181 us -> 157 us (0.87)
  waiting for transfers between devices: 70.7 us -> 20 us
  blocking collectives: 0 us -> 29.1 us
  local copies, waits for them, and re-layouts: 16.8 us -> 14.3 us
    all_gather x2 -> x1, waiting for transfers between devices: 34.2 us -> 0.01 us  [body(): right = lax.all_gather(quarter, ROW)]
    all_to_all x0 -> x1, blocking collectives: none -> 29.1 us  [body(): strip = lax.all_to_all(spread, 'z', 0, 0)]
    ppermute x13 -> x14, waiting for transfers between devices: 36.5 us -> 20 us  [the longest x12 16.2 us: send(): return lax.ppermute(x, axis, pairs)]
    unnamed x32 -> x20, local copies, waits for them, and re-layouts: 14.2 us -> 10.5 us
    pallas_call x2, Pallas kernels: 41.5 us -> 39.1 us  [the longest x1 25.3 us: second(): pl.pallas_call(second_kernel, out_shape=[jax.ShapeDtypeStruct((2, rows, W...]
    ppermute x13 -> x14, starting transfers between devices: 29.7 us -> 29 us  [the longest x12 25 us: send(): return lax.ppermute(x, axis, pairs)]
  transfers between devices with their start and end apart: 16 -> 16, of which waited for: 8 -> 8; matrix products, arithmetic and copies ran while one was open for 1% -> 3% of each run, Pallas kernels for 23% -> 25%
where the time goes in v3:
time: 157 us; the launch traced here: 155 us
  Pallas kernels  47.2 us (30%)
  blocking collectives  29.1 us (19%)
  starting transfers between devices  29 us (18%)
  waiting for transfers between devices  20 us (13%)
  local copies, waits for them, and re-layouts  14.3 us (9%)
  between operations  13.6 us (9%)
  other arithmetic  1.9 us (1%)
    all_to_all x1, blocking collectives, body(): strip = lax.all_to_all(spread, 'z', 0, 0)  29.1 us
    pallas_call x1, Pallas kernels, second(): pl.pallas_call(second_kernel, out_shape=[jax.ShapeDtypeStruct((2, rows, W...  25.3 us
    ppermute x12, starting transfers between devices, send(): return lax.ppermute(x, axis, pairs)  25 us
    ppermute x12, waiting for transfers between devices, send(): return lax.ppermute(x, axis, pairs)  16.2 us
    pallas_call x1, Pallas kernels, first(): pl.pallas_call(first_kernel, out_shape=jax.ShapeDtypeStruct(FACTOR, jnp.f...  13.8 us
    unnamed x20, local copies, waits for them, and re-layouts  10.5 us
    pallas_call x1, Pallas kernels, update(): pl.pallas_call(update_kernel, grid=(columns // 2,), out_shape=jax.ShapeDt...  8.16 us
    ppermute x2, starting transfers between devices, swap(): return lax.ppermute(x, 'k', [(0, 1), (1, 0)])  3.99 us
  transfers between devices with their start and end apart: 16, of which 8 were waited for; matrix products, arithmetic and copies ran while one was open for 3% of the time, Pallas kernels for 25%

profile of v3, /device:TPU:1, one launch (start us, length us, event | category | flops | bytes accessed | tf_op | source)
XLA Modules:
  0.0 155.2 jit_solution(14718418683308825237)
XLA Ops:
  6.5 1.6 %slice.43 = f32[3,1,128,128]{3,2,1,0:T(8,128)} slice(f32[3,12,128,128]{3,2,1,0:T(8,128)} %bitcast.45), slice={[0:3], [0:1], [0:128], [0:128]} | slice | bytes 393216 | tf_op jit(solution)/shard_map/slice | solution.py:409
  9.1 5.5 %collective-permute-start = (f32[128,128]{1,0:T(8,128)S(1)}, f32[128,128]{1,0:T(8,128)S(1)}, u32[]{:S(2)}, u32[]{:S(2)}) collective-permute-start(f32[128,128]{1,0:T(8,128)S(1)} %slice_bitcast_fusion.5), channel_id=1, source_target_pairs={{0,128},{1,129},{2,130},{3,131},{4,132},{5,133},{6,134},{7,135},{8... | collective-permute-start | bytes 196616 | tf_op jit(solution)/shard_map/ppermute | solution.py:386
  14.6 1.3 collective-permute-start.1
  15.9 1.3 collective-permute-start.2
  17.2 1.2 slice_bitcast_fusion
  19.4 2.6 %collective-permute-start.11 = (f32[12,32,128]{2,1,0:T(8,128)S(1)}, f32[12,32,128]{2,1,0:T(8,128)S(1)}, u32[]{:S(2)}, u32[]{:S(2)}) collective-permute-start(f32[12,32,128]{2,1,0:T(8,128)S(1)} %get-tuple-element.33), channel_id=1, source_target_pairs={{0,128},{1,129},{2,130},{3,131},{4,132},{5,133},{6,134},{7,135},{8... | collective-permute-start | bytes 589832 | tf_op jit(solution)/shard_map/ppermute | solution.py:386
  22.0 1.7 %collective-permute-start.12 = (f32[12,32,128]{2,1,0:T(8,128)S(1)}, f32[12,32,128]{2,1,0:T(8,128)S(1)}, u32[]{:S(2)}, u32[]{:S(2)}) collective-permute-start(f32[12,32,128]{2,1,0:T(8,128)S(1)} %get-tuple-element.32), channel_id=1, source_target_pairs={{0,192},{1,193},{2,194},{3,195},{4,196},{5,197},{6,198},{7,199},{8... | collective-permute-start | bytes 589832 | tf_op jit(solution)/shard_map/ppermute | solution.py:386
  23.7 1.3 collective-permute-start.13
  25.0 1.3 collective-permute-done.12
  26.3 3.4 %collective-permute-done.13 = f32[12,32,128]{2,1,0:T(8,128)S(1)} collective-permute-done((f32[12,32,128]{2,1,0:T(8,128)S(1)}, f32[12,32,128]{2,1,0:T(8,128)S(1)}, u32[]{:S(2)}, u32[]{:S(2)}) %collective-permute-start.13) | collective-permute-done | bytes 196640 | tf_op jit(solution)/shard_map/ppermute | solution.py:386
  30.5 29.1 %all_to_all.5 = f32[8,128,128]{2,1,0:T(8,128)S(1)} all-to-all(f32[8,128,128]{2,1,0:T(8,128)S(1)} %broadcast_in_dim.3), channel_id=1, replica_groups=mesh['x'=4,'y'=4,'k'=2,'z'=8] {'z'}, dimensions={0} | all-to-all | bytes 1048576 | tf_op jit(solution)/shard_map/all_to_all | solution.py:416
  59.6 3.4 %collective-permute-start.3 = (f32[4,128,128]{2,1,0:T(8,128)S(1)}, f32[4,128,128]{2,1,0:T(8,128)S(1)}, u32[]{:S(2)}, u32[]{:S(2)}) collective-permute-start(f32[4,128,128]{2,1,0:T(8,128)S(1)} %slice.41), channel_id=1, source_target_pairs={{0,16},{16,0},{1,17},{17,1},{2,18},{18,2},{3,19},{19,3},{4,20},{20... | collective-permute-start | bytes 786440 | tf_op jit(solution)/shard_map/ppermute | solution.py:386
  63.0 2.0 %collective-permute-start.4 = (f32[4,128,128]{2,1,0:T(8,128)S(1)}, f32[4,128,128]{2,1,0:T(8,128)S(1)}, u32[]{:S(2)}, u32[]{:S(2)}) collective-permute-start(f32[4,128,128]{2,1,0:T(8,128)S(1)} %slice.41), channel_id=1, source_target_pairs={{0,32},{16,48},{1,33},{17,49},{2,34},{18,50},{3,35},{19,51},{4,36}... | collective-permute-start | bytes 786440 | tf_op jit(solution)/shard_map/ppermute | solution.py:386
  65.0 1.3 collective-permute-start.5
  66.4 1.5 collective-permute-done.3
  67.8 5.1 %collective-permute-done.4 = f32[4,128,128]{2,1,0:T(8,128)S(1)} collective-permute-done((f32[4,128,128]{2,1,0:T(8,128)S(1)}, f32[4,128,128]{2,1,0:T(8,128)S(1)}, u32[]{:S(2)}, u32[]{:S(2)}) %collective-permute-start.4) | collective-permute-done | bytes 262176 | tf_op jit(solution)/shard_map/ppermute | solution.py:386
  73.0 4.9 %collective-permute-done.5 = f32[4,128,128]{2,1,0:T(8,128)S(1)} collective-permute-done((f32[4,128,128]{2,1,0:T(8,128)S(1)}, f32[4,128,128]{2,1,0:T(8,128)S(1)}, u32[]{:S(2)}, u32[]{:S(2)}) %collective-permute-start.5) | collective-permute-done | bytes 262176 | tf_op jit(solution)/shard_map/ppermute | solution.py:386
  78.0 2.8 %collective-permute-start.6 = (f32[2,4,128,128]{3,2,1,0:T(8,128)S(1)}, f32[2,4,128,128]{3,2,1,0:T(8,128)S(1)}, u32[]{:S(2)}, u32[]{:S(2)}) collective-permute-start(f32[2,4,128,128]{3,2,1,0:T(8,128)S(1)} %pad_maximum_fusion.1.near_ref), channel_id=1, source_target_pairs={{0,8},{8,0},{1,9},{9,1},{2,10},{10,2},{3,11},{11,3},{4,12},{12,4},... | collective-permute-start | bytes 1572872 | tf_op jit(solution)/shard_map/ppermute | solution.py:382
  80.9 1.5 collective-permute-done.6.far_ref
  82.3 4.6 %collective-permute-start.8 = (f32[4,128,128]{2,1,0:T(8,128)S(1)}, f32[4,128,128]{2,1,0:T(8,128)S(1)}, u32[]{:S(2)}, u32[]{:S(2)}) collective-permute-start(f32[4,128,128]{2,1,0:T(8,128)S(1)} %get-tuple-element.22), channel_id=1, source_target_pairs={{0,32},{16,48},{32,0},{48,16},{1,33},{17,49},{33,1},{49,17},{2,34}... | collective-permute-start | bytes 786440 | tf_op jit(solution)/shard_map/ppermute | solution.py:386
  86.9 13.8 %first.1.w0_ref = f32[768,512]{1,0:T(8,128)S(1)} custom-call(s32[4]{0:T(128)S(1)} %pad_add_fusion.ids_ref, f32[2,4,128,128]{3,2,1,0:T(8,128)S(1)} %pad_maximum_fusion.1.near_ref, f32[2,4,128,128]{3,2,1,0:T(8,128)S(1)} %collective-permute-done.6.far_ref), custom_call_target="tpu_custom_call" | custom-call | flops 8589934592 | bytes 4194304 | tf_op jit(solution)/shard_map/first/pallas_call | solution.py:190
  100.7 1.1 copy-done.8
  102.0 1.2 collective-permute-start.10
  103.2 2.3 %collective-permute-done.10.far_ref = f32[4,4,128,128]{3,2,1,0:T(8,128)S(1)} collective-permute-done((f32[4,4,128,128]{3,2,1,0:T(8,128)S(1)}, f32[4,4,128,128]{3,2,1,0:T(8,128)S(1)}, u32[]{:S(2)}, u32[]{:S(2)}) %collective-permute-start.10) | collective-permute-done | bytes 1048608 | tf_op jit(solution)/shard_map/ppermute | solution.py:382
  105.5 1.1 copy-done.6
  106.5 1.4 copy-done.5
  108.0 1.2 copy-done.7
  109.2 1.5 copy-done.9
  110.7 25.3 %second.1 = (bf16[2,384,1024]{2,1,0:T(8,128)(2,1)S(1)}, f32[3,128,128]{2,1,0:T(8,128)S(1)}) custom-call(s32[4]{0:T(128)S(1)} %pad_add_fusion.ids_ref, f32[768,512]{1,0:T(8,128)S(1)} %copy-done.9, f32[4,4,128,128]{3,2,1,0:T(8,128)S(1)} %pad_maximum_fusion.near_ref, f32[4,4,128,128]{3,2,1,0:T(8,128)S(1)} %copy-done.7, f32[8,3,128,128]{3,2,1,0:T(8,128)S(1)} %bitcast.50), custom_call_target="tpu_custom_call" | custom-call | flops 17179869184 | bytes 8388608 | tf_op jit(solution)/shard_map/second/pallas_call | solution.py:312
  136.0 1.1 copy-done.1
  137.8 1.4 copy-done.2
  140.2 8.2 %update.1 = f32[3,12,128,128]{3,2,1,0:T(8,128)} custom-call(s32[4]{0:T(128)S(1)} %pad_add_fusion.ids_ref, bf16[2,384,1024]{2,1,0:T(8,128)(2,1)S(1)} %copy-done.2, f32[3,128,128]{2,1,0:T(8,128)S(1)} %copy-done.4, f32[4,8,12,32,128]{4,3,2,1,0:T(8,128)} %bitcast.51, f32[3,12,128,128]{3,2,1,0:T(8,128)S(1)} %bitcast.49), custom_call_target="tpu_custom_call" | custom-call | tf_op jit(solution)/shard_map/update/pallas_call | solution.py:364
  (38 shorter events, 4.6 us)
Async XLA Ops:
  6.5 96.6 %all-gather.5.cloned.1.call-start = ((), (), s32[]{:S(2)}) async-start(), calls=%async_computation.1 | async-start | bytes 1769472 | tf_op jit(solution)/shard_map/all_gather | solution.py:409
  8.2 129.6 %all-gather.7.cloned.1.call-start = ((), (), s32[]{:S(2)}) async-start(), calls=%async_computation.2 | async-start | bytes 6488064 | tf_op jit(solution)/shard_map/all_gather | solution.py:421
  9.1 9.3 %collective-permute-start = (f32[128,128]{1,0:T(8,128)S(1)}, f32[128,128]{1,0:T(8,128)S(1)}, u32[]{:S(2)}, u32[]{:S(2)}) collective-permute-start(f32[128,128]{1,0:T(8,128)S(1)} %slice_bitcast_fusion.5), channel_id=1, source_target_pairs={{0,128},{1,129},{2,130},{3,131},{4,132},{5,133},{6,134},{7,135},{8... | collective-permute-start | bytes 196616 | tf_op jit(solution)/shard_map/ppermute | solution.py:386
  14.6 3.8 %collective-permute-start.1 = (f32[128,128]{1,0:T(8,128)S(1)}, f32[128,128]{1,0:T(8,128)S(1)}, u32[]{:S(2)}, u32[]{:S(2)}) collective-permute-start(f32[128,128]{1,0:T(8,128)S(1)} %slice_bitcast_fusion.5), channel_id=1, source_target_pairs={{0,192},{1,193},{2,194},{3,195},{4,196},{5,197},{6,198},{7,199},{8... | collective-permute-start | bytes 196616 | tf_op jit(solution)/shard_map/ppermute | solution.py:386
  15.9 2.6 %collective-permute-start.2 = (f32[128,128]{1,0:T(8,128)S(1)}, f32[128,128]{1,0:T(8,128)S(1)}, u32[]{:S(2)}, u32[]{:S(2)}) collective-permute-start(f32[128,128]{1,0:T(8,128)S(1)} %slice_bitcast_fusion.5), channel_id=1, source_target_pairs={{0,64},{1,65},{2,66},{3,67},{4,68},{5,69},{6,70},{7,71},{8,72},{9,... | collective-permute-start | bytes 196616 | tf_op jit(solution)/shard_map/ppermute | solution.py:386
  19.4 5.6 %collective-permute-start.11 = (f32[12,32,128]{2,1,0:T(8,128)S(1)}, f32[12,32,128]{2,1,0:T(8,128)S(1)}, u32[]{:S(2)}, u32[]{:S(2)}) collective-permute-start(f32[12,32,128]{2,1,0:T(8,128)S(1)} %get-tuple-element.33), channel_id=1, source_target_pairs={{0,128},{1,129},{2,130},{3,131},{4,132},{5,133},{6,134},{7,135},{8... | collective-permute-start | bytes 589832 | tf_op jit(solution)/shard_map/ppermute | solution.py:386
  22.0 4.3 %collective-permute-start.12 = (f32[12,32,128]{2,1,0:T(8,128)S(1)}, f32[12,32,128]{2,1,0:T(8,128)S(1)}, u32[]{:S(2)}, u32[]{:S(2)}) collective-permute-start(f32[12,32,128]{2,1,0:T(8,128)S(1)} %get-tuple-element.32), channel_id=1, source_target_pairs={{0,192},{1,193},{2,194},{3,195},{4,196},{5,197},{6,198},{7,199},{8... | collective-permute-start | bytes 589832 | tf_op jit(solution)/shard_map/ppermute | solution.py:386
  23.7 6.0 %collective-permute-start.13 = (f32[12,32,128]{2,1,0:T(8,128)S(1)}, f32[12,32,128]{2,1,0:T(8,128)S(1)}, u32[]{:S(2)}, u32[]{:S(2)}) collective-permute-start(f32[12,32,128]{2,1,0:T(8,128)S(1)} %get-tuple-element.31), channel_id=1, source_target_pairs={{0,64},{1,65},{2,66},{3,67},{4,68},{5,69},{6,70},{7,71},{8,72},{9,... | collective-permute-start | bytes 589832 | tf_op jit(solution)/shard_map/ppermute | solution.py:386
  59.6 8.3 %collective-permute-start.3 = (f32[4,128,128]{2,1,0:T(8,128)S(1)}, f32[4,128,128]{2,1,0:T(8,128)S(1)}, u32[]{:S(2)}, u32[]{:S(2)}) collective-permute-start(f32[4,128,128]{2,1,0:T(8,128)S(1)} %slice.41), channel_id=1, source_target_pairs={{0,16},{16,0},{1,17},{17,1},{2,18},{18,2},{3,19},{19,3},{4,20},{20... | collective-permute-start | bytes 786440 | tf_op jit(solution)/shard_map/ppermute | solution.py:386
  63.0 10.0 %collective-permute-start.4 = (f32[4,128,128]{2,1,0:T(8,128)S(1)}, f32[4,128,128]{2,1,0:T(8,128)S(1)}, u32[]{:S(2)}, u32[]{:S(2)}) collective-permute-start(f32[4,128,128]{2,1,0:T(8,128)S(1)} %slice.41), channel_id=1, source_target_pairs={{0,32},{16,48},{1,33},{17,49},{2,34},{18,50},{3,35},{19,51},{4,36}... | collective-permute-start | bytes 786440 | tf_op jit(solution)/shard_map/ppermute | solution.py:386
  65.0 12.8 %collective-permute-start.5 = (f32[4,128,128]{2,1,0:T(8,128)S(1)}, f32[4,128,128]{2,1,0:T(8,128)S(1)}, u32[]{:S(2)}, u32[]{:S(2)}) collective-permute-start(f32[4,128,128]{2,1,0:T(8,128)S(1)} %slice.41), channel_id=1, source_target_pairs={{0,48},{16,32},{1,49},{17,33},{2,50},{18,34},{3,51},{19,35},{4,52}... | collective-permute-start | bytes 786440 | tf_op jit(solution)/shard_map/ppermute | solution.py:386
  78.0 4.3 %collective-permute-start.6 = (f32[2,4,128,128]{3,2,1,0:T(8,128)S(1)}, f32[2,4,128,128]{3,2,1,0:T(8,128)S(1)}, u32[]{:S(2)}, u32[]{:S(2)}) collective-permute-start(f32[2,4,128,128]{3,2,1,0:T(8,128)S(1)} %pad_maximum_fusion.1.near_ref), channel_id=1, source_target_pairs={{0,8},{8,0},{1,9},{9,1},{2,10},{10,2},{3,11},{11,3},{4,12},{12,4},... | collective-permute-start | bytes 1572872 | tf_op jit(solution)/shard_map/ppermute | solution.py:382
  82.3 19.5 %collective-permute-start.7 = (f32[4,128,128]{2,1,0:T(8,128)S(1)}, f32[4,128,128]{2,1,0:T(8,128)S(1)}, u32[]{:S(2)}, u32[]{:S(2)}) collective-permute-start(f32[4,128,128]{2,1,0:T(8,128)S(1)} %get-tuple-element.22), channel_id=1, source_target_pairs={{0,16},{16,32},{32,48},{48,0},{1,17},{17,33},{33,49},{49,1},{2,18}... | collective-permute-start | bytes 786440 | tf_op jit(solution)/shard_map/ppermute | solution.py:386
  82.3 19.5 %collective-permute-start.8 = (f32[4,128,128]{2,1,0:T(8,128)S(1)}, f32[4,128,128]{2,1,0:T(8,128)S(1)}, u32[]{:S(2)}, u32[]{:S(2)}) collective-permute-start(f32[4,128,128]{2,1,0:T(8,128)S(1)} %get-tuple-element.22), channel_id=1, source_target_pairs={{0,32},{16,48},{32,0},{48,16},{1,33},{17,49},{33,1},{49,17},{2,34}... | collective-permute-start | bytes 786440 | tf_op jit(solution)/shard_map/ppermute | solution.py:386
  86.9 14.9 %collective-permute-start.9 = (f32[4,128,128]{2,1,0:T(8,128)S(1)}, f32[4,128,128]{2,1,0:T(8,128)S(1)}, u32[]{:S(2)}, u32[]{:S(2)}) collective-permute-start(f32[4,128,128]{2,1,0:T(8,128)S(1)} %get-tuple-element.22), channel_id=1, source_target_pairs={{0,48},{16,0},{32,16},{48,32},{1,49},{17,1},{33,17},{49,33},{2,50}... | collective-permute-start | bytes 786440 | tf_op jit(solution)/shard_map/ppermute | solution.py:386
  100.7 1.1 copy-start.8
  102.0 3.5 %collective-permute-start.10 = (f32[4,4,128,128]{3,2,1,0:T(8,128)S(1)}, f32[4,4,128,128]{3,2,1,0:T(8,128)S(1)}, u32[]{:S(2)}, u32[]{:S(2)}) collective-permute-start(f32[4,4,128,128]{3,2,1,0:T(8,128)S(1)} %pad_maximum_fusion.near_ref), channel_id=1, source_target_pairs={{0,8},{8,0},{1,9},{9,1},{2,10},{10,2},{3,11},{11,3},{4,12},{12,4},... | collective-permute-start | bytes 3145736 | tf_op jit(solution)/shard_map/ppermute | solution.py:382
  105.4 1.1 copy-start.6
  106.5 1.4 copy-start.5
  108.0 1.2 copy-start.7
  109.2 1.5 copy-start.9
  110.7 27.1 %copy-start = (f32[3,128,12,128]{3,1,2,0:T(8,128)S(1)}, f32[3,128,12,128]{3,1,2,0:T(8,128)}, u32[]{:S(2)}) copy-start(f32[3,128,12,128]{3,1,2,0:T(8,128)} %param.1) | copy-start | bytes 7077892
  136.0 1.1 copy-start.1
  137.1 0.7 copy-start.3
  137.8 1.4 copy-start.2
  139.2 0.9 copy-start.4
Sparse Core Ops, SparseCore 0:
  9.1 46.5 all-gather.4
  58.3 62.2 all-gather.6

commit v4 on v3

--- a/solution.py
+++ b/solution.py
@@ -12,6 +12,7 @@
 WIDTH = TILE * TILES
 PANEL = TILE * HALF
 GROUP = 16
+GRANT = 24 << 20
 ROW = ("x", "y", "k")
 VMEM = pl.BlockSpec(memory_space=pltpu.VMEM)
 SMEM = pl.BlockSpec(memory_space=pltpu.SMEM)
@@ -193,7 +194,7 @@
         in_specs=[SMEM, VMEM, VMEM],
         out_specs=VMEM,
         scratch_shapes=panel_scratch(),
-        compiler_params=pltpu.CompilerParams(vmem_limit_bytes=24 << 20),
+        compiler_params=pltpu.CompilerParams(vmem_limit_bytes=GRANT),
         cost_estimate=pl.CostEstimate(flops=8 << 30, bytes_accessed=4 << 20, transcendentals=0),
         name="first",
     )(ids, near, far)
@@ -297,14 +298,22 @@
 
 
 def second_kernel(
-    ids_ref, w0_ref, near_ref, far_ref, own_hbm, t_ref, c_ref,
-    own_ref, arrived, x_ref, w1_ref, s_ref, b_ref, *scratch
+    ids_ref, w0_ref, near_ref, far_ref, own_hbm, t_hbm, c_hbm,
+    t_ref, c_ref, own_ref, sems, x_ref, w1_ref, s_ref, b_ref, *scratch
 ):
-    copy = pltpu.make_async_copy(own_hbm, own_ref, arrived)
+    copy = pltpu.make_async_copy(own_hbm, own_ref, sems.at[0])
     copy.start()
     factor_second(ids_ref, w0_ref, near_ref, far_ref, x_ref, w1_ref, b_ref, *scratch)
     copy.wait()
     apply_inverse(ids_ref, own_ref, w0_ref, x_ref, w1_ref, t_ref, c_ref, s_ref)
+    out = [
+        pltpu.make_async_copy(t_ref, t_hbm, sems.at[1]),
+        pltpu.make_async_copy(c_ref, c_hbm, sems.at[2]),
+    ]
+    for copy in out:
+        copy.start()
+    for copy in out:
+        copy.wait()
 
 
 def second(ids, w0, near, far, own):
@@ -316,17 +325,19 @@
             jax.ShapeDtypeStruct((own.shape[1], TILE, TILE), jnp.float32),
         ],
         in_specs=[SMEM, VMEM, VMEM, VMEM, pl.BlockSpec(memory_space=pl.ANY)],
-        out_specs=[VMEM, VMEM],
+        out_specs=[pl.BlockSpec(memory_space=pltpu.HBM)] * 2,
         scratch_shapes=[
+            pltpu.VMEM((2, rows, WIDTH), jnp.bfloat16),
+            pltpu.VMEM((own.shape[1], TILE, TILE), jnp.float32),
             pltpu.VMEM(own.shape, jnp.float32),
-            pltpu.SemaphoreType.DMA,
+            pltpu.SemaphoreType.DMA((3,)),
             pltpu.VMEM((PANEL, PANEL), jnp.float32),
             pltpu.VMEM(FACTOR, jnp.float32),
             pltpu.VMEM((rows, WIDTH), jnp.float32),
             pltpu.VMEM((WIDTH, PANEL), jnp.float32),
         ]
         + panel_scratch(),
-        compiler_params=pltpu.CompilerParams(vmem_limit_bytes=40 << 20),
+        compiler_params=pltpu.CompilerParams(vmem_limit_bytes=GRANT),
         cost_estimate=pl.CostEstimate(flops=16 << 30, bytes_accessed=8 << 20, transcendentals=0),
         name="second",
     )(ids, w0, near, far, own)
@@ -337,7 +348,14 @@
     tiles, _, _ = c_ref.shape
     rows = tiles * TILE
     quarters = [
-        jnp.concatenate([right_ref[x, r, i] for r in range(TILES) for x in range(4)], 0)
+        jnp.concatenate(
+            [
+                right_ref[x, r, i]
+                for r in range(TILES)
+                for x in range(4)
+            ],
+            0,
+        )
         for i in range(2)
     ]
     right = jnp.concatenate(quarters, 1)
@@ -373,7 +391,7 @@
             block,
         ],
         out_specs=block,
-        compiler_params=pltpu.CompilerParams(vmem_limit_bytes=44 << 20),
+        compiler_params=pltpu.CompilerParams(vmem_limit_bytes=60 << 20),
         name="update",
     )(ids, t, c, right, kernel)
 
@@ -397,9 +415,28 @@
     return near, swap(near)
 
 
-def gather_second(strip):
+def round_y(block):
     n = lax.axis_size("y")
-    return [strip] + [send(strip, "y", [(i, (i + d) % n) for i in range(n)]) for d in range(1, n)]
+    return [block] + [send(block, "y", [(i, (i + d) % n) for i in range(n)]) for d in range(1, n)]
+
+
+def gather_z(block, later):
+    n = lax.axis_size("z")
+    k, z = lax.axis_index("k"), lax.axis_index("z")
+    pair = jnp.stack([block, swap(block)])
+    parts = []
+    for d in (1, 2, 3):
+        up = [(i, (i + d) % n) for i in range(n)]
+        down = [(n + i, n + (i - d) % n) for i in range(n)]
+        parts.append(send(pair, ("k", "z"), up + down))
+    far = send(block, "z", [(i, (i + n // 2) % n) for i in range(n)])
+    parts, later = lax.optimization_barrier((parts, later))
+    mine = jnp.stack([p[0] for p in parts])
+    other = swap(jnp.stack([p[1] for p in parts]))
+    below = jnp.where(k == 0, mine, other)
+    above = jnp.where(k == 0, other, mine)
+    ring = jnp.concatenate([block[None], above, far[None], below[::-1]])
+    return lax.dynamic_slice_in_dim(jnp.concatenate([ring, ring]), (n - z) % n, n, 0), later
 
 
 def body(kernel):
@@ -411,19 +448,19 @@
     corner = kernel[0, 0]
     for d in (1, 3, 2):
         corner = jnp.where(x == d, send(kernel[0, 0], "x", [(0, d)]), corner)
-    corner, head = lax.optimization_barrier((corner, kernel[0]))
-    spread = jnp.broadcast_to(corner, (TILES, TILE, TILE))
-    strip = lax.all_to_all(spread, "z", 0, 0)
+    strip, head = gather_z(corner, kernel[0])
     quarters = head.reshape(-1, 4, TILE // 4, TILE)
+    pieces = [send(quarters[:, d], "x", [(0, d)]) for d in (1, 3, 2)]
+    strip, pieces = lax.optimization_barrier((strip, pieces))
     quarter = quarters[:, 0]
-    for d in (1, 3, 2):
-        quarter = jnp.where(x == d, send(quarters[:, d], "x", [(0, d)]), quarter)
+    for d, piece in zip((1, 3, 2), pieces):
+        quarter = jnp.where(x == d, piece, quarter)
     right = lax.all_gather(quarter, ROW)
     right = right.reshape(4, TILES, -1, TILE // 4, TILE)
 
     near, far = gather_first(strip[:HALF])
-    near, far, rest = lax.optimization_barrier((near, far, strip[HALF:]))
-    parts = gather_second(rest)
+    near, far, rest, own = lax.optimization_barrier((near, far, strip[HALF:], own))
+    parts = round_y(rest)
     w0 = first(ids, near, far)
     w0, parts = lax.optimization_barrier((w0, parts))
     more = jnp.stack(parts)

time: 157 us -> 144 us (0.917)
  blocking collectives: 29.1 us -> 0 us
  starting transfers between devices: 29 us -> 50.7 us
  local copies, waits for them, and re-layouts: 14.3 us -> 5.65 us
  waiting for transfers between devices: 20 us -> 22.4 us
    all_to_all x1 -> x0, blocking collectives: 29.1 us -> none  [body(): strip = lax.all_to_all(spread, 'z', 0, 0)]
    ppermute x12 -> x16, starting transfers between devices: 25 us -> 38.6 us  [send(): return lax.ppermute(x, axis, pairs)]
    unnamed x20 -> x12, local copies, waits for them, and re-layouts: 10.5 us -> 1.86 us
    ppermute x2 -> x4, starting transfers between devices: 3.99 us -> 12.1 us  [swap(): return lax.ppermute(x, 'k', [(0, 1), (1, 0)])]
    ppermute x12 -> x16, waiting for transfers between devices: 16.2 us -> 18.6 us  [send(): return lax.ppermute(x, axis, pairs)]
    ppermute x2 -> x4, waiting for transfers between devices: 3.74 us -> 3.75 us  [swap(): return lax.ppermute(x, 'k', [(0, 1), (1, 0)])]
  transfers between devices with their start and end apart: 16 -> 22, of which waited for: 8 -> 10; matrix products, arithmetic and copies ran while one was open for 3% -> 3% of each run, Pallas kernels for 25% -> 28%
where the time goes in v4:
time: 144 us; the launch traced here: 143 us
  starting transfers between devices  50.7 us (35%)
  Pallas kernels  48.5 us (34%)
  waiting for transfers between devices  22.4 us (16%)
  between operations  13.7 us (10%)
  local copies, waits for them, and re-layouts  5.65 us (4%)
  other arithmetic  2.01 us (1%)
    ppermute x16, starting transfers between devices, send(): return lax.ppermute(x, axis, pairs)  38.6 us
    pallas_call x1, Pallas kernels, second(): pl.pallas_call(second_kernel, out_shape=[jax.ShapeDtypeStruct((2, rows, W...  25.7 us
    ppermute x16, waiting for transfers between devices, send(): return lax.ppermute(x, axis, pairs)  18.6 us
    pallas_call x1, Pallas kernels, first(): pl.pallas_call(first_kernel, out_shape=jax.ShapeDtypeStruct(FACTOR, jnp.f...  13.8 us
    ppermute x4, starting transfers between devices, swap(): return lax.ppermute(x, 'k', [(0, 1), (1, 0)])  12.1 us
    pallas_call x1, Pallas kernels, update(): pl.pallas_call(update_kernel, grid=(columns // 2,), out_shape=jax.ShapeDt...  9 us
    ppermute x4, waiting for transfers between devices, swap(): return lax.ppermute(x, 'k', [(0, 1), (1, 0)])  3.75 us
  transfers between devices with their start and end apart: 22, of which 10 were waited for; matrix products, arithmetic and copies ran while one was open for 3% of the time, Pallas kernels for 28%

profile of v4, /device:TPU:1, one launch (start us, length us, event | category | flops | bytes accessed | tf_op | source)
XLA Modules:
  0.0 143.0 jit_solution(18381393614922418870)
XLA Ops:
  7.4 5.5 %collective-permute-start = (f32[128,128]{1,0:T(8,128)S(1)}, f32[128,128]{1,0:T(8,128)S(1)}, u32[]{:S(2)}, u32[]{:S(2)}) collective-permute-start(f32[128,128]{1,0:T(8,128)S(1)} %slice_bitcast_fusion.5), channel_id=1, source_target_pairs={{0,128},{1,129},{2,130},{3,131},{4,132},{5,133},{6,134},{7,135},{8... | collective-permute-start | bytes 196616 | tf_op jit(solution)/shard_map/ppermute | solution.py:404
  12.9 1.3 collective-permute-start.1
  14.2 1.3 collective-permute-start.2
  15.5 1.3 collective-permute-done.2
  17.6 1.6 %collective-permute-start.3 = (f32[128,128]{1,0:T(8,128)S(1)}, f32[128,128]{1,0:T(8,128)S(1)}, u32[]{:S(2)}, u32[]{:S(2)}) collective-permute-start(f32[128,128]{1,0:T(8,128)S(1)} %get-tuple-element.44), channel_id=1, source_target_pairs={{0,8},{8,0},{1,9},{9,1},{2,10},{10,2},{3,11},{11,3},{4,12},{12,4},... | collective-permute-start | bytes 196616 | tf_op jit(solution)/shard_map/ppermute | solution.py:400
  19.2 1.6 %slice.68 = f32[3,1,128,128]{3,2,1,0:T(8,128)} slice(f32[3,12,128,128]{3,2,1,0:T(8,128)} %bitcast.57), slice={[0:3], [0:1], [0:128], [0:128]} | slice | bytes 393216 | tf_op jit(solution)/shard_map/slice | solution.py:446
  21.0 5.7 %collective-permute-start.4 = (f32[2,128,128]{2,1,0:T(8,128)S(1)}, f32[2,128,128]{2,1,0:T(8,128)S(1)}, u32[]{:S(2)}, u32[]{:S(2)}) collective-permute-start(f32[2,128,128]{2,1,0:T(8,128)S(1)} %pad_maximum_fusion.4), channel_id=1, source_target_pairs={{0,1},{1,2},{2,3},{3,4},{4,5},{5,6},{6,7},{7,0},{8,15},{9,8},{10,9... | collective-permute-start | bytes 393224 | tf_op jit(solution)/shard_map/ppermute | solution.py:404
  26.6 1.2 collective-permute-start.5
  28.2 1.2 slice_bitcast_fusion
  29.4 4.6 %collective-permute-start.8 = (f32[128,128]{1,0:T(8,128)S(1)}, f32[128,128]{1,0:T(8,128)S(1)}, u32[]{:S(2)}, u32[]{:S(2)}) collective-permute-start(f32[128,128]{1,0:T(8,128)S(1)} %get-tuple-element.44), channel_id=1, source_target_pairs={{0,4},{1,5},{2,6},{3,7},{4,0},{5,1},{6,2},{7,3},{8,12},{9,13},{10,... | collective-permute-start | bytes 196616 | tf_op jit(solution)/shard_map/ppermute | solution.py:404
  34.1 8.0 %collective-permute-start.7 = (f32[3,128,128]{2,1,0:T(8,128)S(1)}, f32[3,128,128]{2,1,0:T(8,128)S(1)}, u32[]{:S(2)}, u32[]{:S(2)}) collective-permute-start(f32[3,128,128]{2,1,0:T(8,128)S(1)} %pad_maximum_fusion.2), channel_id=1, source_target_pairs={{0,8},{8,0},{1,9},{9,1},{2,10},{10,2},{3,11},{11,3},{4,12},{12,4},... | collective-permute-start | bytes 589832 | tf_op jit(solution)/shard_map/ppermute | solution.py:400
  42.1 4.0 %collective-permute-start.9 = (f32[12,32,128]{2,1,0:T(8,128)S(1)}, f32[12,32,128]{2,1,0:T(8,128)S(1)}, u32[]{:S(2)}, u32[]{:S(2)}) collective-permute-start(f32[12,32,128]{2,1,0:T(8,128)S(1)} %get-tuple-element.49), channel_id=1, source_target_pairs={{0,64},{1,65},{2,66},{3,67},{4,68},{5,69},{6,70},{7,71},{8,72},{9,... | collective-permute-start | bytes 589832 | tf_op jit(solution)/shard_map/ppermute | solution.py:404
  46.1 1.3 collective-permute-start.10
  47.4 1.3 collective-permute-start.11
  49.0 1.4 %collective-permute-done.9 = f32[12,32,128]{2,1,0:T(8,128)S(1)} collective-permute-done((f32[12,32,128]{2,1,0:T(8,128)S(1)}, f32[12,32,128]{2,1,0:T(8,128)S(1)}, u32[]{:S(2)}, u32[]{:S(2)}) %collective-permute-start.9) | collective-permute-done | bytes 196640 | tf_op jit(solution)/shard_map/ppermute | solution.py:404
  50.4 1.3 collective-permute-done.10
  51.7 2.9 %collective-permute-done.11 = f32[12,32,128]{2,1,0:T(8,128)S(1)} collective-permute-done((f32[12,32,128]{2,1,0:T(8,128)S(1)}, f32[12,32,128]{2,1,0:T(8,128)S(1)}, u32[]{:S(2)}, u32[]{:S(2)}) %collective-permute-start.11) | collective-permute-done | bytes 196640 | tf_op jit(solution)/shard_map/ppermute | solution.py:404
  55.5 3.3 %collective-permute-start.12 = (f32[4,128,128]{2,1,0:T(8,128)S(1)}, f32[4,128,128]{2,1,0:T(8,128)S(1)}, u32[]{:S(2)}, u32[]{:S(2)}) collective-permute-start(f32[4,128,128]{2,1,0:T(8,128)S(1)} %slice.59), channel_id=1, source_target_pairs={{0,16},{16,0},{1,17},{17,1},{2,18},{18,2},{3,19},{19,3},{4,20},{20... | collective-permute-start | bytes 786440 | tf_op jit(solution)/shard_map/ppermute | solution.py:404
  58.7 2.4 %collective-permute-start.13 = (f32[4,128,128]{2,1,0:T(8,128)S(1)}, f32[4,128,128]{2,1,0:T(8,128)S(1)}, u32[]{:S(2)}, u32[]{:S(2)}) collective-permute-start(f32[4,128,128]{2,1,0:T(8,128)S(1)} %slice.59), channel_id=1, source_target_pairs={{0,32},{16,48},{1,33},{17,49},{2,34},{18,50},{3,35},{19,51},{4,36}... | collective-permute-start | bytes 786440 | tf_op jit(solution)/shard_map/ppermute | solution.py:404
  61.1 1.3 collective-permute-start.14
  62.5 1.9 %collective-permute-done.12 = f32[4,128,128]{2,1,0:T(8,128)S(1)} collective-permute-done((f32[4,128,128]{2,1,0:T(8,128)S(1)}, f32[4,128,128]{2,1,0:T(8,128)S(1)}, u32[]{:S(2)}, u32[]{:S(2)}) %collective-permute-start.12) | collective-permute-done | bytes 262176 | tf_op jit(solution)/shard_map/ppermute | solution.py:404
  64.4 4.8 %collective-permute-done.13 = f32[4,128,128]{2,1,0:T(8,128)S(1)} collective-permute-done((f32[4,128,128]{2,1,0:T(8,128)S(1)}, f32[4,128,128]{2,1,0:T(8,128)S(1)}, u32[]{:S(2)}, u32[]{:S(2)}) %collective-permute-start.13) | collective-permute-done | bytes 262176 | tf_op jit(solution)/shard_map/ppermute | solution.py:404
  69.2 4.1 %collective-permute-done.14 = f32[4,128,128]{2,1,0:T(8,128)S(1)} collective-permute-done((f32[4,128,128]{2,1,0:T(8,128)S(1)}, f32[4,128,128]{2,1,0:T(8,128)S(1)}, u32[]{:S(2)}, u32[]{:S(2)}) %collective-permute-start.14) | collective-permute-done | bytes 262176 | tf_op jit(solution)/shard_map/ppermute | solution.py:404
  73.4 1.4 collective-permute-start.15
  74.9 1.5 %collective-permute-done.15.far_ref = f32[2,4,128,128]{3,2,1,0:T(8,128)S(1)} collective-permute-done((f32[2,4,128,128]{3,2,1,0:T(8,128)S(1)}, f32[2,4,128,128]{3,2,1,0:T(8,128)S(1)}, u32[]{:S(2)}, u32[]{:S(2)}) %collective-permute-start.15) | collective-permute-done | bytes 524320 | tf_op jit(solution)/shard_map/ppermute | solution.py:400
  76.9 4.0 %collective-permute-start.17 = (f32[4,128,128]{2,1,0:T(8,128)S(1)}, f32[4,128,128]{2,1,0:T(8,128)S(1)}, u32[]{:S(2)}, u32[]{:S(2)}) collective-permute-start(f32[4,128,128]{2,1,0:T(8,128)S(1)} %get-tuple-element.33), channel_id=1, source_target_pairs={{0,32},{16,48},{32,0},{48,16},{1,33},{17,49},{33,1},{49,17},{2,34}... | collective-permute-start | bytes 786440 | tf_op jit(solution)/shard_map/ppermute | solution.py:404
  81.5 13.8 %first.1.w0_ref = f32[768,512]{1,0:T(8,128)S(1)} custom-call(s32[4]{0:T(128)S(1)} %pad_add_fusion.ids_ref, f32[2,4,128,128]{3,2,1,0:T(8,128)S(1)} %pad_maximum_fusion.1.near_ref, f32[2,4,128,128]{3,2,1,0:T(8,128)S(1)} %collective-permute-done.15.far_ref), custom_call_target="tpu_custom_call" | custom-call | flops 8589934592 | bytes 4194304 | tf_op jit(solution)/shard_map/first/pallas_call | solution.py:191
  96.3 1.1 collective-permute-start.19
  97.4 2.3 %collective-permute-done.19.far_ref = f32[4,4,128,128]{3,2,1,0:T(8,128)S(1)} collective-permute-done((f32[4,4,128,128]{3,2,1,0:T(8,128)S(1)}, f32[4,4,128,128]{3,2,1,0:T(8,128)S(1)}, u32[]{:S(2)}, u32[]{:S(2)}) %collective-permute-start.19) | collective-permute-done | bytes 1048608 | tf_op jit(solution)/shard_map/ppermute | solution.py:400
  99.7 25.7 %second.1 = (bf16[2,384,1024]{2,1,0:T(8,128)(2,1)S(1)}, f32[3,128,128]{2,1,0:T(8,128)S(1)}) custom-call(s32[4]{0:T(128)S(1)} %pad_add_fusion.ids_ref, f32[768,512]{1,0:T(8,128)S(1)} %first.1.w0_ref, f32[4,4,128,128]{3,2,1,0:T(8,128)S(1)} %pad_maximum_fusion.near_ref, f32[4,4,128,128]{3,2,1,0:T(8,128)S(1)} %collective-permute-done.19.far_ref, ...), custom_call_target="tpu_custom_call" | custom-call | flops 17179869184 | bytes 8388608 | tf_op jit(solution)/shard_map/second/pallas_call | solution.py:321
  125.4 1.1 copy-done
  127.2 9.0 %update.1 = f32[3,12,128,128]{3,2,1,0:T(8,128)} custom-call(s32[4]{0:T(128)} %copy-done.2, bf16[2,384,1024]{2,1,0:T(8,128)(2,1)} %copy-done, f32[3,128,128]{2,1,0:T(8,128)} %copy-done.1, f32[4,8,12,32,128]{4,3,2,1,0:T(8,128)} %bitcast.54, f32[3,12,128,128]{3,2,1,0:T(8,128)} %bitcast.59), custom_call_target="tpu_custom_call" | custom-call | tf_op jit(solution)/shard_map/update/pallas_call | solution.py:382
  (48 shorter events, 6.3 us)
Async XLA Ops:
  6.5 69.8 %all-gather.5.cloned.1.call-start = ((), (), s32[]{:S(2)}) async-start(), calls=%async_computation | async-start | bytes 1769472 | tf_op jit(solution)/shard_map/all_gather | solution.py:446
  7.4 8.1 %collective-permute-start = (f32[128,128]{1,0:T(8,128)S(1)}, f32[128,128]{1,0:T(8,128)S(1)}, u32[]{:S(2)}, u32[]{:S(2)}) collective-permute-start(f32[128,128]{1,0:T(8,128)S(1)} %slice_bitcast_fusion.5), channel_id=1, source_target_pairs={{0,128},{1,129},{2,130},{3,131},{4,132},{5,133},{6,134},{7,135},{8... | collective-permute-start | bytes 196616 | tf_op jit(solution)/shard_map/ppermute | solution.py:404
  12.9 2.6 %collective-permute-start.1 = (f32[128,128]{1,0:T(8,128)S(1)}, f32[128,128]{1,0:T(8,128)S(1)}, u32[]{:S(2)}, u32[]{:S(2)}) collective-permute-start(f32[128,128]{1,0:T(8,128)S(1)} %slice_bitcast_fusion.5), channel_id=1, source_target_pairs={{0,192},{1,193},{2,194},{3,195},{4,196},{5,197},{6,198},{7,199},{8... | collective-permute-start | bytes 196616 | tf_op jit(solution)/shard_map/ppermute | solution.py:404
  14.2 2.6 %collective-permute-start.2 = (f32[128,128]{1,0:T(8,128)S(1)}, f32[128,128]{1,0:T(8,128)S(1)}, u32[]{:S(2)}, u32[]{:S(2)}) collective-permute-start(f32[128,128]{1,0:T(8,128)S(1)} %slice_bitcast_fusion.5), channel_id=1, source_target_pairs={{0,64},{1,65},{2,66},{3,67},{4,68},{5,69},{6,70},{7,71},{8,72},{9,... | collective-permute-start | bytes 196616 | tf_op jit(solution)/shard_map/ppermute | solution.py:404
  17.6 3.3 %collective-permute-start.3 = (f32[128,128]{1,0:T(8,128)S(1)}, f32[128,128]{1,0:T(8,128)S(1)}, u32[]{:S(2)}, u32[]{:S(2)}) collective-permute-start(f32[128,128]{1,0:T(8,128)S(1)} %get-tuple-element.44), channel_id=1, source_target_pairs={{0,8},{8,0},{1,9},{9,1},{2,10},{10,2},{3,11},{11,3},{4,12},{12,4},... | collective-permute-start | bytes 196616 | tf_op jit(solution)/shard_map/ppermute | solution.py:400
  20.9 106.3 %all-gather.7.cloned.1.call-start = ((), (), s32[]{:S(2)}) async-start(), calls=%async_computation.1 | async-start | bytes 6488064 | tf_op jit(solution)/shard_map/all_gather | solution.py:458
  21.0 13.1 %collective-permute-start.4 = (f32[2,128,128]{2,1,0:T(8,128)S(1)}, f32[2,128,128]{2,1,0:T(8,128)S(1)}, u32[]{:S(2)}, u32[]{:S(2)}) collective-permute-start(f32[2,128,128]{2,1,0:T(8,128)S(1)} %pad_maximum_fusion.4), channel_id=1, source_target_pairs={{0,1},{1,2},{2,3},{3,4},{4,5},{5,6},{6,7},{7,0},{8,15},{9,8},{10,9... | collective-permute-start | bytes 393224 | tf_op jit(solution)/shard_map/ppermute | solution.py:404
  26.6 7.4 %collective-permute-start.5 = (f32[2,128,128]{2,1,0:T(8,128)S(1)}, f32[2,128,128]{2,1,0:T(8,128)S(1)}, u32[]{:S(2)}, u32[]{:S(2)}) collective-permute-start(f32[2,128,128]{2,1,0:T(8,128)S(1)} %pad_maximum_fusion.4), channel_id=1, source_target_pairs={{0,2},{1,3},{2,4},{3,5},{4,6},{5,7},{6,0},{7,1},{8,14},{9,15},{10,... | collective-permute-start | bytes 393224 | tf_op jit(solution)/shard_map/ppermute | solution.py:404
  27.8 6.2 %collective-permute-start.6 = (f32[2,128,128]{2,1,0:T(8,128)S(1)}, f32[2,128,128]{2,1,0:T(8,128)S(1)}, u32[]{:S(2)}, u32[]{:S(2)}) collective-permute-start(f32[2,128,128]{2,1,0:T(8,128)S(1)} %pad_maximum_fusion.4), channel_id=1, source_target_pairs={{0,3},{1,4},{2,5},{3,6},{4,7},{5,0},{6,1},{7,2},{8,13},{9,14},{10,... | collective-permute-start | bytes 393224 | tf_op jit(solution)/shard_map/ppermute | solution.py:404
  29.4 19.4 %collective-permute-start.8 = (f32[128,128]{1,0:T(8,128)S(1)}, f32[128,128]{1,0:T(8,128)S(1)}, u32[]{:S(2)}, u32[]{:S(2)}) collective-permute-start(f32[128,128]{1,0:T(8,128)S(1)} %get-tuple-element.44), channel_id=1, source_target_pairs={{0,4},{1,5},{2,6},{3,7},{4,0},{5,1},{6,2},{7,3},{8,12},{9,13},{10,... | collective-permute-start | bytes 196616 | tf_op jit(solution)/shard_map/ppermute | solution.py:404
  34.1 14.7 %collective-permute-start.7 = (f32[3,128,128]{2,1,0:T(8,128)S(1)}, f32[3,128,128]{2,1,0:T(8,128)S(1)}, u32[]{:S(2)}, u32[]{:S(2)}) collective-permute-start(f32[3,128,128]{2,1,0:T(8,128)S(1)} %pad_maximum_fusion.2), channel_id=1, source_target_pairs={{0,8},{8,0},{1,9},{9,1},{2,10},{10,2},{3,11},{11,3},{4,12},{12,4},... | collective-permute-start | bytes 589832 | tf_op jit(solution)/shard_map/ppermute | solution.py:400
  42.1 8.3 %collective-permute-start.9 = (f32[12,32,128]{2,1,0:T(8,128)S(1)}, f32[12,32,128]{2,1,0:T(8,128)S(1)}, u32[]{:S(2)}, u32[]{:S(2)}) collective-permute-start(f32[12,32,128]{2,1,0:T(8,128)S(1)} %get-tuple-element.49), channel_id=1, source_target_pairs={{0,64},{1,65},{2,66},{3,67},{4,68},{5,69},{6,70},{7,71},{8,72},{9,... | collective-permute-start | bytes 589832 | tf_op jit(solution)/shard_map/ppermute | solution.py:404
  46.1 5.6 %collective-permute-start.10 = (f32[12,32,128]{2,1,0:T(8,128)S(1)}, f32[12,32,128]{2,1,0:T(8,128)S(1)}, u32[]{:S(2)}, u32[]{:S(2)}) collective-permute-start(f32[12,32,128]{2,1,0:T(8,128)S(1)} %get-tuple-element.48), channel_id=1, source_target_pairs={{0,192},{1,193},{2,194},{3,195},{4,196},{5,197},{6,198},{7,199},{8... | collective-permute-start | bytes 589832 | tf_op jit(solution)/shard_map/ppermute | solution.py:404
  47.4 7.2 %collective-permute-start.11 = (f32[12,32,128]{2,1,0:T(8,128)S(1)}, f32[12,32,128]{2,1,0:T(8,128)S(1)}, u32[]{:S(2)}, u32[]{:S(2)}) collective-permute-start(f32[12,32,128]{2,1,0:T(8,128)S(1)} %get-tuple-element.47), channel_id=1, source_target_pairs={{0,128},{1,129},{2,130},{3,131},{4,132},{5,133},{6,134},{7,135},{8... | collective-permute-start | bytes 589832 | tf_op jit(solution)/shard_map/ppermute | solution.py:404
  55.5 8.9 %collective-permute-start.12 = (f32[4,128,128]{2,1,0:T(8,128)S(1)}, f32[4,128,128]{2,1,0:T(8,128)S(1)}, u32[]{:S(2)}, u32[]{:S(2)}) collective-permute-start(f32[4,128,128]{2,1,0:T(8,128)S(1)} %slice.59), channel_id=1, source_target_pairs={{0,16},{16,0},{1,17},{17,1},{2,18},{18,2},{3,19},{19,3},{4,20},{20... | collective-permute-start | bytes 786440 | tf_op jit(solution)/shard_map/ppermute | solution.py:404
  58.7 10.5 %collective-permute-start.13 = (f32[4,128,128]{2,1,0:T(8,128)S(1)}, f32[4,128,128]{2,1,0:T(8,128)S(1)}, u32[]{:S(2)}, u32[]{:S(2)}) collective-permute-start(f32[4,128,128]{2,1,0:T(8,128)S(1)} %slice.59), channel_id=1, source_target_pairs={{0,32},{16,48},{1,33},{17,49},{2,34},{18,50},{3,35},{19,51},{4,36}... | collective-permute-start | bytes 786440 | tf_op jit(solution)/shard_map/ppermute | solution.py:404
  61.1 12.1 %collective-permute-start.14 = (f32[4,128,128]{2,1,0:T(8,128)S(1)}, f32[4,128,128]{2,1,0:T(8,128)S(1)}, u32[]{:S(2)}, u32[]{:S(2)}) collective-permute-start(f32[4,128,128]{2,1,0:T(8,128)S(1)} %slice.59), channel_id=1, source_target_pairs={{0,48},{16,32},{1,49},{17,33},{2,50},{18,34},{3,51},{19,35},{4,52}... | collective-permute-start | bytes 786440 | tf_op jit(solution)/shard_map/ppermute | solution.py:404
  73.4 2.9 %collective-permute-start.15 = (f32[2,4,128,128]{3,2,1,0:T(8,128)S(1)}, f32[2,4,128,128]{3,2,1,0:T(8,128)S(1)}, u32[]{:S(2)}, u32[]{:S(2)}) collective-permute-start(f32[2,4,128,128]{3,2,1,0:T(8,128)S(1)} %pad_maximum_fusion.1.near_ref), channel_id=1, source_target_pairs={{0,8},{8,0},{1,9},{9,1},{2,10},{10,2},{3,11},{11,3},{4,12},{12,4},... | collective-permute-start | bytes 1572872 | tf_op jit(solution)/shard_map/ppermute | solution.py:400
  74.9 24.8 %copy-start.2 = (s32[4]{0:T(128)}, s32[4]{0:T(128)S(1)}, u32[]{:S(2)}) copy-start(s32[4]{0:T(128)S(1)} %pad_add_fusion.ids_ref) | copy-start | bytes 52
  76.3 23.3 %copy-start.3 = (f32[24,1,128,128]{3,2,1,0:T(8,128)S(1)}, f32[24,1,128,128]{3,2,1,0:T(8,128)}, u32[]{:S(2)}) copy-start(f32[24,1,128,128]{3,2,1,0:T(8,128)} %all-gather.5.cloned.1.call-done) | copy-start | bytes 4718596
  76.3 19.0 %collective-permute-start.16 = (f32[4,128,128]{2,1,0:T(8,128)S(1)}, f32[4,128,128]{2,1,0:T(8,128)S(1)}, u32[]{:S(2)}, u32[]{:S(2)}) collective-permute-start(f32[4,128,128]{2,1,0:T(8,128)S(1)} %get-tuple-element.33), channel_id=1, source_target_pairs={{0,16},{16,32},{32,48},{48,0},{1,17},{17,33},{33,49},{49,1},{2,18}... | collective-permute-start | bytes 786440 | tf_op jit(solution)/shard_map/ppermute | solution.py:404
  76.9 19.3 %collective-permute-start.17 = (f32[4,128,128]{2,1,0:T(8,128)S(1)}, f32[4,128,128]{2,1,0:T(8,128)S(1)}, u32[]{:S(2)}, u32[]{:S(2)}) collective-permute-start(f32[4,128,128]{2,1,0:T(8,128)S(1)} %get-tuple-element.33), channel_id=1, source_target_pairs={{0,32},{16,48},{32,0},{48,16},{1,33},{17,49},{33,1},{49,17},{2,34}... | collective-permute-start | bytes 786440 | tf_op jit(solution)/shard_map/ppermute | solution.py:404
  80.9 15.3 %collective-permute-start.18 = (f32[4,128,128]{2,1,0:T(8,128)S(1)}, f32[4,128,128]{2,1,0:T(8,128)S(1)}, u32[]{:S(2)}, u32[]{:S(2)}) collective-permute-start(f32[4,128,128]{2,1,0:T(8,128)S(1)} %get-tuple-element.33), channel_id=1, source_target_pairs={{0,48},{16,0},{32,16},{48,32},{1,49},{17,1},{33,17},{49,33},{2,50}... | collective-permute-start | bytes 786440 | tf_op jit(solution)/shard_map/ppermute | solution.py:404
  96.3 3.4 %collective-permute-start.19 = (f32[4,4,128,128]{3,2,1,0:T(8,128)S(1)}, f32[4,4,128,128]{3,2,1,0:T(8,128)S(1)}, u32[]{:S(2)}, u32[]{:S(2)}) collective-permute-start(f32[4,4,128,128]{3,2,1,0:T(8,128)S(1)} %pad_maximum_fusion.near_ref), channel_id=1, source_target_pairs={{0,8},{8,0},{1,9},{9,1},{2,10},{10,2},{3,11},{11,3},{4,12},{12,4},... | collective-permute-start | bytes 3145736 | tf_op jit(solution)/shard_map/ppermute | solution.py:400
  125.4 1.2 copy-start
  126.5 0.7 copy-start.1
Sparse Core Ops, SparseCore 0:
  21.0 39.8 all-gather.4
  63.4 61.6 all-gather.6

commit v5 on v4

--- a/solution.py
+++ b/solution.py
@@ -33,6 +33,16 @@
 def right_terms(parts, axis):
     h, m, l = parts
     return jnp.concatenate([h, m, h, l, h, m], axis)
+
+
+def left_two(parts, axis):
+    h, m = parts[:2]
+    return jnp.concatenate([h, h, m], axis)
+
+
+def right_two(parts, axis):
+    h, m = parts[:2]
+    return jnp.concatenate([h, m, h], axis)
 
 
 def contract(a, b, da, db):
@@ -240,8 +250,8 @@
         a, (top, bottom) = split(a), inv
         return jnp.concatenate(
             [
-                contract(left_terms([p[:, :wide] for p in a], 1), right_terms(top, 1), 1, 1),
-                contract(left_terms(a, 1), right_terms(bottom, 1), 1, 1),
+                contract(left_two([p[:, :wide] for p in a], 1), right_two(top, 1), 1, 1),
+                contract(left_two(a, 1), right_two(bottom, 1), 1, 1),
             ],
             1,
         )
@@ -254,8 +264,8 @@
         right = [b[:, wide:] for b in bottom]
         return jnp.concatenate(
             [
-                contract(left_terms(a, 1), right_terms(both, 0), 1, 0),
-                contract(left_terms(below, 1), right_terms(right, 0), 1, 0),
+                contract(left_two(a, 1), right_two(both, 0), 1, 0),
+                contract(left_two(below, 1), right_two(right, 0), 1, 0),
             ],
             1,
         )
@@ -269,11 +279,11 @@
     x = split(x_ref[...])
     s0 = times_transpose(own(0), inv0)
     s_ref[:, :PANEL] = s0
-    rest = own(HALF) - contract(left_terms(split(s0), 1), right_terms(x, 0), 1, 0)
+    rest = own(HALF) - contract(left_two(split(s0), 1), right_two(x, 0), 1, 0)
     s1 = times_transpose(rest, inv1)
     s_ref[:, PANEL:] = s1
     t1 = times(s1, inv1)
-    t0 = times(s0 - contract(left_terms(split(t1), 1), right_terms(x, 1), 1, 1), inv0)
+    t0 = times(s0 - contract(left_two(split(t1), 1), right_two(x, 1), 1, 1), inv0)
     for start, t in ((0, t0), (PANEL, t1)):
         high = t.astype(jnp.bfloat16)
         t_ref[0, :, start : start + PANEL] = high
@@ -420,7 +430,7 @@
     return [block] + [send(block, "y", [(i, (i + d) % n) for i in range(n)]) for d in range(1, n)]
 
 
-def gather_z(block, later):
+def gather_z(block):
     n = lax.axis_size("z")
     k, z = lax.axis_index("k"), lax.axis_index("z")
     pair = jnp.stack([block, swap(block)])
@@ -430,34 +440,33 @@
         down = [(n + i, n + (i - d) % n) for i in range(n)]
         parts.append(send(pair, ("k", "z"), up + down))
     far = send(block, "z", [(i, (i + n // 2) % n) for i in range(n)])
-    parts, later = lax.optimization_barrier((parts, later))
+    parts, far = lax.optimization_barrier((parts, far))
     mine = jnp.stack([p[0] for p in parts])
     other = swap(jnp.stack([p[1] for p in parts]))
     below = jnp.where(k == 0, mine, other)
     above = jnp.where(k == 0, other, mine)
     ring = jnp.concatenate([block[None], above, far[None], below[::-1]])
-    return lax.dynamic_slice_in_dim(jnp.concatenate([ring, ring]), (n - z) % n, n, 0), later
+    return lax.dynamic_slice_in_dim(jnp.concatenate([ring, ring]), (n - z) % n, n, 0)
 
 
 def body(kernel):
     kernel = kernel.transpose(0, 2, 1, 3)
     x = lax.axis_index("x")
     ids = jnp.stack([lax.axis_index(a) for a in (ROW, "z", "y", "k")]).astype(jnp.int32)
-    own = lax.all_gather(kernel[:, 0], "z")
-
-    corner = kernel[0, 0]
+    mine, kernel = lax.optimization_barrier((kernel[:, 0], kernel))
+    own = lax.all_gather(mine, "z")
+
+    quarters = kernel[0].reshape(-1, 4, TILE // 4, TILE)
+    corner, quarter = quarters[0], quarters[:, 0]
     for d in (1, 3, 2):
-        corner = jnp.where(x == d, send(kernel[0, 0], "x", [(0, d)]), corner)
-    strip, head = gather_z(corner, kernel[0])
-    quarters = head.reshape(-1, 4, TILE // 4, TILE)
-    pieces = [send(quarters[:, d], "x", [(0, d)]) for d in (1, 3, 2)]
-    strip, pieces = lax.optimization_barrier((strip, pieces))
-    quarter = quarters[:, 0]
-    for d, piece in zip((1, 3, 2), pieces):
-        quarter = jnp.where(x == d, piece, quarter)
+        both = send(jnp.concatenate([quarters[0], quarters[:, d]]), "x", [(0, d)])
+        corner = jnp.where(x == d, both[:4], corner)
+        quarter = jnp.where(x == d, both[4:], quarter)
+    corner = corner.reshape(TILE, TILE)
     right = lax.all_gather(quarter, ROW)
     right = right.reshape(4, TILES, -1, TILE // 4, TILE)
 
+    strip = gather_z(corner)
     near, far = gather_first(strip[:HALF])
     near, far, rest, own = lax.optimization_barrier((near, far, strip[HALF:], own))
     parts = round_y(rest)

time: 144 us -> 143 us (level)
  waiting for transfers between devices: 22.4 us -> 35.3 us
  starting transfers between devices: 50.7 us -> 42.7 us
  Pallas kernels: 48.5 us -> 44.5 us
    ppermute x16 -> x13, waiting for transfers between devices: 18.6 us -> 28.6 us  [send(): return lax.ppermute(x, axis, pairs)]
    ppermute x16 -> x13, starting transfers between devices: 38.6 us -> 32.5 us  [send(): return lax.ppermute(x, axis, pairs)]
    pallas_call x1, Pallas kernels: 25.7 us -> 21.7 us  [second(): pl.pallas_call(second_kernel, out_shape=[jax.ShapeDtypeStruct((2, rows, W...]
    ppermute x4, waiting for transfers between devices: 3.75 us -> 6.65 us  [swap(): return lax.ppermute(x, 'k', [(0, 1), (1, 0)])]
    ppermute x4, starting transfers between devices: 12.1 us -> 10.2 us  [swap(): return lax.ppermute(x, 'k', [(0, 1), (1, 0)])]
  transfers between devices with their start and end apart: 22 -> 19, of which waited for: 10 -> 11; matrix products, arithmetic and copies ran while one was open for 3% -> 2% of each run, Pallas kernels for 28% -> 25%
where the time goes in v5:
time: 143 us
  Pallas kernels  44.5 us (31%)
  starting transfers between devices  42.7 us (30%)
  waiting for transfers between devices  35.3 us (25%)
  between operations  13.7 us (10%)
  local copies, waits for them, and re-layouts  5.67 us (4%)
    ppermute x13, starting transfers between devices, send(): return lax.ppermute(x, axis, pairs)  32.5 us
    ppermute x13, waiting for transfers between devices, send(): return lax.ppermute(x, axis, pairs)  28.6 us
    pallas_call x1, Pallas kernels, second(): pl.pallas_call(second_kernel, out_shape=[jax.ShapeDtypeStruct((2, rows, W...  21.7 us
    pallas_call x1, Pallas kernels, first(): pl.pallas_call(first_kernel, out_shape=jax.ShapeDtypeStruct(FACTOR, jnp.f...  13.8 us
    ppermute x4, starting transfers between devices, swap(): return lax.ppermute(x, 'k', [(0, 1), (1, 0)])  10.2 us
    pallas_call x1, Pallas kernels, update(): pl.pallas_call(update_kernel, grid=(columns // 2,), out_shape=jax.ShapeDt...  9.01 us
    ppermute x4, waiting for transfers between devices, swap(): return lax.ppermute(x, 'k', [(0, 1), (1, 0)])  6.65 us
  transfers between devices with their start and end apart: 19, of which 11 were waited for; matrix products, arithmetic and copies ran while one was open for 2% of the time, Pallas kernels for 25%

profile of v5, /device:TPU:1, one launch (start us, length us, event | category | flops | bytes accessed | tf_op | source)
XLA Modules:
  0.0 143.0 jit_solution(7188376278765681535)
XLA Ops:
  6.5 1.6 %slice_bitcast_fusion.4 = f32[3,128,128]{2,1,0:T(8,128)} fusion(f32[3,12,128,128]{3,2,1,0:T(8,128)} %bitcast.54), kind=kLoop, calls=%fused_computation.14 | loop fusion | bytes 393216 | tf_op jit(solution)/shard_map/squeeze | solution.py:456
  8.2 1.2 slice.70
  10.4 5.5 %collective-permute-start = (f32[16,32,128]{2,1,0:T(8,128)S(1)}, f32[16,32,128]{2,1,0:T(8,128)S(1)}, u32[]{:S(2)}, u32[]{:S(2)}) collective-permute-start(f32[16,32,128]{2,1,0:T(8,128)S(1)} %get-tuple-element.54), channel_id=1, source_target_pairs={{0,128},{1,129},{2,130},{3,131},{4,132},{5,133},{6,134},{7,135},{8... | collective-permute-start | bytes 786440 | tf_op jit(solution)/shard_map/ppermute | solution.py:414
  15.9 1.3 collective-permute-start.1
  17.2 1.3 collective-permute-start.2
  18.5 2.3 %collective-permute-done = f32[16,32,128]{2,1,0:T(8,128)S(1)} collective-permute-done((f32[16,32,128]{2,1,0:T(8,128)S(1)}, f32[16,32,128]{2,1,0:T(8,128)S(1)}, u32[]{:S(2)}, u32[]{:S(2)}) %collective-permute-start) | collective-permute-done | bytes 262176 | tf_op jit(solution)/shard_map/ppermute | solution.py:414
  20.8 1.3 collective-permute-done.1
  22.1 4.3 %collective-permute-done.2 = f32[16,32,128]{2,1,0:T(8,128)S(1)} collective-permute-done((f32[16,32,128]{2,1,0:T(8,128)S(1)}, f32[16,32,128]{2,1,0:T(8,128)S(1)}, u32[]{:S(2)}, u32[]{:S(2)}) %collective-permute-start.2) | collective-permute-done | bytes 262176 | tf_op jit(solution)/shard_map/ppermute | solution.py:414
  27.2 1.6 %collective-permute-start.3 = (f32[128,128]{1,0:T(8,128)S(1)}, f32[128,128]{1,0:T(8,128)S(1)}, u32[]{:S(2)}, u32[]{:S(2)}) collective-permute-start(f32[128,128]{1,0:T(8,128)S(1)} %bitcast.60), channel_id=1, source_target_pairs={{0,8},{8,0},{1,9},{9,1},{2,10},{10,2},{3,11},{11,3},{4,12},{12,4},... | collective-permute-start | bytes 196616 | tf_op jit(solution)/shard_map/ppermute | solution.py:410
  29.8 5.6 %collective-permute-start.4 = (f32[2,128,128]{2,1,0:T(8,128)S(1)}, f32[2,128,128]{2,1,0:T(8,128)S(1)}, u32[]{:S(2)}, u32[]{:S(2)}) collective-permute-start(f32[2,128,128]{2,1,0:T(8,128)S(1)} %pad_maximum_fusion.7), channel_id=1, source_target_pairs={{0,1},{1,2},{2,3},{3,4},{4,5},{5,6},{6,7},{7,0},{8,15},{9,8},{10,9... | collective-permute-start | bytes 393224 | tf_op jit(solution)/shard_map/ppermute | solution.py:414
  35.4 1.2 collective-permute-start.5
  37.1 4.5 %collective-permute-start.7 = (f32[128,128]{1,0:T(8,128)S(1)}, f32[128,128]{1,0:T(8,128)S(1)}, u32[]{:S(2)}, u32[]{:S(2)}) collective-permute-start(f32[128,128]{1,0:T(8,128)S(1)} %bitcast.62), channel_id=1, source_target_pairs={{0,4},{1,5},{2,6},{3,7},{4,0},{5,1},{6,2},{7,3},{8,12},{9,13},{10,... | collective-permute-start | bytes 196616 | tf_op jit(solution)/shard_map/ppermute | solution.py:414
  41.5 6.4 %collective-permute-done.7 = f32[128,128]{1,0:T(8,128)S(1)} collective-permute-done((f32[128,128]{1,0:T(8,128)S(1)}, f32[128,128]{1,0:T(8,128)S(1)}, u32[]{:S(2)}, u32[]{:S(2)}) %collective-permute-start.7) | collective-permute-done | bytes 65568 | tf_op jit(solution)/shard_map/ppermute | solution.py:414
  48.0 5.1 %collective-permute-done.6 = f32[2,128,128]{2,1,0:T(8,128)S(1)} collective-permute-done((f32[2,128,128]{2,1,0:T(8,128)S(1)}, f32[2,128,128]{2,1,0:T(8,128)S(1)}, u32[]{:S(2)}, u32[]{:S(2)}) %collective-permute-start.6) | collective-permute-done | bytes 131104 | tf_op jit(solution)/shard_map/ppermute | solution.py:414
  53.2 5.4 %collective-permute-start.8 = (f32[3,128,128]{2,1,0:T(8,128)S(1)}, f32[3,128,128]{2,1,0:T(8,128)S(1)}, u32[]{:S(2)}, u32[]{:S(2)}) collective-permute-start(f32[3,128,128]{2,1,0:T(8,128)S(1)} %pad_maximum_fusion.5), channel_id=1, source_target_pairs={{0,8},{8,0},{1,9},{9,1},{2,10},{10,2},{3,11},{11,3},{4,12},{12,4},... | collective-permute-start | bytes 589832 | tf_op jit(solution)/shard_map/ppermute | solution.py:410
  58.6 1.1 collective-permute-done.8
  59.9 4.4 %collective-permute-start.10 = (f32[4,128,128]{2,1,0:T(8,128)S(1)}, f32[4,128,128]{2,1,0:T(8,128)S(1)}, u32[]{:S(2)}, u32[]{:S(2)}) collective-permute-start(f32[4,128,128]{2,1,0:T(8,128)S(1)} %get-tuple-element.40), channel_id=1, source_target_pairs={{0,32},{16,48},{1,33},{17,49},{2,34},{18,50},{3,35},{19,51},{4,36}... | collective-permute-start | bytes 786440 | tf_op jit(solution)/shard_map/ppermute | solution.py:414
  64.3 1.3 collective-permute-start.11
  65.6 2.2 %collective-permute-start.9 = (f32[4,128,128]{2,1,0:T(8,128)S(1)}, f32[4,128,128]{2,1,0:T(8,128)S(1)}, u32[]{:S(2)}, u32[]{:S(2)}) collective-permute-start(f32[4,128,128]{2,1,0:T(8,128)S(1)} %get-tuple-element.40), channel_id=1, source_target_pairs={{0,16},{16,0},{1,17},{17,1},{2,18},{18,2},{3,19},{19,3},{4,20},{20... | collective-permute-start | bytes 786440 | tf_op jit(solution)/shard_map/ppermute | solution.py:414
  67.8 1.8 %collective-permute-done.10 = f32[4,128,128]{2,1,0:T(8,128)S(1)} collective-permute-done((f32[4,128,128]{2,1,0:T(8,128)S(1)}, f32[4,128,128]{2,1,0:T(8,128)S(1)}, u32[]{:S(2)}, u32[]{:S(2)}) %collective-permute-start.10) | collective-permute-done | bytes 262176 | tf_op jit(solution)/shard_map/ppermute | solution.py:414
  69.7 7.3 %collective-permute-done.11 = f32[4,128,128]{2,1,0:T(8,128)S(1)} collective-permute-done((f32[4,128,128]{2,1,0:T(8,128)S(1)}, f32[4,128,128]{2,1,0:T(8,128)S(1)}, u32[]{:S(2)}, u32[]{:S(2)}) %collective-permute-start.11) | collective-permute-done | bytes 262176 | tf_op jit(solution)/shard_map/ppermute | solution.py:414
  77.1 1.6 %collective-permute-start.12 = (f32[2,4,128,128]{3,2,1,0:T(8,128)S(1)}, f32[2,4,128,128]{3,2,1,0:T(8,128)S(1)}, u32[]{:S(2)}, u32[]{:S(2)}) collective-permute-start(f32[2,4,128,128]{3,2,1,0:T(8,128)S(1)} %pad_maximum_fusion.1.near_ref), channel_id=1, source_target_pairs={{0,8},{8,0},{1,9},{9,1},{2,10},{10,2},{3,11},{11,3},{4,12},{12,4},... | collective-permute-start | bytes 1572872 | tf_op jit(solution)/shard_map/ppermute | solution.py:410
  78.8 1.5 %collective-permute-done.12.far_ref = f32[2,4,128,128]{3,2,1,0:T(8,128)S(1)} collective-permute-done((f32[2,4,128,128]{3,2,1,0:T(8,128)S(1)}, f32[2,4,128,128]{3,2,1,0:T(8,128)S(1)}, u32[]{:S(2)}, u32[]{:S(2)}) %collective-permute-start.12) | collective-permute-done | bytes 524320 | tf_op jit(solution)/shard_map/ppermute | solution.py:410
  80.3 1.2 collective-permute-start.13
  81.5 2.3 %collective-permute-start.14 = (f32[4,128,128]{2,1,0:T(8,128)S(1)}, f32[4,128,128]{2,1,0:T(8,128)S(1)}, u32[]{:S(2)}, u32[]{:S(2)}) collective-permute-start(f32[4,128,128]{2,1,0:T(8,128)S(1)} %get-tuple-element.32), channel_id=1, source_target_pairs={{0,32},{16,48},{32,0},{48,16},{1,33},{17,49},{33,1},{49,17},{2,34}... | collective-permute-start | bytes 786440 | tf_op jit(solution)/shard_map/ppermute | solution.py:414
  83.8 1.2 collective-permute-start.15
  85.0 13.8 %first.1.w0_ref = f32[768,512]{1,0:T(8,128)S(1)} custom-call(s32[4]{0:T(128)S(1)} %pad_add_fusion.ids_ref, f32[2,4,128,128]{3,2,1,0:T(8,128)S(1)} %pad_maximum_fusion.1.near_ref, f32[2,4,128,128]{3,2,1,0:T(8,128)S(1)} %collective-permute-done.12.far_ref), custom_call_target="tpu_custom_call" | custom-call | flops 8589934592 | bytes 4194304 | tf_op jit(solution)/shard_map/first/pallas_call | solution.py:201
  98.9 1.5 %collective-permute-start.16 = (f32[4,4,128,128]{3,2,1,0:T(8,128)S(1)}, f32[4,4,128,128]{3,2,1,0:T(8,128)S(1)}, u32[]{:S(2)}, u32[]{:S(2)}) collective-permute-start(f32[4,4,128,128]{3,2,1,0:T(8,128)S(1)} %pad_maximum_fusion.near_ref), channel_id=1, source_target_pairs={{0,8},{8,0},{1,9},{9,1},{2,10},{10,2},{3,11},{11,3},{4,12},{12,4},... | collective-permute-start | bytes 3145736 | tf_op jit(solution)/shard_map/ppermute | solution.py:410
  100.4 3.2 %collective-permute-done.16.far_ref = f32[4,4,128,128]{3,2,1,0:T(8,128)S(1)} collective-permute-done((f32[4,4,128,128]{3,2,1,0:T(8,128)S(1)}, f32[4,4,128,128]{3,2,1,0:T(8,128)S(1)}, u32[]{:S(2)}, u32[]{:S(2)}) %collective-permute-start.16) | collective-permute-done | bytes 1048608 | tf_op jit(solution)/shard_map/ppermute | solution.py:410
  103.6 21.7 %second.1 = (bf16[2,384,1024]{2,1,0:T(8,128)(2,1)S(1)}, f32[3,128,128]{2,1,0:T(8,128)S(1)}) custom-call(s32[4]{0:T(128)S(1)} %pad_add_fusion.ids_ref, f32[768,512]{1,0:T(8,128)S(1)} %first.1.w0_ref, f32[4,4,128,128]{3,2,1,0:T(8,128)S(1)} %pad_maximum_fusion.near_ref, f32[4,4,128,128]{3,2,1,0:T(8,128)S(1)} %collective-permute-done.16.far_ref, ...), custom_call_target="tpu_custom_call" | custom-call | flops 17179869184 | bytes 8388608 | tf_op jit(solution)/shard_map/second/pallas_call | solution.py:331
  125.3 1.1 copy-done
  127.2 9.0 %update.1 = f32[3,12,128,128]{3,2,1,0:T(8,128)} custom-call(s32[4]{0:T(128)} %copy-done.2, bf16[2,384,1024]{2,1,0:T(8,128)(2,1)} %copy-done, f32[3,128,128]{2,1,0:T(8,128)} %copy-done.1, f32[4,8,12,32,128]{4,3,2,1,0:T(8,128)} %bitcast.53, f32[3,12,128,128]{3,2,1,0:T(8,128)} %bitcast.57), custom_call_target="tpu_custom_call" | custom-call | tf_op jit(solution)/shard_map/update/pallas_call | solution.py:392
  (43 shorter events, 4.4 us)
Async XLA Ops:
  6.5 73.7 %all-gather.5.cloned.1.call-start = ((), (), s32[]{:S(2)}) async-start(), calls=%async_computation | async-start | bytes 1769472 | tf_op jit(solution)/shard_map/all_gather | solution.py:457
  8.2 119.0 %all-gather.7.cloned.1.call-start = ((), (), s32[]{:S(2)}) async-start(), calls=%async_computation.1 | async-start | bytes 6488064 | tf_op jit(solution)/shard_map/all_gather | solution.py:466
  10.4 10.4 %collective-permute-start = (f32[16,32,128]{2,1,0:T(8,128)S(1)}, f32[16,32,128]{2,1,0:T(8,128)S(1)}, u32[]{:S(2)}, u32[]{:S(2)}) collective-permute-start(f32[16,32,128]{2,1,0:T(8,128)S(1)} %get-tuple-element.54), channel_id=1, source_target_pairs={{0,128},{1,129},{2,130},{3,131},{4,132},{5,133},{6,134},{7,135},{8... | collective-permute-start | bytes 786440 | tf_op jit(solution)/shard_map/ppermute | solution.py:414
  15.9 6.3 %collective-permute-start.1 = (f32[16,32,128]{2,1,0:T(8,128)S(1)}, f32[16,32,128]{2,1,0:T(8,128)S(1)}, u32[]{:S(2)}, u32[]{:S(2)}) collective-permute-start(f32[16,32,128]{2,1,0:T(8,128)S(1)} %get-tuple-element.55), channel_id=1, source_target_pairs={{0,192},{1,193},{2,194},{3,195},{4,196},{5,197},{6,198},{7,199},{8... | collective-permute-start | bytes 786440 | tf_op jit(solution)/shard_map/ppermute | solution.py:414
  17.2 9.2 %collective-permute-start.2 = (f32[16,32,128]{2,1,0:T(8,128)S(1)}, f32[16,32,128]{2,1,0:T(8,128)S(1)}, u32[]{:S(2)}, u32[]{:S(2)}) collective-permute-start(f32[16,32,128]{2,1,0:T(8,128)S(1)} %get-tuple-element.56), channel_id=1, source_target_pairs={{0,64},{1,65},{2,66},{3,67},{4,68},{5,69},{6,70},{7,71},{8,72},{9,... | collective-permute-start | bytes 786440 | tf_op jit(solution)/shard_map/ppermute | solution.py:414
  27.2 2.5 %collective-permute-start.3 = (f32[128,128]{1,0:T(8,128)S(1)}, f32[128,128]{1,0:T(8,128)S(1)}, u32[]{:S(2)}, u32[]{:S(2)}) collective-permute-start(f32[128,128]{1,0:T(8,128)S(1)} %bitcast.60), channel_id=1, source_target_pairs={{0,8},{8,0},{1,9},{9,1},{2,10},{10,2},{3,11},{11,3},{4,12},{12,4},... | collective-permute-start | bytes 196616 | tf_op jit(solution)/shard_map/ppermute | solution.py:410
  29.8 18.2 %collective-permute-start.4 = (f32[2,128,128]{2,1,0:T(8,128)S(1)}, f32[2,128,128]{2,1,0:T(8,128)S(1)}, u32[]{:S(2)}, u32[]{:S(2)}) collective-permute-start(f32[2,128,128]{2,1,0:T(8,128)S(1)} %pad_maximum_fusion.7), channel_id=1, source_target_pairs={{0,1},{1,2},{2,3},{3,4},{4,5},{5,6},{6,7},{7,0},{8,15},{9,8},{10,9... | collective-permute-start | bytes 393224 | tf_op jit(solution)/shard_map/ppermute | solution.py:414
  35.4 12.5 %collective-permute-start.5 = (f32[2,128,128]{2,1,0:T(8,128)S(1)}, f32[2,128,128]{2,1,0:T(8,128)S(1)}, u32[]{:S(2)}, u32[]{:S(2)}) collective-permute-start(f32[2,128,128]{2,1,0:T(8,128)S(1)} %pad_maximum_fusion.7), channel_id=1, source_target_pairs={{0,2},{1,3},{2,4},{3,5},{4,6},{5,7},{6,0},{7,1},{8,14},{9,15},{10,... | collective-permute-start | bytes 393224 | tf_op jit(solution)/shard_map/ppermute | solution.py:414
  36.6 16.5 %collective-permute-start.6 = (f32[2,128,128]{2,1,0:T(8,128)S(1)}, f32[2,128,128]{2,1,0:T(8,128)S(1)}, u32[]{:S(2)}, u32[]{:S(2)}) collective-permute-start(f32[2,128,128]{2,1,0:T(8,128)S(1)} %pad_maximum_fusion.7), channel_id=1, source_target_pairs={{0,3},{1,4},{2,5},{3,6},{4,7},{5,0},{6,1},{7,2},{8,13},{9,14},{10,... | collective-permute-start | bytes 393224 | tf_op jit(solution)/shard_map/ppermute | solution.py:414
  37.1 10.9 %collective-permute-start.7 = (f32[128,128]{1,0:T(8,128)S(1)}, f32[128,128]{1,0:T(8,128)S(1)}, u32[]{:S(2)}, u32[]{:S(2)}) collective-permute-start(f32[128,128]{1,0:T(8,128)S(1)} %bitcast.62), channel_id=1, source_target_pairs={{0,4},{1,5},{2,6},{3,7},{4,0},{5,1},{6,2},{7,3},{8,12},{9,13},{10,... | collective-permute-start | bytes 196616 | tf_op jit(solution)/shard_map/ppermute | solution.py:414
  53.2 6.5 %collective-permute-start.8 = (f32[3,128,128]{2,1,0:T(8,128)S(1)}, f32[3,128,128]{2,1,0:T(8,128)S(1)}, u32[]{:S(2)}, u32[]{:S(2)}) collective-permute-start(f32[3,128,128]{2,1,0:T(8,128)S(1)} %pad_maximum_fusion.5), channel_id=1, source_target_pairs={{0,8},{8,0},{1,9},{9,1},{2,10},{10,2},{3,11},{11,3},{4,12},{12,4},... | collective-permute-start | bytes 589832 | tf_op jit(solution)/shard_map/ppermute | solution.py:410
  59.9 9.8 %collective-permute-start.10 = (f32[4,128,128]{2,1,0:T(8,128)S(1)}, f32[4,128,128]{2,1,0:T(8,128)S(1)}, u32[]{:S(2)}, u32[]{:S(2)}) collective-permute-start(f32[4,128,128]{2,1,0:T(8,128)S(1)} %get-tuple-element.40), channel_id=1, source_target_pairs={{0,32},{16,48},{1,33},{17,49},{2,34},{18,50},{3,35},{19,51},{4,36}... | collective-permute-start | bytes 786440 | tf_op jit(solution)/shard_map/ppermute | solution.py:414
  64.3 12.6 %collective-permute-start.11 = (f32[4,128,128]{2,1,0:T(8,128)S(1)}, f32[4,128,128]{2,1,0:T(8,128)S(1)}, u32[]{:S(2)}, u32[]{:S(2)}) collective-permute-start(f32[4,128,128]{2,1,0:T(8,128)S(1)} %get-tuple-element.40), channel_id=1, source_target_pairs={{0,48},{16,32},{1,49},{17,33},{2,50},{18,34},{3,51},{19,35},{4,52}... | collective-permute-start | bytes 786440 | tf_op jit(solution)/shard_map/ppermute | solution.py:414
  65.6 11.3 %collective-permute-start.9 = (f32[4,128,128]{2,1,0:T(8,128)S(1)}, f32[4,128,128]{2,1,0:T(8,128)S(1)}, u32[]{:S(2)}, u32[]{:S(2)}) collective-permute-start(f32[4,128,128]{2,1,0:T(8,128)S(1)} %get-tuple-element.40), channel_id=1, source_target_pairs={{0,16},{16,0},{1,17},{17,1},{2,18},{18,2},{3,19},{19,3},{4,20},{20... | collective-permute-start | bytes 786440 | tf_op jit(solution)/shard_map/ppermute | solution.py:414
  77.1 3.2 %collective-permute-start.12 = (f32[2,4,128,128]{3,2,1,0:T(8,128)S(1)}, f32[2,4,128,128]{3,2,1,0:T(8,128)S(1)}, u32[]{:S(2)}, u32[]{:S(2)}) collective-permute-start(f32[2,4,128,128]{3,2,1,0:T(8,128)S(1)} %pad_maximum_fusion.1.near_ref), channel_id=1, source_target_pairs={{0,8},{8,0},{1,9},{9,1},{2,10},{10,2},{3,11},{11,3},{4,12},{12,4},... | collective-permute-start | bytes 1572872 | tf_op jit(solution)/shard_map/ppermute | solution.py:410
  78.8 24.9 %copy-start.2 = (s32[4]{0:T(128)}, s32[4]{0:T(128)S(1)}, u32[]{:S(2)}) copy-start(s32[4]{0:T(128)S(1)} %pad_add_fusion.ids_ref) | copy-start | bytes 52
  80.3 23.4 %copy-start.3 = (f32[24,128,128]{2,1,0:T(8,128)S(1)}, f32[24,128,128]{2,1,0:T(8,128)}, u32[]{:S(2)}) copy-start(f32[24,128,128]{2,1,0:T(8,128)} %all-gather.5.cloned.1.call-done) | copy-start | bytes 4718596
  80.3 18.5 %collective-permute-start.13 = (f32[4,128,128]{2,1,0:T(8,128)S(1)}, f32[4,128,128]{2,1,0:T(8,128)S(1)}, u32[]{:S(2)}, u32[]{:S(2)}) collective-permute-start(f32[4,128,128]{2,1,0:T(8,128)S(1)} %get-tuple-element.32), channel_id=1, source_target_pairs={{0,16},{16,32},{32,48},{48,0},{1,17},{17,33},{33,49},{49,1},{2,18}... | collective-permute-start | bytes 786440 | tf_op jit(solution)/shard_map/ppermute | solution.py:414
  81.5 17.3 %collective-permute-start.14 = (f32[4,128,128]{2,1,0:T(8,128)S(1)}, f32[4,128,128]{2,1,0:T(8,128)S(1)}, u32[]{:S(2)}, u32[]{:S(2)}) collective-permute-start(f32[4,128,128]{2,1,0:T(8,128)S(1)} %get-tuple-element.32), channel_id=1, source_target_pairs={{0,32},{16,48},{32,0},{48,16},{1,33},{17,49},{33,1},{49,17},{2,34}... | collective-permute-start | bytes 786440 | tf_op jit(solution)/shard_map/ppermute | solution.py:414
  83.8 15.0 %collective-permute-start.15 = (f32[4,128,128]{2,1,0:T(8,128)S(1)}, f32[4,128,128]{2,1,0:T(8,128)S(1)}, u32[]{:S(2)}, u32[]{:S(2)}) collective-permute-start(f32[4,128,128]{2,1,0:T(8,128)S(1)} %get-tuple-element.32), channel_id=1, source_target_pairs={{0,48},{16,0},{32,16},{48,32},{1,49},{17,1},{33,17},{49,33},{2,50}... | collective-permute-start | bytes 786440 | tf_op jit(solution)/shard_map/ppermute | solution.py:414
  98.9 4.7 %collective-permute-start.16 = (f32[4,4,128,128]{3,2,1,0:T(8,128)S(1)}, f32[4,4,128,128]{3,2,1,0:T(8,128)S(1)}, u32[]{:S(2)}, u32[]{:S(2)}) collective-permute-start(f32[4,4,128,128]{3,2,1,0:T(8,128)S(1)} %pad_maximum_fusion.near_ref), channel_id=1, source_target_pairs={{0,8},{8,0},{1,9},{9,1},{2,10},{10,2},{3,11},{11,3},{4,12},{12,4},... | collective-permute-start | bytes 3145736 | tf_op jit(solution)/shard_map/ppermute | solution.py:410
  125.3 1.1 copy-start
  126.5 0.7 copy-start.1
Sparse Core Ops, SparseCore 0:
  9.1 46.6 all-gather.4
  58.4 61.3 all-gather.6

commit v6 on v5

--- a/solution.py
+++ b/solution.py
@@ -51,6 +51,12 @@
 
 def tile(i):
     return pl.ds(pl.multiple_of(i * TILE, TILE), TILE)
+
+
+def quarter_rows(i, x, d):
+    quarter = TILE // 4
+    start = i * TILE + lax.rem(x + 4 - d, 4) * quarter
+    return pl.ds(pl.multiple_of(start, quarter), quarter)
 
 
 def spread_row(x, i):
@@ -189,11 +195,13 @@
 
 
 def first_kernel(ids_ref, near_ref, far_ref, w_ref, *scratch):
-    k = ids_ref[3]
+    k, x = ids_ref[3], ids_ref[4]
     for ref, side in ((near_ref, k), (far_ref, 1 - k)):
-        for y in range(2):
-            for j in range(HALF):
-                w_ref[tile(2 * y + side), j * TILE : (j + 1) * TILE] = ref[y, j]
+        for d in range(4):
+            for y in range(2):
+                rows = quarter_rows(2 * y + side, x, d)
+                for j in range(HALF):
+                    w_ref[rows, j * TILE : (j + 1) * TILE] = ref[d, y, j]
     factor_panel(w_ref, *scratch)
 
 
@@ -211,12 +219,13 @@
 
 
 def factor_second(ids_ref, w0_ref, near_ref, far_ref, x_ref, w_ref, b_ref, *scratch):
-    y, k = ids_ref[2], ids_ref[3]
+    y, k, x = ids_ref[2], ids_ref[3], ids_ref[4]
     for ref, side in ((near_ref, k), (far_ref, 1 - k)):
         for d in range(4):
-            row = tile(2 * lax.rem(y + 4 - d, 4) + side)
-            for j in range(HALF):
-                b_ref[row, j * TILE : (j + 1) * TILE] = ref[d, j]
+            for e in range(4):
+                rows = quarter_rows(2 * lax.rem(y + 4 - e, 4) + side, x, d)
+                for j in range(HALF):
+                    b_ref[rows, j * TILE : (j + 1) * TILE] = ref[d, e, j]
     parts = split(b_ref[0:PANEL, :])
     for i in range(HALF):
         n = (i + 1) * TILE
@@ -353,20 +362,20 @@
     )(ids, w0, near, far, own)
 
 
-def update_kernel(ids_ref, t_ref, c_ref, right_ref, k_ref, o_ref):
+def update_kernel(ids_ref, t_ref, c_ref, even_ref, odd_ref, k_ref, o_ref):
     step = pl.program_id(0)
     tiles, _, _ = c_ref.shape
     rows = tiles * TILE
     quarters = [
         jnp.concatenate(
             [
-                right_ref[x, r, i]
+                ref[x, r, 0]
                 for r in range(TILES)
                 for x in range(4)
             ],
             0,
         )
-        for i in range(2)
+        for ref in (even_ref, odd_ref)
     ]
     right = jnp.concatenate(quarters, 1)
     high = right.astype(jnp.bfloat16)
@@ -389,6 +398,7 @@
 def update(ids, t, c, right, kernel):
     tiles, columns = kernel.shape[:2]
     block = pl.BlockSpec((tiles, 2, TILE, TILE), lambda j: (0, j, 0, 0))
+    piece = (4, TILES, 1, TILE // 4, TILE)
     return pl.pallas_call(
         update_kernel,
         grid=(columns // 2,),
@@ -397,13 +407,14 @@
             SMEM,
             VMEM,
             VMEM,
-            pl.BlockSpec((4, TILES, 2, TILE // 4, TILE), lambda j: (0, 0, j, 0, 0)),
+            pl.BlockSpec(piece, lambda j: (0, 0, jnp.maximum(2 * j - 1, 0), 0, 0)),
+            pl.BlockSpec(piece, lambda j: (0, 0, 2 * j, 0, 0)),
             block,
         ],
         out_specs=block,
         compiler_params=pltpu.CompilerParams(vmem_limit_bytes=60 << 20),
         name="update",
-    )(ids, t, c, right, kernel)
+    )(ids, t, c, right, right, kernel)
 
 
 def swap(x):
@@ -414,20 +425,9 @@
     return lax.ppermute(x, axis, pairs)
 
 
-def gather_first(strip):
-    y = lax.axis_index("y")
-    one = send(strip, "y", [(0, 1), (1, 0)])
-    two = send(strip, "y", [(0, 3), (1, 2)])
-    three = send(strip, "y", [(0, 2), (1, 3)])
-    upper = jnp.where(y == 0, strip, jnp.where(y == 1, one, jnp.where(y == 2, three, two)))
-    lower = jnp.where(y == 1, strip, jnp.where(y == 0, one, jnp.where(y == 2, two, three)))
-    near = jnp.stack([upper, lower])
-    return near, swap(near)
-
-
-def round_y(block):
-    n = lax.axis_size("y")
-    return [block] + [send(block, "y", [(i, (i + d) % n) for i in range(n)]) for d in range(1, n)]
+def around(block, axis):
+    n = lax.axis_size(axis)
+    return [block] + [send(block, axis, [(i, (i + d) % n) for i in range(n)]) for d in range(1, n)]
 
 
 def gather_z(block):
@@ -452,24 +452,25 @@
 def body(kernel):
     kernel = kernel.transpose(0, 2, 1, 3)
     x = lax.axis_index("x")
-    ids = jnp.stack([lax.axis_index(a) for a in (ROW, "z", "y", "k")]).astype(jnp.int32)
+    y = lax.axis_index("y")
+    places = (ROW, "z", "y", "k", "x")
+    ids = jnp.stack([lax.axis_index(a) for a in places]).astype(jnp.int32)
     mine, kernel = lax.optimization_barrier((kernel[:, 0], kernel))
     own = lax.all_gather(mine, "z")
 
     quarters = kernel[0].reshape(-1, 4, TILE // 4, TILE)
-    corner, quarter = quarters[0], quarters[:, 0]
+    quarter = quarters[:, 0]
     for d in (1, 3, 2):
-        both = send(jnp.concatenate([quarters[0], quarters[:, d]]), "x", [(0, d)])
-        corner = jnp.where(x == d, both[:4], corner)
-        quarter = jnp.where(x == d, both[4:], quarter)
-    corner = corner.reshape(TILE, TILE)
-    right = lax.all_gather(quarter, ROW)
+        quarter = jnp.where(x == d, send(quarters[:, d], "x", [(0, d)]), quarter)
+    right = lax.all_gather(quarter[1:], ROW)
     right = right.reshape(4, TILES, -1, TILE // 4, TILE)
 
-    strip = gather_z(corner)
-    near, far = gather_first(strip[:HALF])
-    near, far, rest, own = lax.optimization_barrier((near, far, strip[HALF:], own))
-    parts = round_y(rest)
+    strips = jnp.stack(around(gather_z(quarter[0]), "y"))
+    top = [lax.dynamic_index_in_dim(strips, (y + 4 - i) % 4, 0, False)[:HALF] for i in range(2)]
+    near = jnp.stack(around(jnp.stack(top), "x"))
+    far = swap(near)
+    near, far, rest, own = lax.optimization_barrier((near, far, strips[:, HALF:], own))
+    parts = around(rest, "x")
     w0 = first(ids, near, far)
     w0, parts = lax.optimization_barrier((w0, parts))
     more = jnp.stack(parts)

time: 143 us -> 130 us (0.909)
  waiting for transfers between devices: 35.3 us -> 23.1 us
    ppermute x13 -> x16, waiting for transfers between devices: 28.6 us -> 16.8 us  [send(): return lax.ppermute(x, axis, pairs)]
    ppermute x4, starting transfers between devices: 10.2 us -> 7.58 us  [swap(): return lax.ppermute(x, 'k', [(0, 1), (1, 0)])]
    ppermute x13 -> x16, starting transfers between devices: 32.5 us -> 34.8 us  [send(): return lax.ppermute(x, axis, pairs)]
  transfers between devices with their start and end apart: 19 -> 22, of which waited for: 11 -> 15; matrix products, arithmetic and copies ran while one was open for 2% -> 2% of each run, Pallas kernels for 25% -> 27%
where the time goes in v6:
time: 130 us; the launch traced here: 129 us
  Pallas kernels  44.4 us (34%)
  starting transfers between devices  42.5 us (33%)
  waiting for transfers between devices  23.1 us (18%)
  between operations  13.6 us (10%)
  local copies, waits for them, and re-layouts  5.56 us (4%)
    ppermute x16, starting transfers between devices, send(): return lax.ppermute(x, axis, pairs)  34.8 us
    pallas_call x1, Pallas kernels, second(): pl.pallas_call(second_kernel, out_shape=[jax.ShapeDtypeStruct((2, rows, W...  21.6 us
    ppermute x16, waiting for transfers between devices, send(): return lax.ppermute(x, axis, pairs)  16.8 us
    pallas_call x1, Pallas kernels, first(): pl.pallas_call(first_kernel, out_shape=jax.ShapeDtypeStruct(FACTOR, jnp.f...  13.8 us
    pallas_call x1, Pallas kernels, update(): pl.pallas_call(update_kernel, grid=(columns // 2,), out_shape=jax.ShapeDt...  9.05 us
    ppermute x4, starting transfers between devices, swap(): return lax.ppermute(x, 'k', [(0, 1), (1, 0)])  7.58 us
    ppermute x4, waiting for transfers between devices, swap(): return lax.ppermute(x, 'k', [(0, 1), (1, 0)])  5.44 us
  transfers between devices with their start and end apart: 22, of which 15 were waited for; matrix products, arithmetic and copies ran while one was open for 2% of the time, Pallas kernels for 27%

profile of v6, /device:TPU:1, one launch (start us, length us, event | category | flops | bytes accessed | tf_op | source)
XLA Modules:
  0.0 129.4 jit_solution(126611724884277800)
XLA Ops:
  6.5 1.6 %slice_bitcast_fusion.4 = f32[3,128,128]{2,1,0:T(8,128)} fusion(f32[3,12,128,128]{3,2,1,0:T(8,128)} %bitcast.57), kind=kLoop, calls=%fused_computation.10 | loop fusion | bytes 393216 | tf_op jit(solution)/shard_map/squeeze | solution.py:458
  8.2 1.2 slice.54
  9.5 5.5 %collective-permute-start = (f32[12,32,128]{2,1,0:T(8,128)S(1)}, f32[12,32,128]{2,1,0:T(8,128)S(1)}, u32[]{:S(2)}, u32[]{:S(2)}) collective-permute-start(f32[12,32,128]{2,1,0:T(8,128)S(1)} %get-tuple-element.41), channel_id=1, source_target_pairs={{0,128},{1,129},{2,130},{3,131},{4,132},{5,133},{6,134},{7,135},{8... | collective-permute-start | bytes 589832 | tf_op jit(solution)/shard_map/ppermute | solution.py:425
  15.0 1.3 %collective-permute-start.1 = (f32[12,32,128]{2,1,0:T(8,128)S(1)}, f32[12,32,128]{2,1,0:T(8,128)S(1)}, u32[]{:S(2)}, u32[]{:S(2)}) collective-permute-start(f32[12,32,128]{2,1,0:T(8,128)S(1)} %get-tuple-element.40), channel_id=1, source_target_pairs={{0,192},{1,193},{2,194},{3,195},{4,196},{5,197},{6,198},{7,199},{8... | collective-permute-start | bytes 589832 | tf_op jit(solution)/shard_map/ppermute | solution.py:425
  16.3 1.3 %collective-permute-start.2 = (f32[12,32,128]{2,1,0:T(8,128)S(1)}, f32[12,32,128]{2,1,0:T(8,128)S(1)}, u32[]{:S(2)}, u32[]{:S(2)}) collective-permute-start(f32[12,32,128]{2,1,0:T(8,128)S(1)} %get-tuple-element.39), channel_id=1, source_target_pairs={{0,64},{1,65},{2,66},{3,67},{4,68},{5,69},{6,70},{7,71},{8,72},{9,... | collective-permute-start | bytes 589832 | tf_op jit(solution)/shard_map/ppermute | solution.py:425
  17.6 0.9 collective-permute-done
  18.5 1.3 %collective-permute-done.1 = f32[12,32,128]{2,1,0:T(8,128)S(1)} collective-permute-done((f32[12,32,128]{2,1,0:T(8,128)S(1)}, f32[12,32,128]{2,1,0:T(8,128)S(1)}, u32[]{:S(2)}, u32[]{:S(2)}) %collective-permute-start.1) | collective-permute-done | bytes 196640 | tf_op jit(solution)/shard_map/ppermute | solution.py:425
  19.8 2.9 %collective-permute-done.2 = f32[12,32,128]{2,1,0:T(8,128)S(1)} collective-permute-done((f32[12,32,128]{2,1,0:T(8,128)S(1)}, f32[12,32,128]{2,1,0:T(8,128)S(1)}, u32[]{:S(2)}, u32[]{:S(2)}) %collective-permute-start.2) | collective-permute-done | bytes 196640 | tf_op jit(solution)/shard_map/ppermute | solution.py:425
  23.5 1.6 %collective-permute-start.3 = (f32[32,128]{1,0:T(8,128)S(1)}, f32[32,128]{1,0:T(8,128)S(1)}, u32[]{:S(2)}, u32[]{:S(2)}) collective-permute-start(f32[32,128]{1,0:T(8,128)S(1)} %get-tuple-element.45), channel_id=1, source_target_pairs={{0,8},{8,0},{1,9},{9,1},{2,10},{10,2},{3,11},{11,3},{4,12},{12,4},... | collective-permute-start | bytes 49160 | tf_op jit(solution)/shard_map/ppermute | solution.py:421
  26.0 5.6 %collective-permute-start.4 = (f32[2,32,128]{2,1,0:T(8,128)S(1)}, f32[2,32,128]{2,1,0:T(8,128)S(1)}, u32[]{:S(2)}, u32[]{:S(2)}) collective-permute-start(f32[2,32,128]{2,1,0:T(8,128)S(1)} %pad_maximum_fusion.6), channel_id=1, source_target_pairs={{0,1},{1,2},{2,3},{3,4},{4,5},{5,6},{6,7},{7,0},{8,15},{9,8},{10,9... | collective-permute-start | bytes 98312 | tf_op jit(solution)/shard_map/ppermute | solution.py:425
  31.6 1.2 collective-permute-start.5
  33.2 4.5 %collective-permute-start.7 = (f32[32,128]{1,0:T(8,128)S(1)}, f32[32,128]{1,0:T(8,128)S(1)}, u32[]{:S(2)}, u32[]{:S(2)}) collective-permute-start(f32[32,128]{1,0:T(8,128)S(1)} %get-tuple-element.45), channel_id=1, source_target_pairs={{0,4},{1,5},{2,6},{3,7},{4,0},{5,1},{6,2},{7,3},{8,12},{9,13},{10,... | collective-permute-start | bytes 49160 | tf_op jit(solution)/shard_map/ppermute | solution.py:425
  37.7 2.6 %collective-permute-done.7 = f32[32,128]{1,0:T(8,128)S(1)} collective-permute-done((f32[32,128]{1,0:T(8,128)S(1)}, f32[32,128]{1,0:T(8,128)S(1)}, u32[]{:S(2)}, u32[]{:S(2)}) %collective-permute-start.7) | collective-permute-done | bytes 16416 | tf_op jit(solution)/shard_map/ppermute | solution.py:425
  40.3 3.0 %collective-permute-start.8 = (f32[3,32,128]{2,1,0:T(8,128)S(1)}, f32[3,32,128]{2,1,0:T(8,128)S(1)}, u32[]{:S(2)}, u32[]{:S(2)}) collective-permute-start(f32[3,32,128]{2,1,0:T(8,128)S(1)} %pad_maximum_fusion.4), channel_id=1, source_target_pairs={{0,8},{8,0},{1,9},{9,1},{2,10},{10,2},{3,11},{11,3},{4,12},{12,4},... | collective-permute-start | bytes 147464 | tf_op jit(solution)/shard_map/ppermute | solution.py:421
  43.4 0.9 collective-permute-done.8
  44.4 1.5 %collective-permute-start.9 = (f32[8,32,128]{2,1,0:T(8,128)S(1)}, f32[8,32,128]{2,1,0:T(8,128)S(1)}, u32[]{:S(2)}, u32[]{:S(2)}) collective-permute-start(f32[8,32,128]{2,1,0:T(8,128)S(1)} %constant_dynamic-slice_fusion.2), channel_id=1, source_target_pairs={{0,16},{16,32},{32,48},{48,0},{1,17},{17,33},{33,49},{49,1},{2,18}... | collective-permute-start | bytes 393224 | tf_op jit(solution)/shard_map/ppermute | solution.py:425
  45.8 2.6 %collective-permute-start.10 = (f32[8,32,128]{2,1,0:T(8,128)S(1)}, f32[8,32,128]{2,1,0:T(8,128)S(1)}, u32[]{:S(2)}, u32[]{:S(2)}) collective-permute-start(f32[8,32,128]{2,1,0:T(8,128)S(1)} %constant_dynamic-slice_fusion.2), channel_id=1, source_target_pairs={{0,32},{16,48},{32,0},{48,16},{1,33},{17,49},{33,1},{49,17},{2,34}... | collective-permute-start | bytes 393224 | tf_op jit(solution)/shard_map/ppermute | solution.py:425
  48.5 1.1 collective-permute-start.11
  49.5 1.2 collective-permute-done.9
  50.7 3.8 %collective-permute-done.10 = f32[8,32,128]{2,1,0:T(8,128)S(1)} collective-permute-done((f32[8,32,128]{2,1,0:T(8,128)S(1)}, f32[8,32,128]{2,1,0:T(8,128)S(1)}, u32[]{:S(2)}, u32[]{:S(2)}) %collective-permute-start.10) | collective-permute-done | bytes 131104 | tf_op jit(solution)/shard_map/ppermute | solution.py:425
  54.6 2.5 %collective-permute-start.12 = (f32[2,4,32,128]{3,2,1,0:T(8,128)S(1)}, f32[2,4,32,128]{3,2,1,0:T(8,128)S(1)}, u32[]{:S(2)}, u32[]{:S(2)}) collective-permute-start(f32[2,4,32,128]{3,2,1,0:T(8,128)S(1)} %get-tuple-element.48), channel_id=1, source_target_pairs={{0,64},{64,128},{128,192},{192,0},{1,65},{65,129},{129,193},{193,1... | collective-permute-start | bytes 393224 | tf_op jit(solution)/shard_map/ppermute | solution.py:425
  57.1 2.5 %collective-permute-start.14 = (f32[2,4,32,128]{3,2,1,0:T(8,128)S(1)}, f32[2,4,32,128]{3,2,1,0:T(8,128)S(1)}, u32[]{:S(2)}, u32[]{:S(2)}) collective-permute-start(f32[2,4,32,128]{3,2,1,0:T(8,128)S(1)} %get-tuple-element.48), channel_id=1, source_target_pairs={{0,192},{64,0},{128,64},{192,128},{1,193},{65,1},{129,65},{193,129... | collective-permute-start | bytes 393224 | tf_op jit(solution)/shard_map/ppermute | solution.py:425
  59.7 2.8 %collective-permute-done.13 = f32[2,4,32,128]{3,2,1,0:T(8,128)S(1)} collective-permute-done((f32[2,4,32,128]{3,2,1,0:T(8,128)S(1)}, f32[2,4,32,128]{3,2,1,0:T(8,128)S(1)}, u32[]{:S(2)}, u32[]{:S(2)}) %collective-permute-start.13) | collective-permute-done | bytes 131104 | tf_op jit(solution)/shard_map/ppermute | solution.py:425
  63.2 2.2 %collective-permute-start.15 = (f32[4,2,4,32,128]{4,3,2,1,0:T(8,128)S(1)}, f32[4,2,4,32,128]{4,3,2,1,0:T(8,128)S(1)}, u32[]{:S(2)}, u32[]{:S(2)}) collective-permute-start(f32[4,2,4,32,128]{4,3,2,1,0:T(8,128)S(1)} %pad_maximum_fusion.2.near_ref), channel_id=1, source_target_pairs={{0,8},{8,0},{1,9},{9,1},{2,10},{10,2},{3,11},{11,3},{4,12},{12,4},... | collective-permute-start | bytes 1572872 | tf_op jit(solution)/shard_map/ppermute | solution.py:421
  65.5 1.4 %collective-permute-done.15.far_ref = f32[4,2,4,32,128]{4,3,2,1,0:T(8,128)S(1)} collective-permute-done((f32[4,2,4,32,128]{4,3,2,1,0:T(8,128)S(1)}, f32[4,2,4,32,128]{4,3,2,1,0:T(8,128)S(1)}, u32[]{:S(2)}, u32[]{:S(2)}) %collective-permute-start.15) | collective-permute-done | bytes 524320 | tf_op jit(solution)/shard_map/ppermute | solution.py:421
  66.9 1.8 %collective-permute-start.16 = (f32[4,4,32,128]{3,2,1,0:T(8,128)S(1)}, f32[4,4,32,128]{3,2,1,0:T(8,128)S(1)}, u32[]{:S(2)}, u32[]{:S(2)}) collective-permute-start(f32[4,4,32,128]{3,2,1,0:T(8,128)S(1)} %slice.76), channel_id=1, source_target_pairs={{0,64},{64,128},{128,192},{192,0},{1,65},{65,129},{129,193},{193,1... | collective-permute-start | bytes 786440 | tf_op jit(solution)/shard_map/ppermute | solution.py:425
  68.7 2.3 %collective-permute-start.17 = (f32[4,4,32,128]{3,2,1,0:T(8,128)S(1)}, f32[4,4,32,128]{3,2,1,0:T(8,128)S(1)}, u32[]{:S(2)}, u32[]{:S(2)}) collective-permute-start(f32[4,4,32,128]{3,2,1,0:T(8,128)S(1)} %slice.76), channel_id=1, source_target_pairs={{0,128},{64,192},{128,0},{192,64},{1,129},{65,193},{129,1},{193,65... | collective-permute-start | bytes 786440 | tf_op jit(solution)/shard_map/ppermute | solution.py:425
  71.8 13.8 %first.1.w0_ref = f32[768,512]{1,0:T(8,128)S(1)} custom-call(s32[5]{0:T(128)S(1)} %stack.85.ids_ref, f32[4,2,4,32,128]{4,3,2,1,0:T(8,128)S(1)} %pad_maximum_fusion.2.near_ref, f32[4,2,4,32,128]{4,3,2,1,0:T(8,128)S(1)} %collective-permute-done.15.far_ref), custom_call_target="tpu_custom_call" | custom-call | flops 8589934592 | bytes 4194304 | tf_op jit(solution)/shard_map/first/pallas_call | solution.py:209
  87.0 2.3 %collective-permute-done.19.far_ref = f32[4,4,4,32,128]{4,3,2,1,0:T(8,128)S(1)} collective-permute-done((f32[4,4,4,32,128]{4,3,2,1,0:T(8,128)S(1)}, f32[4,4,4,32,128]{4,3,2,1,0:T(8,128)S(1)}, u32[]{:S(2)}, u32[]{:S(2)}) %collective-permute-start.19) | collective-permute-done | bytes 1048608 | tf_op jit(solution)/shard_map/ppermute | solution.py:421
  89.3 21.6 %second.1 = (bf16[2,384,1024]{2,1,0:T(8,128)(2,1)S(1)}, f32[3,128,128]{2,1,0:T(8,128)S(1)}) custom-call(s32[5]{0:T(128)S(1)} %stack.85.ids_ref, f32[768,512]{1,0:T(8,128)S(1)} %first.1.w0_ref, f32[4,4,4,32,128]{4,3,2,1,0:T(8,128)S(1)} %pad_maximum_fusion.near_ref, f32[4,4,4,32,128]{4,3,2,1,0:T(8,128)S(1)} %collective-permute-done.19.far_ref, ...), custom_call_target="tpu_custom_call" | custom-call | flops 17179869184 | bytes 8388608 | tf_op jit(solution)/shard_map/second/pallas_call | solution.py:340
  111.0 1.1 copy-done
  113.5 9.1 %update.1 = f32[3,12,128,128]{3,2,1,0:T(8,128)} custom-call(s32[5]{0:T(128)} %copy-done.2, bf16[2,384,1024]{2,1,0:T(8,128)(2,1)} %copy-done, f32[3,128,128]{2,1,0:T(8,128)} %copy-done.1, f32[4,8,11,32,128]{4,3,2,1,0:T(8,128)} %bitcast.55, f32[4,8,11,32,128]{4,3,2,1,0:T(8,128)} %bitcast.56, f32[3,12,128,128]{3,2,1,0:T(8,128)} %bitcast.59), custom_call_target="tpu_custom_call" | custom-call | tf_op jit(solution)/shard_map/update/pallas_call | solution.py:402
  (51 shorter events, 6.9 us)
Async XLA Ops:
  6.5 60.4 %all-gather.5.cloned.1.call-start = ((), (), s32[]{:S(2)}) async-start(), calls=%async_computation | async-start | bytes 1769472 | tf_op jit(solution)/shard_map/all_gather | solution.py:459
  8.2 105.4 %all-gather.7.cloned.1.call-start = ((), (), s32[]{:S(2)}) async-start(), calls=%async_computation.1 | async-start | bytes 5947392 | tf_op jit(solution)/shard_map/all_gather | solution.py:465
  9.5 9.0 %collective-permute-start = (f32[12,32,128]{2,1,0:T(8,128)S(1)}, f32[12,32,128]{2,1,0:T(8,128)S(1)}, u32[]{:S(2)}, u32[]{:S(2)}) collective-permute-start(f32[12,32,128]{2,1,0:T(8,128)S(1)} %get-tuple-element.41), channel_id=1, source_target_pairs={{0,128},{1,129},{2,130},{3,131},{4,132},{5,133},{6,134},{7,135},{8... | collective-permute-start | bytes 589832 | tf_op jit(solution)/shard_map/ppermute | solution.py:425
  15.0 4.8 %collective-permute-start.1 = (f32[12,32,128]{2,1,0:T(8,128)S(1)}, f32[12,32,128]{2,1,0:T(8,128)S(1)}, u32[]{:S(2)}, u32[]{:S(2)}) collective-permute-start(f32[12,32,128]{2,1,0:T(8,128)S(1)} %get-tuple-element.40), channel_id=1, source_target_pairs={{0,192},{1,193},{2,194},{3,195},{4,196},{5,197},{6,198},{7,199},{8... | collective-permute-start | bytes 589832 | tf_op jit(solution)/shard_map/ppermute | solution.py:425
  16.3 6.4 %collective-permute-start.2 = (f32[12,32,128]{2,1,0:T(8,128)S(1)}, f32[12,32,128]{2,1,0:T(8,128)S(1)}, u32[]{:S(2)}, u32[]{:S(2)}) collective-permute-start(f32[12,32,128]{2,1,0:T(8,128)S(1)} %get-tuple-element.39), channel_id=1, source_target_pairs={{0,64},{1,65},{2,66},{3,67},{4,68},{5,69},{6,70},{7,71},{8,72},{9,... | collective-permute-start | bytes 589832 | tf_op jit(solution)/shard_map/ppermute | solution.py:425
  23.5 2.5 %collective-permute-start.3 = (f32[32,128]{1,0:T(8,128)S(1)}, f32[32,128]{1,0:T(8,128)S(1)}, u32[]{:S(2)}, u32[]{:S(2)}) collective-permute-start(f32[32,128]{1,0:T(8,128)S(1)} %get-tuple-element.45), channel_id=1, source_target_pairs={{0,8},{8,0},{1,9},{9,1},{2,10},{10,2},{3,11},{11,3},{4,12},{12,4},... | collective-permute-start | bytes 49160 | tf_op jit(solution)/shard_map/ppermute | solution.py:421
  26.0 14.3 %collective-permute-start.4 = (f32[2,32,128]{2,1,0:T(8,128)S(1)}, f32[2,32,128]{2,1,0:T(8,128)S(1)}, u32[]{:S(2)}, u32[]{:S(2)}) collective-permute-start(f32[2,32,128]{2,1,0:T(8,128)S(1)} %pad_maximum_fusion.6), channel_id=1, source_target_pairs={{0,1},{1,2},{2,3},{3,4},{4,5},{5,6},{6,7},{7,0},{8,15},{9,8},{10,9... | collective-permute-start | bytes 98312 | tf_op jit(solution)/shard_map/ppermute | solution.py:425
  31.6 8.7 %collective-permute-start.5 = (f32[2,32,128]{2,1,0:T(8,128)S(1)}, f32[2,32,128]{2,1,0:T(8,128)S(1)}, u32[]{:S(2)}, u32[]{:S(2)}) collective-permute-start(f32[2,32,128]{2,1,0:T(8,128)S(1)} %pad_maximum_fusion.6), channel_id=1, source_target_pairs={{0,2},{1,3},{2,4},{3,5},{4,6},{5,7},{6,0},{7,1},{8,14},{9,15},{10,... | collective-permute-start | bytes 98312 | tf_op jit(solution)/shard_map/ppermute | solution.py:425
  32.7 7.5 %collective-permute-start.6 = (f32[2,32,128]{2,1,0:T(8,128)S(1)}, f32[2,32,128]{2,1,0:T(8,128)S(1)}, u32[]{:S(2)}, u32[]{:S(2)}) collective-permute-start(f32[2,32,128]{2,1,0:T(8,128)S(1)} %pad_maximum_fusion.6), channel_id=1, source_target_pairs={{0,3},{1,4},{2,5},{3,6},{4,7},{5,0},{6,1},{7,2},{8,13},{9,14},{10,... | collective-permute-start | bytes 98312 | tf_op jit(solution)/shard_map/ppermute | solution.py:425
  33.2 7.1 %collective-permute-start.7 = (f32[32,128]{1,0:T(8,128)S(1)}, f32[32,128]{1,0:T(8,128)S(1)}, u32[]{:S(2)}, u32[]{:S(2)}) collective-permute-start(f32[32,128]{1,0:T(8,128)S(1)} %get-tuple-element.45), channel_id=1, source_target_pairs={{0,4},{1,5},{2,6},{3,7},{4,0},{5,1},{6,2},{7,3},{8,12},{9,13},{10,... | collective-permute-start | bytes 49160 | tf_op jit(solution)/shard_map/ppermute | solution.py:425
  40.3 3.9 %collective-permute-start.8 = (f32[3,32,128]{2,1,0:T(8,128)S(1)}, f32[3,32,128]{2,1,0:T(8,128)S(1)}, u32[]{:S(2)}, u32[]{:S(2)}) collective-permute-start(f32[3,32,128]{2,1,0:T(8,128)S(1)} %pad_maximum_fusion.4), channel_id=1, source_target_pairs={{0,8},{8,0},{1,9},{9,1},{2,10},{10,2},{3,11},{11,3},{4,12},{12,4},... | collective-permute-start | bytes 147464 | tf_op jit(solution)/shard_map/ppermute | solution.py:421
  44.4 6.4 %collective-permute-start.9 = (f32[8,32,128]{2,1,0:T(8,128)S(1)}, f32[8,32,128]{2,1,0:T(8,128)S(1)}, u32[]{:S(2)}, u32[]{:S(2)}) collective-permute-start(f32[8,32,128]{2,1,0:T(8,128)S(1)} %constant_dynamic-slice_fusion.2), channel_id=1, source_target_pairs={{0,16},{16,32},{32,48},{48,0},{1,17},{17,33},{33,49},{49,1},{2,18}... | collective-permute-start | bytes 393224 | tf_op jit(solution)/shard_map/ppermute | solution.py:425
  45.8 8.7 %collective-permute-start.10 = (f32[8,32,128]{2,1,0:T(8,128)S(1)}, f32[8,32,128]{2,1,0:T(8,128)S(1)}, u32[]{:S(2)}, u32[]{:S(2)}) collective-permute-start(f32[8,32,128]{2,1,0:T(8,128)S(1)} %constant_dynamic-slice_fusion.2), channel_id=1, source_target_pairs={{0,32},{16,48},{32,0},{48,16},{1,33},{17,49},{33,1},{49,17},{2,34}... | collective-permute-start | bytes 393224 | tf_op jit(solution)/shard_map/ppermute | solution.py:425
  48.5 6.1 %collective-permute-start.11 = (f32[8,32,128]{2,1,0:T(8,128)S(1)}, f32[8,32,128]{2,1,0:T(8,128)S(1)}, u32[]{:S(2)}, u32[]{:S(2)}) collective-permute-start(f32[8,32,128]{2,1,0:T(8,128)S(1)} %constant_dynamic-slice_fusion.2), channel_id=1, source_target_pairs={{0,48},{16,0},{32,16},{48,32},{1,49},{17,1},{33,17},{49,33},{2,50}... | collective-permute-start | bytes 393224 | tf_op jit(solution)/shard_map/ppermute | solution.py:425
  54.6 5.1 %collective-permute-start.12 = (f32[2,4,32,128]{3,2,1,0:T(8,128)S(1)}, f32[2,4,32,128]{3,2,1,0:T(8,128)S(1)}, u32[]{:S(2)}, u32[]{:S(2)}) collective-permute-start(f32[2,4,32,128]{3,2,1,0:T(8,128)S(1)} %get-tuple-element.48), channel_id=1, source_target_pairs={{0,64},{64,128},{128,192},{192,0},{1,65},{65,129},{129,193},{193,1... | collective-permute-start | bytes 393224 | tf_op jit(solution)/shard_map/ppermute | solution.py:425
  57.1 5.4 %collective-permute-start.13 = (f32[2,4,32,128]{3,2,1,0:T(8,128)S(1)}, f32[2,4,32,128]{3,2,1,0:T(8,128)S(1)}, u32[]{:S(2)}, u32[]{:S(2)}) collective-permute-start(f32[2,4,32,128]{3,2,1,0:T(8,128)S(1)} %get-tuple-element.48), channel_id=1, source_target_pairs={{0,128},{64,192},{128,0},{192,64},{1,129},{65,193},{129,1},{193,65... | collective-permute-start | bytes 393224 | tf_op jit(solution)/shard_map/ppermute | solution.py:425
  57.1 6.0 %collective-permute-start.14 = (f32[2,4,32,128]{3,2,1,0:T(8,128)S(1)}, f32[2,4,32,128]{3,2,1,0:T(8,128)S(1)}, u32[]{:S(2)}, u32[]{:S(2)}) collective-permute-start(f32[2,4,32,128]{3,2,1,0:T(8,128)S(1)} %get-tuple-element.48), channel_id=1, source_target_pairs={{0,192},{64,0},{128,64},{192,128},{1,193},{65,1},{129,65},{193,129... | collective-permute-start | bytes 393224 | tf_op jit(solution)/shard_map/ppermute | solution.py:425
  63.2 3.7 %collective-permute-start.15 = (f32[4,2,4,32,128]{4,3,2,1,0:T(8,128)S(1)}, f32[4,2,4,32,128]{4,3,2,1,0:T(8,128)S(1)}, u32[]{:S(2)}, u32[]{:S(2)}) collective-permute-start(f32[4,2,4,32,128]{4,3,2,1,0:T(8,128)S(1)} %pad_maximum_fusion.2.near_ref), channel_id=1, source_target_pairs={{0,8},{8,0},{1,9},{9,1},{2,10},{10,2},{3,11},{11,3},{4,12},{12,4},... | collective-permute-start | bytes 1572872 | tf_op jit(solution)/shard_map/ppermute | solution.py:421
  65.4 23.9 %copy-start.2 = (s32[5]{0:T(128)}, s32[5]{0:T(128)S(1)}, u32[]{:S(2)}) copy-start(s32[5]{0:T(128)S(1)} %stack.85.ids_ref) | copy-start | bytes 64
  66.9 22.4 %copy-start.3 = (f32[24,128,128]{2,1,0:T(8,128)S(1)}, f32[24,128,128]{2,1,0:T(8,128)}, u32[]{:S(2)}) copy-start(f32[24,128,128]{2,1,0:T(8,128)} %all-gather.5.cloned.1.call-done) | copy-start | bytes 4718596
  66.9 18.7 %collective-permute-start.16 = (f32[4,4,32,128]{3,2,1,0:T(8,128)S(1)}, f32[4,4,32,128]{3,2,1,0:T(8,128)S(1)}, u32[]{:S(2)}, u32[]{:S(2)}) collective-permute-start(f32[4,4,32,128]{3,2,1,0:T(8,128)S(1)} %slice.76), channel_id=1, source_target_pairs={{0,64},{64,128},{128,192},{192,0},{1,65},{65,129},{129,193},{193,1... | collective-permute-start | bytes 786440 | tf_op jit(solution)/shard_map/ppermute | solution.py:425
  68.7 17.5 %collective-permute-start.17 = (f32[4,4,32,128]{3,2,1,0:T(8,128)S(1)}, f32[4,4,32,128]{3,2,1,0:T(8,128)S(1)}, u32[]{:S(2)}, u32[]{:S(2)}) collective-permute-start(f32[4,4,32,128]{3,2,1,0:T(8,128)S(1)} %slice.76), channel_id=1, source_target_pairs={{0,128},{64,192},{128,0},{192,64},{1,129},{65,193},{129,1},{193,65... | collective-permute-start | bytes 786440 | tf_op jit(solution)/shard_map/ppermute | solution.py:425
  71.0 15.2 %collective-permute-start.18 = (f32[4,4,32,128]{3,2,1,0:T(8,128)S(1)}, f32[4,4,32,128]{3,2,1,0:T(8,128)S(1)}, u32[]{:S(2)}, u32[]{:S(2)}) collective-permute-start(f32[4,4,32,128]{3,2,1,0:T(8,128)S(1)} %slice.76), channel_id=1, source_target_pairs={{0,192},{64,0},{128,64},{192,128},{1,193},{65,1},{129,65},{193,129... | collective-permute-start | bytes 786440 | tf_op jit(solution)/shard_map/ppermute | solution.py:425
  86.3 3.0 %collective-permute-start.19 = (f32[4,4,4,32,128]{4,3,2,1,0:T(8,128)S(1)}, f32[4,4,4,32,128]{4,3,2,1,0:T(8,128)S(1)}, u32[]{:S(2)}, u32[]{:S(2)}) collective-permute-start(f32[4,4,4,32,128]{4,3,2,1,0:T(8,128)S(1)} %pad_maximum_fusion.near_ref), channel_id=1, source_target_pairs={{0,8},{8,0},{1,9},{9,1},{2,10},{10,2},{3,11},{11,3},{4,12},{12,4},... | collective-permute-start | bytes 3145736 | tf_op jit(solution)/shard_map/ppermute | solution.py:421
  111.0 1.2 copy-start
  112.1 0.7 copy-start.1
Sparse Core Ops, SparseCore 0:
  9.1 40.7 all-gather.4
  52.5 61.0 all-gather.6

commit v7 on v6

--- a/solution.py
+++ b/solution.py
@@ -219,11 +219,11 @@
 
 
 def factor_second(ids_ref, w0_ref, near_ref, far_ref, x_ref, w_ref, b_ref, *scratch):
-    y, k, x = ids_ref[2], ids_ref[3], ids_ref[4]
+    k, x = ids_ref[3], ids_ref[4]
     for ref, side in ((near_ref, k), (far_ref, 1 - k)):
         for d in range(4):
             for e in range(4):
-                rows = quarter_rows(2 * lax.rem(y + 4 - e, 4) + side, x, d)
+                rows = quarter_rows(2 * e + side, x, d)
                 for j in range(HALF):
                     b_ref[rows, j * TILE : (j + 1) * TILE] = ref[d, e, j]
     parts = split(b_ref[0:PANEL, :])
@@ -366,18 +366,7 @@
     step = pl.program_id(0)
     tiles, _, _ = c_ref.shape
     rows = tiles * TILE
-    quarters = [
-        jnp.concatenate(
-            [
-                ref[x, r, 0]
-                for r in range(TILES)
-                for x in range(4)
-            ],
-            0,
-        )
-        for ref in (even_ref, odd_ref)
-    ]
-    right = jnp.concatenate(quarters, 1)
+    right = jnp.concatenate([ref[...].reshape(WIDTH, TILE) for ref in (even_ref, odd_ref)], 1)
     high = right.astype(jnp.bfloat16)
     low = (right - high.astype(jnp.float32)).astype(jnp.bfloat16)
     left = jnp.concatenate([t_ref[0], t_ref[0], t_ref[1]], 1)
@@ -398,7 +387,7 @@
 def update(ids, t, c, right, kernel):
     tiles, columns = kernel.shape[:2]
     block = pl.BlockSpec((tiles, 2, TILE, TILE), lambda j: (0, j, 0, 0))
-    piece = (4, TILES, 1, TILE // 4, TILE)
+    piece = (TILES, 1, TILE, TILE)
     return pl.pallas_call(
         update_kernel,
         grid=(columns // 2,),
@@ -407,8 +396,8 @@
             SMEM,
             VMEM,
             VMEM,
-            pl.BlockSpec(piece, lambda j: (0, 0, jnp.maximum(2 * j - 1, 0), 0, 0)),
-            pl.BlockSpec(piece, lambda j: (0, 0, 2 * j, 0, 0)),
+            pl.BlockSpec(piece, lambda j: (0, jnp.maximum(2 * j - 1, 0), 0, 0)),
+            pl.BlockSpec(piece, lambda j: (0, 2 * j, 0, 0)),
             block,
         ],
         out_specs=block,
@@ -430,44 +419,29 @@
     return [block] + [send(block, axis, [(i, (i + d) % n) for i in range(n)]) for d in range(1, n)]
 
 
-def gather_z(block):
-    n = lax.axis_size("z")
-    k, z = lax.axis_index("k"), lax.axis_index("z")
-    pair = jnp.stack([block, swap(block)])
-    parts = []
-    for d in (1, 2, 3):
-        up = [(i, (i + d) % n) for i in range(n)]
-        down = [(n + i, n + (i - d) % n) for i in range(n)]
-        parts.append(send(pair, ("k", "z"), up + down))
-    far = send(block, "z", [(i, (i + n // 2) % n) for i in range(n)])
-    parts, far = lax.optimization_barrier((parts, far))
-    mine = jnp.stack([p[0] for p in parts])
-    other = swap(jnp.stack([p[1] for p in parts]))
-    below = jnp.where(k == 0, mine, other)
-    above = jnp.where(k == 0, other, mine)
-    ring = jnp.concatenate([block[None], above, far[None], below[::-1]])
-    return lax.dynamic_slice_in_dim(jnp.concatenate([ring, ring]), (n - z) % n, n, 0)
-
-
 def body(kernel):
     kernel = kernel.transpose(0, 2, 1, 3)
     x = lax.axis_index("x")
-    y = lax.axis_index("y")
     places = (ROW, "z", "y", "k", "x")
     ids = jnp.stack([lax.axis_index(a) for a in places]).astype(jnp.int32)
     mine, kernel = lax.optimization_barrier((kernel[:, 0], kernel))
     own = lax.all_gather(mine, "z")
 
-    quarters = kernel[0].reshape(-1, 4, TILE // 4, TILE)
-    quarter = quarters[:, 0]
+    quarters = kernel[0, 0].reshape(4, TILE // 4, TILE)
+    quarter = quarters[0]
     for d in (1, 3, 2):
-        quarter = jnp.where(x == d, send(quarters[:, d], "x", [(0, d)]), quarter)
-    right = lax.all_gather(quarter[1:], ROW)
-    right = right.reshape(4, TILES, -1, TILE // 4, TILE)
-
-    strips = jnp.stack(around(gather_z(quarter[0]), "y"))
-    top = [lax.dynamic_index_in_dim(strips, (y + 4 - i) % 4, 0, False)[:HALF] for i in range(2)]
-    near = jnp.stack(around(jnp.stack(top), "x"))
+        quarter = jnp.where(x == d, send(quarters[d], "x", [(0, d)]), quarter)
+    quarter, head = lax.optimization_barrier((quarter, kernel[0, 1:]))
+    heads = [send(head, "x", [(0, d)]) for d in (1, 3, 2)]
+
+    strips = jnp.broadcast_to(quarter, (4 * TILES, TILE // 4, TILE))
+    strips = lax.all_to_all(strips, ("y", "z"), 0, 0).reshape(4, TILES, TILE // 4, TILE)
+    near = around(strips[:2, :HALF], "x")
+    near, heads = lax.optimization_barrier((near, heads))
+    for d, block in zip((1, 3, 2), heads):
+        head = jnp.where(x == d, block, head)
+    right = lax.all_gather(head, ("y", "k"))
+    near = jnp.stack(near)
     far = swap(near)
     near, far, rest, own = lax.optimization_barrier((near, far, strips[:, HALF:], own))
     parts = around(rest, "x")

time: 130 us -> 139 us (1.069)
  waiting for transfers between devices: 23.1 us -> 31 us
  other arithmetic: 0.26 us -> 1.91 us
  starting transfers between devices: 42.5 us -> 41.1 us
    all_to_all x0 -> x1, waiting for transfers between devices: none -> 13.1 us  [body(): lax.all_to_all(strips, ('y', 'z'), 0, 0).reshape(4, TILES, TILE // 4, TILE)]
    all_to_all x0 -> x1, starting transfers between devices: none -> 11.2 us  [body(): lax.all_to_all(strips, ('y', 'z'), 0, 0).reshape(4, TILES, TILE // 4, TILE)]
    ppermute x16 -> x12, starting transfers between devices: 34.8 us -> 25.3 us  [send(): return lax.ppermute(x, axis, pairs)]
    ppermute x4 -> x2, starting transfers between devices: 7.58 us -> 4.59 us  [swap(): return lax.ppermute(x, 'k', [(0, 1), (1, 0)])]
    ppermute x16 -> x12, waiting for transfers between devices: 16.8 us -> 14.2 us  [send(): return lax.ppermute(x, axis, pairs)]
    slice x6 -> x1, local copies, waits for them, and re-layouts: 1.92 us -> 0.01 us  [body(): near = around(strips[:2, :HALF], 'x')]
    squeeze x1 -> x2, local copies, waits for them, and re-layouts: 0.04 us -> 1.92 us  [the longest x1 1.16 us: body(): quarter, head = lax.optimization_barrier((quarter, kernel[0, 1:]))]
    ppermute x4 -> x2, waiting for transfers between devices: 5.44 us -> 3.72 us  [swap(): return lax.ppermute(x, 'k', [(0, 1), (1, 0)])]
  transfers between devices with their start and end apart: 22 -> 17, of which waited for: 15 -> 6; matrix products, arithmetic and copies ran while one was open for 2% -> 3% of each run, Pallas kernels for 27% -> 26%
where the time goes in v7:
time: 139 us; the launch traced here: 138 us
  Pallas kernels  44.5 us (32%)
  starting transfers between devices  41.1 us (30%)
  waiting for transfers between devices  31 us (22%)
  between operations  13.6 us (10%)
  local copies, waits for them, and re-layouts  6.3 us (5%)
  other arithmetic  1.91 us (1%)
    ppermute x12, starting transfers between devices, send(): return lax.ppermute(x, axis, pairs)  25.3 us
    pallas_call x1, Pallas kernels, second(): pl.pallas_call(second_kernel, out_shape=[jax.ShapeDtypeStruct((2, rows, W...  21.7 us
    ppermute x12, waiting for transfers between devices, send(): return lax.ppermute(x, axis, pairs)  14.2 us
    pallas_call x1, Pallas kernels, first(): pl.pallas_call(first_kernel, out_shape=jax.ShapeDtypeStruct(FACTOR, jnp.f...  13.7 us
    all_to_all x1, waiting for transfers between devices, body(): lax.all_to_all(strips, ('y', 'z'), 0, 0).reshape(4, TILES, TILE // 4, TILE)  13.1 us
    all_to_all x1, starting transfers between devices, body(): lax.all_to_all(strips, ('y', 'z'), 0, 0).reshape(4, TILES, TILE // 4, TILE)  11.2 us
    pallas_call x1, Pallas kernels, update(): pl.pallas_call(update_kernel, grid=(columns // 2,), out_shape=jax.ShapeDt...  9.05 us
    ppermute x2, starting transfers between devices, swap(): return lax.ppermute(x, 'k', [(0, 1), (1, 0)])  4.59 us
  transfers between devices with their start and end apart: 17, of which 6 were waited for; matrix products, arithmetic and copies ran while one was open for 3% of the time, Pallas kernels for 26%

profile of v7, /device:TPU:1, one launch (start us, length us, event | category | flops | bytes accessed | tf_op | source)
XLA Modules:
  0.0 138.4 jit_solution(15046945743749061301)
XLA Ops:
  6.5 1.6 %slice_bitcast_fusion.1 = f32[3,128,128]{2,1,0:T(8,128)} fusion(f32[3,12,128,128]{3,2,1,0:T(8,128)} %bitcast.37), kind=kLoop, calls=%fused_computation.4 | loop fusion | bytes 393216 | tf_op jit(solution)/shard_map/squeeze | solution.py:427
  8.2 0.8 slice_bitcast_fusion.2
  8.9 5.5 %collective-permute-start = (f32[32,128]{1,0:T(8,128)S(1)}, f32[32,128]{1,0:T(8,128)S(1)}, u32[]{:S(2)}, u32[]{:S(2)}) collective-permute-start(f32[32,128]{1,0:T(8,128)S(1)} %get-tuple-element.51), channel_id=1, source_target_pairs={{0,128},{1,129},{2,130},{3,131},{4,132},{5,133},{6,134},{7,135},{8... | collective-permute-start | bytes 49160 | tf_op jit(solution)/shard_map/ppermute | solution.py:414
  14.4 1.3 collective-permute-start.1
  15.7 1.3 collective-permute-start.2
  17.0 1.2 slice_bitcast_fusion
  18.2 0.7 fusion.1
  18.9 0.9 broadcast_in_dim.3
  19.8 11.2 %all-to-all-start = ((f32[32,32,128]{2,1,0:T(8,128)}), f32[32,32,128]{2,1,0:T(8,128)S(1)}, u32[]{:S(2)}, u32[]{:S(2)}) async-start(f32[32,32,128]{2,1,0:T(8,128)} %broadcast_in_dim.3), calls=%async_computation | async-start | bytes 1048576 | tf_op jit(solution)/shard_map/all_to_all | solution.py:438
  31.1 3.3 %collective-permute-start.6 = (f32[11,128,128]{2,1,0:T(8,128)S(1)}, f32[11,128,128]{2,1,0:T(8,128)S(1)}, u32[]{:S(2)}, u32[]{:S(2)}) collective-permute-start(f32[11,128,128]{2,1,0:T(8,128)S(1)} %slice_bitcast_fusion), channel_id=1, source_target_pairs={{0,64},{1,65},{2,66},{3,67},{4,68},{5,69},{6,70},{7,71},{8,72},{9,... | collective-permute-start | bytes 2162696 | tf_op jit(solution)/shard_map/ppermute | solution.py:414
  34.4 1.3 collective-permute-start.7
  35.7 2.2 %collective-permute-start.8 = (f32[11,128,128]{2,1,0:T(8,128)S(1)}, f32[11,128,128]{2,1,0:T(8,128)}, u32[]{:S(2)}, u32[]{:S(2)}) collective-permute-start(f32[11,128,128]{2,1,0:T(8,128)S(1)} %slice_bitcast_fusion), channel_id=1, source_target_pairs={{0,128},{1,129},{2,130},{3,131},{4,132},{5,133},{6,134},{7,135},{8... | collective-permute-start | bytes 2162696 | tf_op jit(solution)/shard_map/ppermute | solution.py:414
  37.9 13.1 %all-to-all-done = f32[32,32,128]{2,1,0:T(8,128)S(1)} async-done(((f32[32,32,128]{2,1,0:T(8,128)}), f32[32,32,128]{2,1,0:T(8,128)S(1)}, u32[]{:S(2)}, u32[]{:S(2)}) %all-to-all-start) | async-done | bytes 524320 | tf_op jit(solution)/shard_map/all_to_all | solution.py:438
  50.9 1.1 collective-permute-start.3
  52.0 1.2 collective-permute-start.4
  53.2 1.3 collective-permute-start.5
  54.5 8.6 %collective-permute-done.8 = f32[11,128,128]{2,1,0:T(8,128)} collective-permute-done((f32[11,128,128]{2,1,0:T(8,128)S(1)}, f32[11,128,128]{2,1,0:T(8,128)}, u32[]{:S(2)}, u32[]{:S(2)}) %collective-permute-start.8) | collective-permute-done | bytes 720928 | tf_op jit(solution)/shard_map/ppermute | solution.py:414
  63.1 2.8 %collective-permute-done.3 = f32[2,4,32,128]{3,2,1,0:T(8,128)S(1)} collective-permute-done((f32[2,4,32,128]{3,2,1,0:T(8,128)S(1)}, f32[2,4,32,128]{3,2,1,0:T(8,128)S(1)}, u32[]{:S(2)}, u32[]{:S(2)}) %collective-permute-start.3) | collective-permute-done | bytes 131104 | tf_op jit(solution)/shard_map/ppermute | solution.py:414
  65.9 2.8 %collective-permute-done.4 = f32[2,4,32,128]{3,2,1,0:T(8,128)S(1)} collective-permute-done((f32[2,4,32,128]{3,2,1,0:T(8,128)S(1)}, f32[2,4,32,128]{3,2,1,0:T(8,128)S(1)}, u32[]{:S(2)}, u32[]{:S(2)}) %collective-permute-start.4) | collective-permute-done | bytes 131104 | tf_op jit(solution)/shard_map/ppermute | solution.py:414
  68.7 1.1 select_select_fusion
  69.9 3.1 %collective-permute-start.9 = (f32[4,2,4,32,128]{4,3,2,1,0:T(8,128)S(1)}, f32[4,2,4,32,128]{4,3,2,1,0:T(8,128)S(1)}, u32[]{:S(2)}, u32[]{:S(2)}) collective-permute-start(f32[4,2,4,32,128]{4,3,2,1,0:T(8,128)S(1)} %pad_maximum_fusion.1.near_ref), channel_id=1, source_target_pairs={{0,8},{8,0},{1,9},{9,1},{2,10},{10,2},{3,11},{11,3},{4,12},{12,4},... | collective-permute-start | bytes 1572872 | tf_op jit(solution)/shard_map/ppermute | solution.py:410
  73.1 1.4 %collective-permute-done.9.far_ref = f32[4,2,4,32,128]{4,3,2,1,0:T(8,128)S(1)} collective-permute-done((f32[4,2,4,32,128]{4,3,2,1,0:T(8,128)S(1)}, f32[4,2,4,32,128]{4,3,2,1,0:T(8,128)S(1)}, u32[]{:S(2)}, u32[]{:S(2)}) %collective-permute-start.9) | collective-permute-done | bytes 524320 | tf_op jit(solution)/shard_map/ppermute | solution.py:410
  74.5 0.8 collective-permute-start.10
  75.3 4.0 %collective-permute-start.11 = (f32[4,4,32,128]{3,2,1,0:T(8,128)S(1)}, f32[4,4,32,128]{3,2,1,0:T(8,128)S(1)}, u32[]{:S(2)}, u32[]{:S(2)}) collective-permute-start(f32[4,4,32,128]{3,2,1,0:T(8,128)S(1)} %slice.43), channel_id=1, source_target_pairs={{0,128},{64,192},{128,0},{192,64},{1,129},{65,193},{129,1},{193,65... | collective-permute-start | bytes 786440 | tf_op jit(solution)/shard_map/ppermute | solution.py:414
  79.3 2.1 %collective-permute-start.12 = (f32[4,4,32,128]{3,2,1,0:T(8,128)S(1)}, f32[4,4,32,128]{3,2,1,0:T(8,128)S(1)}, u32[]{:S(2)}, u32[]{:S(2)}) collective-permute-start(f32[4,4,32,128]{3,2,1,0:T(8,128)S(1)} %slice.43), channel_id=1, source_target_pairs={{0,192},{64,0},{128,64},{192,128},{1,193},{65,1},{129,65},{193,129... | collective-permute-start | bytes 786440 | tf_op jit(solution)/shard_map/ppermute | solution.py:414
  81.4 13.7 %first.1.w0_ref = f32[768,512]{1,0:T(8,128)S(1)} custom-call(s32[5]{0:T(128)S(1)} %stack.53.ids_ref, f32[4,2,4,32,128]{4,3,2,1,0:T(8,128)S(1)} %pad_maximum_fusion.1.near_ref, f32[4,2,4,32,128]{4,3,2,1,0:T(8,128)S(1)} %collective-permute-done.9.far_ref), custom_call_target="tpu_custom_call" | custom-call | flops 8589934592 | bytes 4194304 | tf_op jit(solution)/shard_map/first/pallas_call | solution.py:209
  95.3 1.5 %collective-permute-start.13 = (f32[4,4,4,32,128]{4,3,2,1,0:T(8,128)S(1)}, f32[4,4,4,32,128]{4,3,2,1,0:T(8,128)S(1)}, u32[]{:S(2)}, u32[]{:S(2)}) collective-permute-start(f32[4,4,4,32,128]{4,3,2,1,0:T(8,128)S(1)} %pad_maximum_fusion.near_ref), channel_id=1, source_target_pairs={{0,8},{8,0},{1,9},{9,1},{2,10},{10,2},{3,11},{11,3},{4,12},{12,4},... | collective-permute-start | bytes 3145736 | tf_op jit(solution)/shard_map/ppermute | solution.py:410
  96.8 2.3 %collective-permute-done.13.far_ref = f32[4,4,4,32,128]{4,3,2,1,0:T(8,128)S(1)} collective-permute-done((f32[4,4,4,32,128]{4,3,2,1,0:T(8,128)S(1)}, f32[4,4,4,32,128]{4,3,2,1,0:T(8,128)S(1)}, u32[]{:S(2)}, u32[]{:S(2)}) %collective-permute-start.13) | collective-permute-done | bytes 1048608 | tf_op jit(solution)/shard_map/ppermute | solution.py:410
  99.1 21.7 %second.1 = (bf16[2,384,1024]{2,1,0:T(8,128)(2,1)S(1)}, f32[3,128,128]{2,1,0:T(8,128)S(1)}) custom-call(s32[5]{0:T(128)S(1)} %stack.53.ids_ref, f32[768,512]{1,0:T(8,128)S(1)} %first.1.w0_ref, f32[4,4,4,32,128]{4,3,2,1,0:T(8,128)S(1)} %pad_maximum_fusion.near_ref, f32[4,4,4,32,128]{4,3,2,1,0:T(8,128)S(1)} %collective-permute-done.13.far_ref, ...), custom_call_target="tpu_custom_call" | custom-call | flops 17179869184 | bytes 8388608 | tf_op jit(solution)/shard_map/second/pallas_call | solution.py:340
  120.7 1.1 copy-done
  121.9 0.7 copy-done.1
  122.5 9.1 %update.1 = f32[3,12,128,128]{3,2,1,0:T(8,128)} custom-call(s32[5]{0:T(128)} %copy-done.2, bf16[2,384,1024]{2,1,0:T(8,128)(2,1)} %copy-done, f32[3,128,128]{2,1,0:T(8,128)} %copy-done.1, f32[8,11,128,128]{3,2,1,0:T(8,128)} %bitcast.35, f32[8,11,128,128]{3,2,1,0:T(8,128)} %bitcast.36, f32[3,12,128,128]{3,2,1,0:T(8,128)} %bitcast.41), custom_call_target="tpu_custom_call" | custom-call | tf_op jit(solution)/shard_map/update/pallas_call | solution.py:391
  (26 shorter events, 0.4 us)
Async XLA Ops:
  6.5 68.0 %all-gather.5.cloned.1.call-start = ((), (), s32[]{:S(2)}) async-start(), calls=%async_computation.1 | async-start | bytes 1769472 | tf_op jit(solution)/shard_map/all_gather | solution.py:428
  8.9 9.3 %collective-permute-start = (f32[32,128]{1,0:T(8,128)S(1)}, f32[32,128]{1,0:T(8,128)S(1)}, u32[]{:S(2)}, u32[]{:S(2)}) collective-permute-start(f32[32,128]{1,0:T(8,128)S(1)} %get-tuple-element.51), channel_id=1, source_target_pairs={{0,128},{1,129},{2,130},{3,131},{4,132},{5,133},{6,134},{7,135},{8... | collective-permute-start | bytes 49160 | tf_op jit(solution)/shard_map/ppermute | solution.py:414
  14.4 3.8 %collective-permute-start.1 = (f32[32,128]{1,0:T(8,128)S(1)}, f32[32,128]{1,0:T(8,128)S(1)}, u32[]{:S(2)}, u32[]{:S(2)}) collective-permute-start(f32[32,128]{1,0:T(8,128)S(1)} %get-tuple-element.50), channel_id=1, source_target_pairs={{0,192},{1,193},{2,194},{3,195},{4,196},{5,197},{6,198},{7,199},{8... | collective-permute-start | bytes 49160 | tf_op jit(solution)/shard_map/ppermute | solution.py:414
  15.7 2.5 %collective-permute-start.2 = (f32[32,128]{1,0:T(8,128)S(1)}, f32[32,128]{1,0:T(8,128)S(1)}, u32[]{:S(2)}, u32[]{:S(2)}) collective-permute-start(f32[32,128]{1,0:T(8,128)S(1)} %get-tuple-element.49), channel_id=1, source_target_pairs={{0,64},{1,65},{2,66},{3,67},{4,68},{5,69},{6,70},{7,71},{8,72},{9,... | collective-permute-start | bytes 49160 | tf_op jit(solution)/shard_map/ppermute | solution.py:414
  19.8 31.1 %all-to-all-start = ((f32[32,32,128]{2,1,0:T(8,128)}), f32[32,32,128]{2,1,0:T(8,128)S(1)}, u32[]{:S(2)}, u32[]{:S(2)}) async-start(f32[32,32,128]{2,1,0:T(8,128)} %broadcast_in_dim.3), calls=%async_computation | async-start | bytes 1048576 | tf_op jit(solution)/shard_map/all_to_all | solution.py:438
  31.0 91.5 %all-gather.7.cloned.1.call-start = ((), (), s32[]{:S(2)}) async-start(), calls=%async_computation.2 | async-start | bytes 6488064 | tf_op jit(solution)/shard_map/all_gather | solution.py:443
  31.1 22.1 %collective-permute-start.6 = (f32[11,128,128]{2,1,0:T(8,128)S(1)}, f32[11,128,128]{2,1,0:T(8,128)S(1)}, u32[]{:S(2)}, u32[]{:S(2)}) collective-permute-start(f32[11,128,128]{2,1,0:T(8,128)S(1)} %slice_bitcast_fusion), channel_id=1, source_target_pairs={{0,64},{1,65},{2,66},{3,67},{4,68},{5,69},{6,70},{7,71},{8,72},{9,... | collective-permute-start | bytes 2162696 | tf_op jit(solution)/shard_map/ppermute | solution.py:414
  34.4 20.2 %collective-permute-start.7 = (f32[11,128,128]{2,1,0:T(8,128)S(1)}, f32[11,128,128]{2,1,0:T(8,128)S(1)}, u32[]{:S(2)}, u32[]{:S(2)}) collective-permute-start(f32[11,128,128]{2,1,0:T(8,128)S(1)} %slice_bitcast_fusion), channel_id=1, source_target_pairs={{0,192},{1,193},{2,194},{3,195},{4,196},{5,197},{6,198},{7,199},{8... | collective-permute-start | bytes 2162696 | tf_op jit(solution)/shard_map/ppermute | solution.py:414
  35.7 27.4 %collective-permute-start.8 = (f32[11,128,128]{2,1,0:T(8,128)S(1)}, f32[11,128,128]{2,1,0:T(8,128)}, u32[]{:S(2)}, u32[]{:S(2)}) collective-permute-start(f32[11,128,128]{2,1,0:T(8,128)S(1)} %slice_bitcast_fusion), channel_id=1, source_target_pairs={{0,128},{1,129},{2,130},{3,131},{4,132},{5,133},{6,134},{7,135},{8... | collective-permute-start | bytes 2162696 | tf_op jit(solution)/shard_map/ppermute | solution.py:414
  50.9 15.0 %collective-permute-start.3 = (f32[2,4,32,128]{3,2,1,0:T(8,128)S(1)}, f32[2,4,32,128]{3,2,1,0:T(8,128)S(1)}, u32[]{:S(2)}, u32[]{:S(2)}) collective-permute-start(f32[2,4,32,128]{3,2,1,0:T(8,128)S(1)} %slice.42), channel_id=1, source_target_pairs={{0,64},{64,128},{128,192},{192,0},{1,65},{65,129},{129,193},{193,1... | collective-permute-start | bytes 393224 | tf_op jit(solution)/shard_map/ppermute | solution.py:414
  52.0 16.7 %collective-permute-start.4 = (f32[2,4,32,128]{3,2,1,0:T(8,128)S(1)}, f32[2,4,32,128]{3,2,1,0:T(8,128)S(1)}, u32[]{:S(2)}, u32[]{:S(2)}) collective-permute-start(f32[2,4,32,128]{3,2,1,0:T(8,128)S(1)} %slice.42), channel_id=1, source_target_pairs={{0,128},{64,192},{128,0},{192,64},{1,129},{65,193},{129,1},{193,65... | collective-permute-start | bytes 393224 | tf_op jit(solution)/shard_map/ppermute | solution.py:414
  53.2 15.6 %collective-permute-start.5 = (f32[2,4,32,128]{3,2,1,0:T(8,128)S(1)}, f32[2,4,32,128]{3,2,1,0:T(8,128)S(1)}, u32[]{:S(2)}, u32[]{:S(2)}) collective-permute-start(f32[2,4,32,128]{3,2,1,0:T(8,128)S(1)} %slice.42), channel_id=1, source_target_pairs={{0,192},{64,0},{128,64},{192,128},{1,193},{65,1},{129,65},{193,129... | collective-permute-start | bytes 393224 | tf_op jit(solution)/shard_map/ppermute | solution.py:414
  69.9 4.7 %collective-permute-start.9 = (f32[4,2,4,32,128]{4,3,2,1,0:T(8,128)S(1)}, f32[4,2,4,32,128]{4,3,2,1,0:T(8,128)S(1)}, u32[]{:S(2)}, u32[]{:S(2)}) collective-permute-start(f32[4,2,4,32,128]{4,3,2,1,0:T(8,128)S(1)} %pad_maximum_fusion.1.near_ref), channel_id=1, source_target_pairs={{0,8},{8,0},{1,9},{9,1},{2,10},{10,2},{3,11},{11,3},{4,12},{12,4},... | collective-permute-start | bytes 1572872 | tf_op jit(solution)/shard_map/ppermute | solution.py:410
  73.1 26.0 %copy-start.2 = (s32[5]{0:T(128)}, s32[5]{0:T(128)S(1)}, u32[]{:S(2)}) copy-start(s32[5]{0:T(128)S(1)} %stack.53.ids_ref) | copy-start | bytes 64
  74.5 24.5 %copy-start.3 = (f32[24,128,128]{2,1,0:T(8,128)S(1)}, f32[24,128,128]{2,1,0:T(8,128)}, u32[]{:S(2)}) copy-start(f32[24,128,128]{2,1,0:T(8,128)} %all-gather.5.cloned.1.call-done) | copy-start | bytes 4718596
  74.5 20.6 %collective-permute-start.10 = (f32[4,4,32,128]{3,2,1,0:T(8,128)S(1)}, f32[4,4,32,128]{3,2,1,0:T(8,128)S(1)}, u32[]{:S(2)}, u32[]{:S(2)}) collective-permute-start(f32[4,4,32,128]{3,2,1,0:T(8,128)S(1)} %slice.43), channel_id=1, source_target_pairs={{0,64},{64,128},{128,192},{192,0},{1,65},{65,129},{129,193},{193,1... | collective-permute-start | bytes 786440 | tf_op jit(solution)/shard_map/ppermute | solution.py:414
  75.3 19.9 %collective-permute-start.11 = (f32[4,4,32,128]{3,2,1,0:T(8,128)S(1)}, f32[4,4,32,128]{3,2,1,0:T(8,128)S(1)}, u32[]{:S(2)}, u32[]{:S(2)}) collective-permute-start(f32[4,4,32,128]{3,2,1,0:T(8,128)S(1)} %slice.43), channel_id=1, source_target_pairs={{0,128},{64,192},{128,0},{192,64},{1,129},{65,193},{129,1},{193,65... | collective-permute-start | bytes 786440 | tf_op jit(solution)/shard_map/ppermute | solution.py:414
  79.3 15.8 %collective-permute-start.12 = (f32[4,4,32,128]{3,2,1,0:T(8,128)S(1)}, f32[4,4,32,128]{3,2,1,0:T(8,128)S(1)}, u32[]{:S(2)}, u32[]{:S(2)}) collective-permute-start(f32[4,4,32,128]{3,2,1,0:T(8,128)S(1)} %slice.43), channel_id=1, source_target_pairs={{0,192},{64,0},{128,64},{192,128},{1,193},{65,1},{129,65},{193,129... | collective-permute-start | bytes 786440 | tf_op jit(solution)/shard_map/ppermute | solution.py:414
  95.3 3.8 %collective-permute-start.13 = (f32[4,4,4,32,128]{4,3,2,1,0:T(8,128)S(1)}, f32[4,4,4,32,128]{4,3,2,1,0:T(8,128)S(1)}, u32[]{:S(2)}, u32[]{:S(2)}) collective-permute-start(f32[4,4,4,32,128]{4,3,2,1,0:T(8,128)S(1)} %pad_maximum_fusion.near_ref), channel_id=1, source_target_pairs={{0,8},{8,0},{1,9},{9,1},{2,10},{10,2},{3,11},{11,3},{4,12},{12,4},... | collective-permute-start | bytes 3145736 | tf_op jit(solution)/shard_map/ppermute | solution.py:410
  120.7 1.1 copy-start
  121.9 0.7 copy-start.1
Sparse Core Ops, SparseCore 0:
  9.1 47.7 all-gather.4
  69.9 47.3 all-gather.6

commit v8 on v6

--- a/solution.py
+++ b/solution.py
@@ -362,59 +362,53 @@
     )(ids, w0, near, far, own)
 
 
-def update_kernel(ids_ref, t_ref, c_ref, even_ref, odd_ref, k_ref, o_ref):
-    step = pl.program_id(0)
-    tiles, _, _ = c_ref.shape
-    rows = tiles * TILE
-    quarters = [
-        jnp.concatenate(
-            [
-                ref[x, r, 0]
-                for r in range(TILES)
-                for x in range(4)
-            ],
-            0,
-        )
-        for ref in (even_ref, odd_ref)
-    ]
-    right = jnp.concatenate(quarters, 1)
+def update_kernel(ids_ref, t_ref, c_ref, *refs):
+    *right_refs, k_ref, o_ref = refs
+    n = len(right_refs)
+    right = jnp.concatenate(
+        [
+            jnp.concatenate([ref[x, r, 0] for r in range(TILES) for x in range(4)], 0)
+            for ref in right_refs
+        ],
+        1,
+    )
     high = right.astype(jnp.bfloat16)
     low = (right - high.astype(jnp.float32)).astype(jnp.bfloat16)
     left = jnp.concatenate([t_ref[0], t_ref[0], t_ref[1]], 1)
     product = contract(left, jnp.concatenate([high, low, high], 0), 1, 0)
-    product = product.reshape(tiles, TILE, 2 * TILE)
-    for i in range(2):
+    product = product.reshape(-1, TILE, n * TILE)
+    for i in range(n):
         o_ref[:, i] = k_ref[:, i] - product[:, :, i * TILE : (i + 1) * TILE]
 
     @pl.when(ids_ref[0] < TILES)
     def _():
         o_ref[0] = jnp.zeros(o_ref.shape[1:], jnp.float32)
 
-    @pl.when(step == 0)
+    @pl.when(pl.program_id(0) == 0)
     def _():
         o_ref[:, 0] = c_ref[...]
 
 
 def update(ids, t, c, right, kernel):
     tiles, columns = kernel.shape[:2]
-    block = pl.BlockSpec((tiles, 2, TILE, TILE), lambda j: (0, j, 0, 0))
-    piece = (4, TILES, 1, TILE // 4, TILE)
+    n = 4
+    block = pl.BlockSpec((tiles, n, TILE, TILE), lambda j: (0, j, 0, 0))
+
+    def piece(i):
+        return pl.BlockSpec(
+            (4, TILES, 1, TILE // 4, TILE),
+            lambda j: (0, 0, jnp.maximum(n * j + i - 1, 0), 0, 0),
+        )
+
     return pl.pallas_call(
         update_kernel,
-        grid=(columns // 2,),
+        grid=(columns // n,),
         out_shape=jax.ShapeDtypeStruct(kernel.shape, jnp.float32),
-        in_specs=[
-            SMEM,
-            VMEM,
-            VMEM,
-            pl.BlockSpec(piece, lambda j: (0, 0, jnp.maximum(2 * j - 1, 0), 0, 0)),
-            pl.BlockSpec(piece, lambda j: (0, 0, 2 * j, 0, 0)),
-            block,
-        ],
+        in_specs=[SMEM, VMEM, VMEM] + [piece(i) for i in range(n)] + [block],
         out_specs=block,
         compiler_params=pltpu.CompilerParams(vmem_limit_bytes=60 << 20),
         name="update",
-    )(ids, t, c, right, right, kernel)
+    )(ids, t, c, *[right] * n, kernel)
 
 
 def swap(x):
@@ -468,8 +462,8 @@
     strips = jnp.stack(around(gather_z(quarter[0]), "y"))
     top = [lax.dynamic_index_in_dim(strips, (y + 4 - i) % 4, 0, False)[:HALF] for i in range(2)]
     near = jnp.stack(around(jnp.stack(top), "x"))
+    near, rest, own = lax.optimization_barrier((near, strips[:, HALF:], own))
     far = swap(near)
-    near, far, rest, own = lax.optimization_barrier((near, far, strips[:, HALF:], own))
     parts = around(rest, "x")
     w0 = first(ids, near, far)
     w0, parts = lax.optimization_barrier((w0, parts))

time: 130 us -> 128 us (0.985)
    ppermute x4, waiting for transfers between devices: 5.44 us -> 4.01 us  [swap(): return lax.ppermute(x, 'k', [(0, 1), (1, 0)])]
  transfers between devices with their start and end apart: 22 -> 22, of which waited for: 15 -> 14; matrix products, arithmetic and copies ran while one was open for 2% -> 2% of each run, Pallas kernels for 27% -> 28%
where the time goes in v8:
time: 128 us
  Pallas kernels  43.5 us (34%)
  starting transfers between devices  42.8 us (33%)
  waiting for transfers between devices  22 us (17%)
  between operations  13.6 us (11%)
  local copies, waits for them, and re-layouts  5.56 us (4%)
    ppermute x16, starting transfers between devices, send(): return lax.ppermute(x, axis, pairs)  34.9 us
    pallas_call x1, Pallas kernels, second(): pl.pallas_call(second_kernel, out_shape=[jax.ShapeDtypeStruct((2, rows, W...  21.7 us
    ppermute x16, waiting for transfers between devices, send(): return lax.ppermute(x, axis, pairs)  16.6 us
    pallas_call x1, Pallas kernels, first(): pl.pallas_call(first_kernel, out_shape=jax.ShapeDtypeStruct(FACTOR, jnp.f...  13.7 us
    pallas_call x1, Pallas kernels, update(): pl.pallas_call(update_kernel, grid=(columns // n,), out_shape=jax.ShapeDt...  8.12 us
    ppermute x4, starting transfers between devices, swap(): return lax.ppermute(x, 'k', [(0, 1), (1, 0)])  7.83 us
    ppermute x4, waiting for transfers between devices, swap(): return lax.ppermute(x, 'k', [(0, 1), (1, 0)])  4.01 us
  transfers between devices with their start and end apart: 22, of which 14 were waited for; matrix products, arithmetic and copies ran while one was open for 2% of the time, Pallas kernels for 28%

profile of v8, /device:TPU:1, one launch (start us, length us, event | category | flops | bytes accessed | tf_op | source)
XLA Modules:
  0.0 127.8 jit_solution(5376465309740532236)
XLA Ops:
  6.5 1.6 %slice_bitcast_fusion.4 = f32[3,128,128]{2,1,0:T(8,128)} fusion(f32[3,12,128,128]{3,2,1,0:T(8,128)} %bitcast.59), kind=kLoop, calls=%fused_computation.10 | loop fusion | bytes 393216 | tf_op jit(solution)/shard_map/squeeze | solution.py:452
  8.2 1.2 slice.54
  9.5 5.5 %collective-permute-start = (f32[12,32,128]{2,1,0:T(8,128)S(1)}, f32[12,32,128]{2,1,0:T(8,128)S(1)}, u32[]{:S(2)}, u32[]{:S(2)}) collective-permute-start(f32[12,32,128]{2,1,0:T(8,128)S(1)} %get-tuple-element.39), channel_id=1, source_target_pairs={{0,128},{1,129},{2,130},{3,131},{4,132},{5,133},{6,134},{7,135},{8... | collective-permute-start | bytes 589832 | tf_op jit(solution)/shard_map/ppermute | solution.py:419
  15.0 1.3 %collective-permute-start.1 = (f32[12,32,128]{2,1,0:T(8,128)S(1)}, f32[12,32,128]{2,1,0:T(8,128)S(1)}, u32[]{:S(2)}, u32[]{:S(2)}) collective-permute-start(f32[12,32,128]{2,1,0:T(8,128)S(1)} %get-tuple-element.38), channel_id=1, source_target_pairs={{0,192},{1,193},{2,194},{3,195},{4,196},{5,197},{6,198},{7,199},{8... | collective-permute-start | bytes 589832 | tf_op jit(solution)/shard_map/ppermute | solution.py:419
  16.3 1.3 %collective-permute-start.2 = (f32[12,32,128]{2,1,0:T(8,128)S(1)}, f32[12,32,128]{2,1,0:T(8,128)S(1)}, u32[]{:S(2)}, u32[]{:S(2)}) collective-permute-start(f32[12,32,128]{2,1,0:T(8,128)S(1)} %get-tuple-element.37), channel_id=1, source_target_pairs={{0,64},{1,65},{2,66},{3,67},{4,68},{5,69},{6,70},{7,71},{8,72},{9,... | collective-permute-start | bytes 589832 | tf_op jit(solution)/shard_map/ppermute | solution.py:419
  17.6 0.9 collective-permute-done
  18.5 1.3 %collective-permute-done.1 = f32[12,32,128]{2,1,0:T(8,128)S(1)} collective-permute-done((f32[12,32,128]{2,1,0:T(8,128)S(1)}, f32[12,32,128]{2,1,0:T(8,128)S(1)}, u32[]{:S(2)}, u32[]{:S(2)}) %collective-permute-start.1) | collective-permute-done | bytes 196640 | tf_op jit(solution)/shard_map/ppermute | solution.py:419
  19.8 2.9 %collective-permute-done.2 = f32[12,32,128]{2,1,0:T(8,128)S(1)} collective-permute-done((f32[12,32,128]{2,1,0:T(8,128)S(1)}, f32[12,32,128]{2,1,0:T(8,128)S(1)}, u32[]{:S(2)}, u32[]{:S(2)}) %collective-permute-start.2) | collective-permute-done | bytes 196640 | tf_op jit(solution)/shard_map/ppermute | solution.py:419
  23.5 1.6 %collective-permute-start.3 = (f32[32,128]{1,0:T(8,128)S(1)}, f32[32,128]{1,0:T(8,128)S(1)}, u32[]{:S(2)}, u32[]{:S(2)}) collective-permute-start(f32[32,128]{1,0:T(8,128)S(1)} %get-tuple-element.43), channel_id=1, source_target_pairs={{0,8},{8,0},{1,9},{9,1},{2,10},{10,2},{3,11},{11,3},{4,12},{12,4},... | collective-permute-start | bytes 49160 | tf_op jit(solution)/shard_map/ppermute | solution.py:415
  26.0 5.6 %collective-permute-start.4 = (f32[2,32,128]{2,1,0:T(8,128)S(1)}, f32[2,32,128]{2,1,0:T(8,128)S(1)}, u32[]{:S(2)}, u32[]{:S(2)}) collective-permute-start(f32[2,32,128]{2,1,0:T(8,128)S(1)} %pad_maximum_fusion.6), channel_id=1, source_target_pairs={{0,1},{1,2},{2,3},{3,4},{4,5},{5,6},{6,7},{7,0},{8,15},{9,8},{10,9... | collective-permute-start | bytes 98312 | tf_op jit(solution)/shard_map/ppermute | solution.py:419
  31.6 1.2 collective-permute-start.5
  33.2 4.5 %collective-permute-start.7 = (f32[32,128]{1,0:T(8,128)S(1)}, f32[32,128]{1,0:T(8,128)S(1)}, u32[]{:S(2)}, u32[]{:S(2)}) collective-permute-start(f32[32,128]{1,0:T(8,128)S(1)} %get-tuple-element.43), channel_id=1, source_target_pairs={{0,4},{1,5},{2,6},{3,7},{4,0},{5,1},{6,2},{7,3},{8,12},{9,13},{10,... | collective-permute-start | bytes 49160 | tf_op jit(solution)/shard_map/ppermute | solution.py:419
  37.7 2.6 %collective-permute-done.7 = f32[32,128]{1,0:T(8,128)S(1)} collective-permute-done((f32[32,128]{1,0:T(8,128)S(1)}, f32[32,128]{1,0:T(8,128)S(1)}, u32[]{:S(2)}, u32[]{:S(2)}) %collective-permute-start.7) | collective-permute-done | bytes 16416 | tf_op jit(solution)/shard_map/ppermute | solution.py:419
  40.3 3.0 %collective-permute-start.8 = (f32[3,32,128]{2,1,0:T(8,128)S(1)}, f32[3,32,128]{2,1,0:T(8,128)S(1)}, u32[]{:S(2)}, u32[]{:S(2)}) collective-permute-start(f32[3,32,128]{2,1,0:T(8,128)S(1)} %pad_maximum_fusion.4), channel_id=1, source_target_pairs={{0,8},{8,0},{1,9},{9,1},{2,10},{10,2},{3,11},{11,3},{4,12},{12,4},... | collective-permute-start | bytes 147464 | tf_op jit(solution)/shard_map/ppermute | solution.py:415
  44.4 1.5 %collective-permute-start.9 = (f32[8,32,128]{2,1,0:T(8,128)S(1)}, f32[8,32,128]{2,1,0:T(8,128)S(1)}, u32[]{:S(2)}, u32[]{:S(2)}) collective-permute-start(f32[8,32,128]{2,1,0:T(8,128)S(1)} %constant_dynamic-slice_fusion.2), channel_id=1, source_target_pairs={{0,16},{16,32},{32,48},{48,0},{1,17},{17,33},{33,49},{49,1},{2,18}... | collective-permute-start | bytes 393224 | tf_op jit(solution)/shard_map/ppermute | solution.py:419
  45.8 2.6 %collective-permute-start.10 = (f32[8,32,128]{2,1,0:T(8,128)S(1)}, f32[8,32,128]{2,1,0:T(8,128)S(1)}, u32[]{:S(2)}, u32[]{:S(2)}) collective-permute-start(f32[8,32,128]{2,1,0:T(8,128)S(1)} %constant_dynamic-slice_fusion.2), channel_id=1, source_target_pairs={{0,32},{16,48},{32,0},{48,16},{1,33},{17,49},{33,1},{49,17},{2,34}... | collective-permute-start | bytes 393224 | tf_op jit(solution)/shard_map/ppermute | solution.py:419
  48.5 1.1 collective-permute-start.11
  49.5 1.2 collective-permute-done.9
  50.7 3.8 %collective-permute-done.10 = f32[8,32,128]{2,1,0:T(8,128)S(1)} collective-permute-done((f32[8,32,128]{2,1,0:T(8,128)S(1)}, f32[8,32,128]{2,1,0:T(8,128)S(1)}, u32[]{:S(2)}, u32[]{:S(2)}) %collective-permute-start.10) | collective-permute-done | bytes 131104 | tf_op jit(solution)/shard_map/ppermute | solution.py:419
  54.6 2.5 %collective-permute-start.12 = (f32[2,4,32,128]{3,2,1,0:T(8,128)S(1)}, f32[2,4,32,128]{3,2,1,0:T(8,128)S(1)}, u32[]{:S(2)}, u32[]{:S(2)}) collective-permute-start(f32[2,4,32,128]{3,2,1,0:T(8,128)S(1)} %get-tuple-element.46), channel_id=1, source_target_pairs={{0,64},{64,128},{128,192},{192,0},{1,65},{65,129},{129,193},{193,1... | collective-permute-start | bytes 393224 | tf_op jit(solution)/shard_map/ppermute | solution.py:419
  57.1 2.5 %collective-permute-start.14 = (f32[2,4,32,128]{3,2,1,0:T(8,128)S(1)}, f32[2,4,32,128]{3,2,1,0:T(8,128)S(1)}, u32[]{:S(2)}, u32[]{:S(2)}) collective-permute-start(f32[2,4,32,128]{3,2,1,0:T(8,128)S(1)} %get-tuple-element.46), channel_id=1, source_target_pairs={{0,192},{64,0},{128,64},{192,128},{1,193},{65,1},{129,65},{193,129... | collective-permute-start | bytes 393224 | tf_op jit(solution)/shard_map/ppermute | solution.py:419
  59.7 2.8 %collective-permute-done.13 = f32[2,4,32,128]{3,2,1,0:T(8,128)S(1)} collective-permute-done((f32[2,4,32,128]{3,2,1,0:T(8,128)S(1)}, f32[2,4,32,128]{3,2,1,0:T(8,128)S(1)}, u32[]{:S(2)}, u32[]{:S(2)}) %collective-permute-start.13) | collective-permute-done | bytes 131104 | tf_op jit(solution)/shard_map/ppermute | solution.py:419
  63.2 2.2 %collective-permute-start.15 = (f32[4,2,4,32,128]{4,3,2,1,0:T(8,128)S(1)}, f32[4,2,4,32,128]{4,3,2,1,0:T(8,128)S(1)}, u32[]{:S(2)}, u32[]{:S(2)}) collective-permute-start(f32[4,2,4,32,128]{4,3,2,1,0:T(8,128)S(1)} %pad_maximum_fusion.2.near_ref), channel_id=1, source_target_pairs={{0,8},{8,0},{1,9},{9,1},{2,10},{10,2},{3,11},{11,3},{4,12},{12,4},... | collective-permute-start | bytes 1572872 | tf_op jit(solution)/shard_map/ppermute | solution.py:415
  65.5 1.8 %collective-permute-start.16 = (f32[4,4,32,128]{3,2,1,0:T(8,128)S(1)}, f32[4,4,32,128]{3,2,1,0:T(8,128)S(1)}, u32[]{:S(2)}, u32[]{:S(2)}) collective-permute-start(f32[4,4,32,128]{3,2,1,0:T(8,128)S(1)} %slice.76), channel_id=1, source_target_pairs={{0,64},{64,128},{128,192},{192,0},{1,65},{65,129},{129,193},{193,1... | collective-permute-start | bytes 786440 | tf_op jit(solution)/shard_map/ppermute | solution.py:419
  67.3 2.3 %collective-permute-start.17 = (f32[4,4,32,128]{3,2,1,0:T(8,128)S(1)}, f32[4,4,32,128]{3,2,1,0:T(8,128)S(1)}, u32[]{:S(2)}, u32[]{:S(2)}) collective-permute-start(f32[4,4,32,128]{3,2,1,0:T(8,128)S(1)} %slice.76), channel_id=1, source_target_pairs={{0,128},{64,192},{128,0},{192,64},{1,129},{65,193},{129,1},{193,65... | collective-permute-start | bytes 786440 | tf_op jit(solution)/shard_map/ppermute | solution.py:419
  70.4 13.7 %first.1.w0_ref = f32[768,512]{1,0:T(8,128)S(1)} custom-call(s32[5]{0:T(128)S(1)} %stack.85.ids_ref, f32[4,2,4,32,128]{4,3,2,1,0:T(8,128)S(1)} %pad_maximum_fusion.2.near_ref, f32[4,2,4,32,128]{4,3,2,1,0:T(8,128)S(1)} %collective-permute-done.15.far_ref), custom_call_target="tpu_custom_call" | custom-call | flops 8589934592 | bytes 4194304 | tf_op jit(solution)/shard_map/first/pallas_call | solution.py:209
  84.6 1.0 collective-permute-start.19
  85.6 2.3 %collective-permute-done.19.far_ref = f32[4,4,4,32,128]{4,3,2,1,0:T(8,128)S(1)} collective-permute-done((f32[4,4,4,32,128]{4,3,2,1,0:T(8,128)S(1)}, f32[4,4,4,32,128]{4,3,2,1,0:T(8,128)S(1)}, u32[]{:S(2)}, u32[]{:S(2)}) %collective-permute-start.19) | collective-permute-done | bytes 1048608 | tf_op jit(solution)/shard_map/ppermute | solution.py:415
  87.9 21.7 %second.1 = (bf16[2,384,1024]{2,1,0:T(8,128)(2,1)S(1)}, f32[3,128,128]{2,1,0:T(8,128)S(1)}) custom-call(s32[5]{0:T(128)S(1)} %stack.85.ids_ref, f32[768,512]{1,0:T(8,128)S(1)} %first.1.w0_ref, f32[4,4,4,32,128]{4,3,2,1,0:T(8,128)S(1)} %pad_maximum_fusion.near_ref, f32[4,4,4,32,128]{4,3,2,1,0:T(8,128)S(1)} %collective-permute-done.19.far_ref, ...), custom_call_target="tpu_custom_call" | custom-call | flops 17179869184 | bytes 8388608 | tf_op jit(solution)/shard_map/second/pallas_call | solution.py:340
  109.6 1.1 copy-done
  111.4 1.4 %all-gather.7.cloned.1.call-done = f32[352,32,128]{2,1,0:T(8,128)} async-done(((f32[11,32,128]{2,1,0:T(8,128)}), f32[352,32,128]{2,1,0:T(8,128)}) %all-gather.7.cloned.1.call-update) | async-done | bytes 5767184 | tf_op jit(solution)/shard_map/all_gather | solution.py:459
  112.8 8.1 %update.1 = f32[3,12,128,128]{3,2,1,0:T(8,128)} custom-call(s32[5]{0:T(128)} %copy-done.2, bf16[2,384,1024]{2,1,0:T(8,128)(2,1)} %copy-done, f32[3,128,128]{2,1,0:T(8,128)} %copy-done.1, f32[4,8,11,32,128]{4,3,2,1,0:T(8,128)} %bitcast.55, f32[4,8,11,32,128]{4,3,2,1,0:T(8,128)} %bitcast.56, f32[4,8,11,32,128]{4,3,2,1,0:T(8,128)} %bitcast.57, ...), custom_call_target="tpu_custom_call" | custom-call | tf_op jit(solution)/shard_map/update/pallas_call | solution.py:403
  (51 shorter events, 6.0 us)
Async XLA Ops:
  6.5 56.6 %all-gather.5.cloned.1.call-start = ((), (), s32[]{:S(2)}) async-start(), calls=%async_computation | async-start | bytes 1769472 | tf_op jit(solution)/shard_map/all_gather | solution.py:453
  8.2 104.6 %all-gather.7.cloned.1.call-start = ((), (), s32[]{:S(2)}) async-start(), calls=%async_computation.1 | async-start | bytes 5947392 | tf_op jit(solution)/shard_map/all_gather | solution.py:459
  9.5 9.0 %collective-permute-start = (f32[12,32,128]{2,1,0:T(8,128)S(1)}, f32[12,32,128]{2,1,0:T(8,128)S(1)}, u32[]{:S(2)}, u32[]{:S(2)}) collective-permute-start(f32[12,32,128]{2,1,0:T(8,128)S(1)} %get-tuple-element.39), channel_id=1, source_target_pairs={{0,128},{1,129},{2,130},{3,131},{4,132},{5,133},{6,134},{7,135},{8... | collective-permute-start | bytes 589832 | tf_op jit(solution)/shard_map/ppermute | solution.py:419
  15.0 4.8 %collective-permute-start.1 = (f32[12,32,128]{2,1,0:T(8,128)S(1)}, f32[12,32,128]{2,1,0:T(8,128)S(1)}, u32[]{:S(2)}, u32[]{:S(2)}) collective-permute-start(f32[12,32,128]{2,1,0:T(8,128)S(1)} %get-tuple-element.38), channel_id=1, source_target_pairs={{0,192},{1,193},{2,194},{3,195},{4,196},{5,197},{6,198},{7,199},{8... | collective-permute-start | bytes 589832 | tf_op jit(solution)/shard_map/ppermute | solution.py:419
  16.3 6.4 %collective-permute-start.2 = (f32[12,32,128]{2,1,0:T(8,128)S(1)}, f32[12,32,128]{2,1,0:T(8,128)S(1)}, u32[]{:S(2)}, u32[]{:S(2)}) collective-permute-start(f32[12,32,128]{2,1,0:T(8,128)S(1)} %get-tuple-element.37), channel_id=1, source_target_pairs={{0,64},{1,65},{2,66},{3,67},{4,68},{5,69},{6,70},{7,71},{8,72},{9,... | collective-permute-start | bytes 589832 | tf_op jit(solution)/shard_map/ppermute | solution.py:419
  23.5 2.5 %collective-permute-start.3 = (f32[32,128]{1,0:T(8,128)S(1)}, f32[32,128]{1,0:T(8,128)S(1)}, u32[]{:S(2)}, u32[]{:S(2)}) collective-permute-start(f32[32,128]{1,0:T(8,128)S(1)} %get-tuple-element.43), channel_id=1, source_target_pairs={{0,8},{8,0},{1,9},{9,1},{2,10},{10,2},{3,11},{11,3},{4,12},{12,4},... | collective-permute-start | bytes 49160 | tf_op jit(solution)/shard_map/ppermute | solution.py:415
  26.0 14.3 %collective-permute-start.4 = (f32[2,32,128]{2,1,0:T(8,128)S(1)}, f32[2,32,128]{2,1,0:T(8,128)S(1)}, u32[]{:S(2)}, u32[]{:S(2)}) collective-permute-start(f32[2,32,128]{2,1,0:T(8,128)S(1)} %pad_maximum_fusion.6), channel_id=1, source_target_pairs={{0,1},{1,2},{2,3},{3,4},{4,5},{5,6},{6,7},{7,0},{8,15},{9,8},{10,9... | collective-permute-start | bytes 98312 | tf_op jit(solution)/shard_map/ppermute | solution.py:419
  31.6 8.7 %collective-permute-start.5 = (f32[2,32,128]{2,1,0:T(8,128)S(1)}, f32[2,32,128]{2,1,0:T(8,128)S(1)}, u32[]{:S(2)}, u32[]{:S(2)}) collective-permute-start(f32[2,32,128]{2,1,0:T(8,128)S(1)} %pad_maximum_fusion.6), channel_id=1, source_target_pairs={{0,2},{1,3},{2,4},{3,5},{4,6},{5,7},{6,0},{7,1},{8,14},{9,15},{10,... | collective-permute-start | bytes 98312 | tf_op jit(solution)/shard_map/ppermute | solution.py:419
  32.7 7.5 %collective-permute-start.6 = (f32[2,32,128]{2,1,0:T(8,128)S(1)}, f32[2,32,128]{2,1,0:T(8,128)S(1)}, u32[]{:S(2)}, u32[]{:S(2)}) collective-permute-start(f32[2,32,128]{2,1,0:T(8,128)S(1)} %pad_maximum_fusion.6), channel_id=1, source_target_pairs={{0,3},{1,4},{2,5},{3,6},{4,7},{5,0},{6,1},{7,2},{8,13},{9,14},{10,... | collective-permute-start | bytes 98312 | tf_op jit(solution)/shard_map/ppermute | solution.py:419
  33.2 7.1 %collective-permute-start.7 = (f32[32,128]{1,0:T(8,128)S(1)}, f32[32,128]{1,0:T(8,128)S(1)}, u32[]{:S(2)}, u32[]{:S(2)}) collective-permute-start(f32[32,128]{1,0:T(8,128)S(1)} %get-tuple-element.43), channel_id=1, source_target_pairs={{0,4},{1,5},{2,6},{3,7},{4,0},{5,1},{6,2},{7,3},{8,12},{9,13},{10,... | collective-permute-start | bytes 49160 | tf_op jit(solution)/shard_map/ppermute | solution.py:419
  40.3 3.9 %collective-permute-start.8 = (f32[3,32,128]{2,1,0:T(8,128)S(1)}, f32[3,32,128]{2,1,0:T(8,128)S(1)}, u32[]{:S(2)}, u32[]{:S(2)}) collective-permute-start(f32[3,32,128]{2,1,0:T(8,128)S(1)} %pad_maximum_fusion.4), channel_id=1, source_target_pairs={{0,8},{8,0},{1,9},{9,1},{2,10},{10,2},{3,11},{11,3},{4,12},{12,4},... | collective-permute-start | bytes 147464 | tf_op jit(solution)/shard_map/ppermute | solution.py:415
  44.4 6.4 %collective-permute-start.9 = (f32[8,32,128]{2,1,0:T(8,128)S(1)}, f32[8,32,128]{2,1,0:T(8,128)S(1)}, u32[]{:S(2)}, u32[]{:S(2)}) collective-permute-start(f32[8,32,128]{2,1,0:T(8,128)S(1)} %constant_dynamic-slice_fusion.2), channel_id=1, source_target_pairs={{0,16},{16,32},{32,48},{48,0},{1,17},{17,33},{33,49},{49,1},{2,18}... | collective-permute-start | bytes 393224 | tf_op jit(solution)/shard_map/ppermute | solution.py:419
  45.8 8.7 %collective-permute-start.10 = (f32[8,32,128]{2,1,0:T(8,128)S(1)}, f32[8,32,128]{2,1,0:T(8,128)S(1)}, u32[]{:S(2)}, u32[]{:S(2)}) collective-permute-start(f32[8,32,128]{2,1,0:T(8,128)S(1)} %constant_dynamic-slice_fusion.2), channel_id=1, source_target_pairs={{0,32},{16,48},{32,0},{48,16},{1,33},{17,49},{33,1},{49,17},{2,34}... | collective-permute-start | bytes 393224 | tf_op jit(solution)/shard_map/ppermute | solution.py:419
  48.5 6.1 %collective-permute-start.11 = (f32[8,32,128]{2,1,0:T(8,128)S(1)}, f32[8,32,128]{2,1,0:T(8,128)S(1)}, u32[]{:S(2)}, u32[]{:S(2)}) collective-permute-start(f32[8,32,128]{2,1,0:T(8,128)S(1)} %constant_dynamic-slice_fusion.2), channel_id=1, source_target_pairs={{0,48},{16,0},{32,16},{48,32},{1,49},{17,1},{33,17},{49,33},{2,50}... | collective-permute-start | bytes 393224 | tf_op jit(solution)/shard_map/ppermute | solution.py:419
  54.6 5.1 %collective-permute-start.12 = (f32[2,4,32,128]{3,2,1,0:T(8,128)S(1)}, f32[2,4,32,128]{3,2,1,0:T(8,128)S(1)}, u32[]{:S(2)}, u32[]{:S(2)}) collective-permute-start(f32[2,4,32,128]{3,2,1,0:T(8,128)S(1)} %get-tuple-element.46), channel_id=1, source_target_pairs={{0,64},{64,128},{128,192},{192,0},{1,65},{65,129},{129,193},{193,1... | collective-permute-start | bytes 393224 | tf_op jit(solution)/shard_map/ppermute | solution.py:419
  57.1 5.4 %collective-permute-start.13 = (f32[2,4,32,128]{3,2,1,0:T(8,128)S(1)}, f32[2,4,32,128]{3,2,1,0:T(8,128)S(1)}, u32[]{:S(2)}, u32[]{:S(2)}) collective-permute-start(f32[2,4,32,128]{3,2,1,0:T(8,128)S(1)} %get-tuple-element.46), channel_id=1, source_target_pairs={{0,128},{64,192},{128,0},{192,64},{1,129},{65,193},{129,1},{193,65... | collective-permute-start | bytes 393224 | tf_op jit(solution)/shard_map/ppermute | solution.py:419
  57.1 6.0 %collective-permute-start.14 = (f32[2,4,32,128]{3,2,1,0:T(8,128)S(1)}, f32[2,4,32,128]{3,2,1,0:T(8,128)S(1)}, u32[]{:S(2)}, u32[]{:S(2)}) collective-permute-start(f32[2,4,32,128]{3,2,1,0:T(8,128)S(1)} %get-tuple-element.46), channel_id=1, source_target_pairs={{0,192},{64,0},{128,64},{192,128},{1,193},{65,1},{129,65},{193,129... | collective-permute-start | bytes 393224 | tf_op jit(solution)/shard_map/ppermute | solution.py:419
  63.2 7.3 %collective-permute-start.15 = (f32[4,2,4,32,128]{4,3,2,1,0:T(8,128)S(1)}, f32[4,2,4,32,128]{4,3,2,1,0:T(8,128)S(1)}, u32[]{:S(2)}, u32[]{:S(2)}) collective-permute-start(f32[4,2,4,32,128]{4,3,2,1,0:T(8,128)S(1)} %pad_maximum_fusion.2.near_ref), channel_id=1, source_target_pairs={{0,8},{8,0},{1,9},{9,1},{2,10},{10,2},{3,11},{11,3},{4,12},{12,4},... | collective-permute-start | bytes 1572872 | tf_op jit(solution)/shard_map/ppermute | solution.py:415
  65.5 22.4 %copy-start.2 = (s32[5]{0:T(128)}, s32[5]{0:T(128)S(1)}, u32[]{:S(2)}) copy-start(s32[5]{0:T(128)S(1)} %stack.85.ids_ref) | copy-start | bytes 64
  65.5 22.4 %copy-start.3 = (f32[24,128,128]{2,1,0:T(8,128)S(1)}, f32[24,128,128]{2,1,0:T(8,128)}, u32[]{:S(2)}) copy-start(f32[24,128,128]{2,1,0:T(8,128)} %all-gather.5.cloned.1.call-done) | copy-start | bytes 4718596
  65.5 18.7 %collective-permute-start.16 = (f32[4,4,32,128]{3,2,1,0:T(8,128)S(1)}, f32[4,4,32,128]{3,2,1,0:T(8,128)S(1)}, u32[]{:S(2)}, u32[]{:S(2)}) collective-permute-start(f32[4,4,32,128]{3,2,1,0:T(8,128)S(1)} %slice.76), channel_id=1, source_target_pairs={{0,64},{64,128},{128,192},{192,0},{1,65},{65,129},{129,193},{193,1... | collective-permute-start | bytes 786440 | tf_op jit(solution)/shard_map/ppermute | solution.py:419
  67.3 17.2 %collective-permute-start.17 = (f32[4,4,32,128]{3,2,1,0:T(8,128)S(1)}, f32[4,4,32,128]{3,2,1,0:T(8,128)S(1)}, u32[]{:S(2)}, u32[]{:S(2)}) collective-permute-start(f32[4,4,32,128]{3,2,1,0:T(8,128)S(1)} %slice.76), channel_id=1, source_target_pairs={{0,128},{64,192},{128,0},{192,64},{1,129},{65,193},{129,1},{193,65... | collective-permute-start | bytes 786440 | tf_op jit(solution)/shard_map/ppermute | solution.py:419
  69.6 15.0 %collective-permute-start.18 = (f32[4,4,32,128]{3,2,1,0:T(8,128)S(1)}, f32[4,4,32,128]{3,2,1,0:T(8,128)S(1)}, u32[]{:S(2)}, u32[]{:S(2)}) collective-permute-start(f32[4,4,32,128]{3,2,1,0:T(8,128)S(1)} %slice.76), channel_id=1, source_target_pairs={{0,192},{64,0},{128,64},{192,128},{1,193},{65,1},{129,65},{193,129... | collective-permute-start | bytes 786440 | tf_op jit(solution)/shard_map/ppermute | solution.py:419
  84.6 3.3 %collective-permute-start.19 = (f32[4,4,4,32,128]{4,3,2,1,0:T(8,128)S(1)}, f32[4,4,4,32,128]{4,3,2,1,0:T(8,128)S(1)}, u32[]{:S(2)}, u32[]{:S(2)}) collective-permute-start(f32[4,4,4,32,128]{4,3,2,1,0:T(8,128)S(1)} %pad_maximum_fusion.near_ref), channel_id=1, source_target_pairs={{0,8},{8,0},{1,9},{9,1},{2,10},{10,2},{3,11},{11,3},{4,12},{12,4},... | collective-permute-start | bytes 3145736 | tf_op jit(solution)/shard_map/ppermute | solution.py:415
  109.6 1.2 copy-start
  110.7 0.7 copy-start.1
Sparse Core Ops, SparseCore 0:
  9.1 40.7 all-gather.4
  52.5 60.2 all-gather.6

commit v9 on v8

--- a/solution.py
+++ b/solution.py
@@ -103,7 +103,7 @@
             g = spread_row(cols[j + 1][q0], i)
             d = spread_row(cols[j + 1][q0], i + 1)
             first = 1.0 / p
-            second = p * (1.0 / (p * d - g * g))
+            second = 1.0 / (d - g * first * g)
             eliminate(j, first)
             eliminate(j + 1, second)
         for q in range(2):

time: 128 us -> 128 us (level)
  transfers between devices with their start and end apart: 22 -> 22, of which waited for: 14 -> 13; matrix products, arithmetic and copies ran while one was open for 2% -> 2% of each run, Pallas kernels for 28% -> 28%
where the time goes in v9:
time: 128 us
  Pallas kernels  44.3 us (35%)
  starting transfers between devices  42.8 us (33%)
  waiting for transfers between devices  21 us (16%)
  between operations  13.7 us (11%)
  local copies, waits for them, and re-layouts  5.56 us (4%)
    ppermute x16, starting transfers between devices, send(): return lax.ppermute(x, axis, pairs)  34.9 us
    pallas_call x1, Pallas kernels, second(): pl.pallas_call(second_kernel, out_shape=[jax.ShapeDtypeStruct((2, rows, W...  22 us
    ppermute x16, waiting for transfers between devices, send(): return lax.ppermute(x, axis, pairs)  16.2 us
    pallas_call x1, Pallas kernels, first(): pl.pallas_call(first_kernel, out_shape=jax.ShapeDtypeStruct(FACTOR, jnp.f...  14.2 us
    pallas_call x1, Pallas kernels, update(): pl.pallas_call(update_kernel, grid=(columns // n,), out_shape=jax.ShapeDt...  8.12 us
    ppermute x4, starting transfers between devices, swap(): return lax.ppermute(x, 'k', [(0, 1), (1, 0)])  7.83 us
    ppermute x4, waiting for transfers between devices, swap(): return lax.ppermute(x, 'k', [(0, 1), (1, 0)])  4.01 us
  transfers between devices with their start and end apart: 22, of which 13 were waited for; matrix products, arithmetic and copies ran while one was open for 2% of the time, Pallas kernels for 28%

profile of v9, /device:TPU:1, one launch (start us, length us, event | category | flops | bytes accessed | tf_op | source)
XLA Modules:
  0.0 127.6 jit_solution(12279270325571485996)
XLA Ops:
  6.5 1.6 %slice_bitcast_fusion.4 = f32[3,128,128]{2,1,0:T(8,128)} fusion(f32[3,12,128,128]{3,2,1,0:T(8,128)} %bitcast.59), kind=kLoop, calls=%fused_computation.10 | loop fusion | bytes 393216 | tf_op jit(solution)/shard_map/squeeze | solution.py:452
  8.2 1.2 slice.54
  9.5 5.5 %collective-permute-start = (f32[12,32,128]{2,1,0:T(8,128)S(1)}, f32[12,32,128]{2,1,0:T(8,128)S(1)}, u32[]{:S(2)}, u32[]{:S(2)}) collective-permute-start(f32[12,32,128]{2,1,0:T(8,128)S(1)} %get-tuple-element.39), channel_id=1, source_target_pairs={{0,128},{1,129},{2,130},{3,131},{4,132},{5,133},{6,134},{7,135},{8... | collective-permute-start | bytes 589832 | tf_op jit(solution)/shard_map/ppermute | solution.py:419
  15.0 1.3 %collective-permute-start.1 = (f32[12,32,128]{2,1,0:T(8,128)S(1)}, f32[12,32,128]{2,1,0:T(8,128)S(1)}, u32[]{:S(2)}, u32[]{:S(2)}) collective-permute-start(f32[12,32,128]{2,1,0:T(8,128)S(1)} %get-tuple-element.38), channel_id=1, source_target_pairs={{0,192},{1,193},{2,194},{3,195},{4,196},{5,197},{6,198},{7,199},{8... | collective-permute-start | bytes 589832 | tf_op jit(solution)/shard_map/ppermute | solution.py:419
  16.3 1.3 %collective-permute-start.2 = (f32[12,32,128]{2,1,0:T(8,128)S(1)}, f32[12,32,128]{2,1,0:T(8,128)S(1)}, u32[]{:S(2)}, u32[]{:S(2)}) collective-permute-start(f32[12,32,128]{2,1,0:T(8,128)S(1)} %get-tuple-element.37), channel_id=1, source_target_pairs={{0,64},{1,65},{2,66},{3,67},{4,68},{5,69},{6,70},{7,71},{8,72},{9,... | collective-permute-start | bytes 589832 | tf_op jit(solution)/shard_map/ppermute | solution.py:419
  17.6 0.9 collective-permute-done
  18.5 1.3 %collective-permute-done.1 = f32[12,32,128]{2,1,0:T(8,128)S(1)} collective-permute-done((f32[12,32,128]{2,1,0:T(8,128)S(1)}, f32[12,32,128]{2,1,0:T(8,128)S(1)}, u32[]{:S(2)}, u32[]{:S(2)}) %collective-permute-start.1) | collective-permute-done | bytes 196640 | tf_op jit(solution)/shard_map/ppermute | solution.py:419
  19.8 2.9 %collective-permute-done.2 = f32[12,32,128]{2,1,0:T(8,128)S(1)} collective-permute-done((f32[12,32,128]{2,1,0:T(8,128)S(1)}, f32[12,32,128]{2,1,0:T(8,128)S(1)}, u32[]{:S(2)}, u32[]{:S(2)}) %collective-permute-start.2) | collective-permute-done | bytes 196640 | tf_op jit(solution)/shard_map/ppermute | solution.py:419
  23.5 1.6 %collective-permute-start.3 = (f32[32,128]{1,0:T(8,128)S(1)}, f32[32,128]{1,0:T(8,128)S(1)}, u32[]{:S(2)}, u32[]{:S(2)}) collective-permute-start(f32[32,128]{1,0:T(8,128)S(1)} %get-tuple-element.43), channel_id=1, source_target_pairs={{0,8},{8,0},{1,9},{9,1},{2,10},{10,2},{3,11},{11,3},{4,12},{12,4},... | collective-permute-start | bytes 49160 | tf_op jit(solution)/shard_map/ppermute | solution.py:415
  26.0 5.6 %collective-permute-start.4 = (f32[2,32,128]{2,1,0:T(8,128)S(1)}, f32[2,32,128]{2,1,0:T(8,128)S(1)}, u32[]{:S(2)}, u32[]{:S(2)}) collective-permute-start(f32[2,32,128]{2,1,0:T(8,128)S(1)} %pad_maximum_fusion.6), channel_id=1, source_target_pairs={{0,1},{1,2},{2,3},{3,4},{4,5},{5,6},{6,7},{7,0},{8,15},{9,8},{10,9... | collective-permute-start | bytes 98312 | tf_op jit(solution)/shard_map/ppermute | solution.py:419
  31.6 1.2 collective-permute-start.5
  33.2 4.5 %collective-permute-start.7 = (f32[32,128]{1,0:T(8,128)S(1)}, f32[32,128]{1,0:T(8,128)S(1)}, u32[]{:S(2)}, u32[]{:S(2)}) collective-permute-start(f32[32,128]{1,0:T(8,128)S(1)} %get-tuple-element.43), channel_id=1, source_target_pairs={{0,4},{1,5},{2,6},{3,7},{4,0},{5,1},{6,2},{7,3},{8,12},{9,13},{10,... | collective-permute-start | bytes 49160 | tf_op jit(solution)/shard_map/ppermute | solution.py:419
  37.7 2.6 %collective-permute-done.7 = f32[32,128]{1,0:T(8,128)S(1)} collective-permute-done((f32[32,128]{1,0:T(8,128)S(1)}, f32[32,128]{1,0:T(8,128)S(1)}, u32[]{:S(2)}, u32[]{:S(2)}) %collective-permute-start.7) | collective-permute-done | bytes 16416 | tf_op jit(solution)/shard_map/ppermute | solution.py:419
  40.3 3.0 %collective-permute-start.8 = (f32[3,32,128]{2,1,0:T(8,128)S(1)}, f32[3,32,128]{2,1,0:T(8,128)S(1)}, u32[]{:S(2)}, u32[]{:S(2)}) collective-permute-start(f32[3,32,128]{2,1,0:T(8,128)S(1)} %pad_maximum_fusion.4), channel_id=1, source_target_pairs={{0,8},{8,0},{1,9},{9,1},{2,10},{10,2},{3,11},{11,3},{4,12},{12,4},... | collective-permute-start | bytes 147464 | tf_op jit(solution)/shard_map/ppermute | solution.py:415
  43.4 0.9 collective-permute-done.8
  44.4 1.5 %collective-permute-start.9 = (f32[8,32,128]{2,1,0:T(8,128)S(1)}, f32[8,32,128]{2,1,0:T(8,128)S(1)}, u32[]{:S(2)}, u32[]{:S(2)}) collective-permute-start(f32[8,32,128]{2,1,0:T(8,128)S(1)} %constant_dynamic-slice_fusion.2), channel_id=1, source_target_pairs={{0,16},{16,32},{32,48},{48,0},{1,17},{17,33},{33,49},{49,1},{2,18}... | collective-permute-start | bytes 393224 | tf_op jit(solution)/shard_map/ppermute | solution.py:419
  45.8 2.6 %collective-permute-start.10 = (f32[8,32,128]{2,1,0:T(8,128)S(1)}, f32[8,32,128]{2,1,0:T(8,128)S(1)}, u32[]{:S(2)}, u32[]{:S(2)}) collective-permute-start(f32[8,32,128]{2,1,0:T(8,128)S(1)} %constant_dynamic-slice_fusion.2), channel_id=1, source_target_pairs={{0,32},{16,48},{32,0},{48,16},{1,33},{17,49},{33,1},{49,17},{2,34}... | collective-permute-start | bytes 393224 | tf_op jit(solution)/shard_map/ppermute | solution.py:419
  48.5 1.1 collective-permute-start.11
  49.5 1.2 collective-permute-done.9
  50.7 3.8 %collective-permute-done.10 = f32[8,32,128]{2,1,0:T(8,128)S(1)} collective-permute-done((f32[8,32,128]{2,1,0:T(8,128)S(1)}, f32[8,32,128]{2,1,0:T(8,128)S(1)}, u32[]{:S(2)}, u32[]{:S(2)}) %collective-permute-start.10) | collective-permute-done | bytes 131104 | tf_op jit(solution)/shard_map/ppermute | solution.py:419
  54.6 2.5 %collective-permute-start.12 = (f32[2,4,32,128]{3,2,1,0:T(8,128)S(1)}, f32[2,4,32,128]{3,2,1,0:T(8,128)S(1)}, u32[]{:S(2)}, u32[]{:S(2)}) collective-permute-start(f32[2,4,32,128]{3,2,1,0:T(8,128)S(1)} %get-tuple-element.46), channel_id=1, source_target_pairs={{0,64},{64,128},{128,192},{192,0},{1,65},{65,129},{129,193},{193,1... | collective-permute-start | bytes 393224 | tf_op jit(solution)/shard_map/ppermute | solution.py:419
  57.1 2.5 %collective-permute-start.14 = (f32[2,4,32,128]{3,2,1,0:T(8,128)S(1)}, f32[2,4,32,128]{3,2,1,0:T(8,128)S(1)}, u32[]{:S(2)}, u32[]{:S(2)}) collective-permute-start(f32[2,4,32,128]{3,2,1,0:T(8,128)S(1)} %get-tuple-element.46), channel_id=1, source_target_pairs={{0,192},{64,0},{128,64},{192,128},{1,193},{65,1},{129,65},{193,129... | collective-permute-start | bytes 393224 | tf_op jit(solution)/shard_map/ppermute | solution.py:419
  59.7 2.8 %collective-permute-done.13 = f32[2,4,32,128]{3,2,1,0:T(8,128)S(1)} collective-permute-done((f32[2,4,32,128]{3,2,1,0:T(8,128)S(1)}, f32[2,4,32,128]{3,2,1,0:T(8,128)S(1)}, u32[]{:S(2)}, u32[]{:S(2)}) %collective-permute-start.13) | collective-permute-done | bytes 131104 | tf_op jit(solution)/shard_map/ppermute | solution.py:419
  63.2 2.2 %collective-permute-start.15 = (f32[4,2,4,32,128]{4,3,2,1,0:T(8,128)S(1)}, f32[4,2,4,32,128]{4,3,2,1,0:T(8,128)S(1)}, u32[]{:S(2)}, u32[]{:S(2)}) collective-permute-start(f32[4,2,4,32,128]{4,3,2,1,0:T(8,128)S(1)} %pad_maximum_fusion.2.near_ref), channel_id=1, source_target_pairs={{0,8},{8,0},{1,9},{9,1},{2,10},{10,2},{3,11},{11,3},{4,12},{12,4},... | collective-permute-start | bytes 1572872 | tf_op jit(solution)/shard_map/ppermute | solution.py:415
  65.5 1.8 %collective-permute-start.16 = (f32[4,4,32,128]{3,2,1,0:T(8,128)S(1)}, f32[4,4,32,128]{3,2,1,0:T(8,128)S(1)}, u32[]{:S(2)}, u32[]{:S(2)}) collective-permute-start(f32[4,4,32,128]{3,2,1,0:T(8,128)S(1)} %slice.76), channel_id=1, source_target_pairs={{0,64},{64,128},{128,192},{192,0},{1,65},{65,129},{129,193},{193,1... | collective-permute-start | bytes 786440 | tf_op jit(solution)/shard_map/ppermute | solution.py:419
  67.3 2.3 %collective-permute-start.17 = (f32[4,4,32,128]{3,2,1,0:T(8,128)S(1)}, f32[4,4,32,128]{3,2,1,0:T(8,128)S(1)}, u32[]{:S(2)}, u32[]{:S(2)}) collective-permute-start(f32[4,4,32,128]{3,2,1,0:T(8,128)S(1)} %slice.76), channel_id=1, source_target_pairs={{0,128},{64,192},{128,0},{192,64},{1,129},{65,193},{129,1},{193,65... | collective-permute-start | bytes 786440 | tf_op jit(solution)/shard_map/ppermute | solution.py:419
  70.4 14.2 %first.1.w0_ref = f32[768,512]{1,0:T(8,128)S(1)} custom-call(s32[5]{0:T(128)S(1)} %stack.85.ids_ref, f32[4,2,4,32,128]{4,3,2,1,0:T(8,128)S(1)} %pad_maximum_fusion.2.near_ref, f32[4,2,4,32,128]{4,3,2,1,0:T(8,128)S(1)} %collective-permute-done.15.far_ref), custom_call_target="tpu_custom_call" | custom-call | flops 8589934592 | bytes 4194304 | tf_op jit(solution)/shard_map/first/pallas_call | solution.py:209
  84.8 1.0 collective-permute-start.19
  85.7 2.3 %collective-permute-done.19.far_ref = f32[4,4,4,32,128]{4,3,2,1,0:T(8,128)S(1)} collective-permute-done((f32[4,4,4,32,128]{4,3,2,1,0:T(8,128)S(1)}, f32[4,4,4,32,128]{4,3,2,1,0:T(8,128)S(1)}, u32[]{:S(2)}, u32[]{:S(2)}) %collective-permute-start.19) | collective-permute-done | bytes 1048608 | tf_op jit(solution)/shard_map/ppermute | solution.py:415
  88.0 22.0 %second.1 = (bf16[2,384,1024]{2,1,0:T(8,128)(2,1)S(1)}, f32[3,128,128]{2,1,0:T(8,128)S(1)}) custom-call(s32[5]{0:T(128)S(1)} %stack.85.ids_ref, f32[768,512]{1,0:T(8,128)S(1)} %first.1.w0_ref, f32[4,4,4,32,128]{4,3,2,1,0:T(8,128)S(1)} %pad_maximum_fusion.near_ref, f32[4,4,4,32,128]{4,3,2,1,0:T(8,128)S(1)} %collective-permute-done.19.far_ref, ...), custom_call_target="tpu_custom_call" | custom-call | flops 17179869184 | bytes 8388608 | tf_op jit(solution)/shard_map/second/pallas_call | solution.py:340
  110.1 1.1 copy-done
  112.6 8.1 %update.1 = f32[3,12,128,128]{3,2,1,0:T(8,128)} custom-call(s32[5]{0:T(128)} %copy-done.2, bf16[2,384,1024]{2,1,0:T(8,128)(2,1)} %copy-done, f32[3,128,128]{2,1,0:T(8,128)} %copy-done.1, f32[4,8,11,32,128]{4,3,2,1,0:T(8,128)} %bitcast.55, f32[4,8,11,32,128]{4,3,2,1,0:T(8,128)} %bitcast.56, f32[4,8,11,32,128]{4,3,2,1,0:T(8,128)} %bitcast.57, ...), custom_call_target="tpu_custom_call" | custom-call | tf_op jit(solution)/shard_map/update/pallas_call | solution.py:403
  (51 shorter events, 5.5 us)
Async XLA Ops:
  6.5 56.6 %all-gather.5.cloned.1.call-start = ((), (), s32[]{:S(2)}) async-start(), calls=%async_computation | async-start | bytes 1769472 | tf_op jit(solution)/shard_map/all_gather | solution.py:453
  8.2 104.4 %all-gather.7.cloned.1.call-start = ((), (), s32[]{:S(2)}) async-start(), calls=%async_computation.1 | async-start | bytes 5947392 | tf_op jit(solution)/shard_map/all_gather | solution.py:459
  9.5 9.0 %collective-permute-start = (f32[12,32,128]{2,1,0:T(8,128)S(1)}, f32[12,32,128]{2,1,0:T(8,128)S(1)}, u32[]{:S(2)}, u32[]{:S(2)}) collective-permute-start(f32[12,32,128]{2,1,0:T(8,128)S(1)} %get-tuple-element.39), channel_id=1, source_target_pairs={{0,128},{1,129},{2,130},{3,131},{4,132},{5,133},{6,134},{7,135},{8... | collective-permute-start | bytes 589832 | tf_op jit(solution)/shard_map/ppermute | solution.py:419
  15.0 4.8 %collective-permute-start.1 = (f32[12,32,128]{2,1,0:T(8,128)S(1)}, f32[12,32,128]{2,1,0:T(8,128)S(1)}, u32[]{:S(2)}, u32[]{:S(2)}) collective-permute-start(f32[12,32,128]{2,1,0:T(8,128)S(1)} %get-tuple-element.38), channel_id=1, source_target_pairs={{0,192},{1,193},{2,194},{3,195},{4,196},{5,197},{6,198},{7,199},{8... | collective-permute-start | bytes 589832 | tf_op jit(solution)/shard_map/ppermute | solution.py:419
  16.3 6.4 %collective-permute-start.2 = (f32[12,32,128]{2,1,0:T(8,128)S(1)}, f32[12,32,128]{2,1,0:T(8,128)S(1)}, u32[]{:S(2)}, u32[]{:S(2)}) collective-permute-start(f32[12,32,128]{2,1,0:T(8,128)S(1)} %get-tuple-element.37), channel_id=1, source_target_pairs={{0,64},{1,65},{2,66},{3,67},{4,68},{5,69},{6,70},{7,71},{8,72},{9,... | collective-permute-start | bytes 589832 | tf_op jit(solution)/shard_map/ppermute | solution.py:419
  23.5 2.5 %collective-permute-start.3 = (f32[32,128]{1,0:T(8,128)S(1)}, f32[32,128]{1,0:T(8,128)S(1)}, u32[]{:S(2)}, u32[]{:S(2)}) collective-permute-start(f32[32,128]{1,0:T(8,128)S(1)} %get-tuple-element.43), channel_id=1, source_target_pairs={{0,8},{8,0},{1,9},{9,1},{2,10},{10,2},{3,11},{11,3},{4,12},{12,4},... | collective-permute-start | bytes 49160 | tf_op jit(solution)/shard_map/ppermute | solution.py:415
  26.0 14.3 %collective-permute-start.4 = (f32[2,32,128]{2,1,0:T(8,128)S(1)}, f32[2,32,128]{2,1,0:T(8,128)S(1)}, u32[]{:S(2)}, u32[]{:S(2)}) collective-permute-start(f32[2,32,128]{2,1,0:T(8,128)S(1)} %pad_maximum_fusion.6), channel_id=1, source_target_pairs={{0,1},{1,2},{2,3},{3,4},{4,5},{5,6},{6,7},{7,0},{8,15},{9,8},{10,9... | collective-permute-start | bytes 98312 | tf_op jit(solution)/shard_map/ppermute | solution.py:419
  31.6 8.7 %collective-permute-start.5 = (f32[2,32,128]{2,1,0:T(8,128)S(1)}, f32[2,32,128]{2,1,0:T(8,128)S(1)}, u32[]{:S(2)}, u32[]{:S(2)}) collective-permute-start(f32[2,32,128]{2,1,0:T(8,128)S(1)} %pad_maximum_fusion.6), channel_id=1, source_target_pairs={{0,2},{1,3},{2,4},{3,5},{4,6},{5,7},{6,0},{7,1},{8,14},{9,15},{10,... | collective-permute-start | bytes 98312 | tf_op jit(solution)/shard_map/ppermute | solution.py:419
  32.7 7.5 %collective-permute-start.6 = (f32[2,32,128]{2,1,0:T(8,128)S(1)}, f32[2,32,128]{2,1,0:T(8,128)S(1)}, u32[]{:S(2)}, u32[]{:S(2)}) collective-permute-start(f32[2,32,128]{2,1,0:T(8,128)S(1)} %pad_maximum_fusion.6), channel_id=1, source_target_pairs={{0,3},{1,4},{2,5},{3,6},{4,7},{5,0},{6,1},{7,2},{8,13},{9,14},{10,... | collective-permute-start | bytes 98312 | tf_op jit(solution)/shard_map/ppermute | solution.py:419
  33.2 7.1 %collective-permute-start.7 = (f32[32,128]{1,0:T(8,128)S(1)}, f32[32,128]{1,0:T(8,128)S(1)}, u32[]{:S(2)}, u32[]{:S(2)}) collective-permute-start(f32[32,128]{1,0:T(8,128)S(1)} %get-tuple-element.43), channel_id=1, source_target_pairs={{0,4},{1,5},{2,6},{3,7},{4,0},{5,1},{6,2},{7,3},{8,12},{9,13},{10,... | collective-permute-start | bytes 49160 | tf_op jit(solution)/shard_map/ppermute | solution.py:419
  40.3 3.9 %collective-permute-start.8 = (f32[3,32,128]{2,1,0:T(8,128)S(1)}, f32[3,32,128]{2,1,0:T(8,128)S(1)}, u32[]{:S(2)}, u32[]{:S(2)}) collective-permute-start(f32[3,32,128]{2,1,0:T(8,128)S(1)} %pad_maximum_fusion.4), channel_id=1, source_target_pairs={{0,8},{8,0},{1,9},{9,1},{2,10},{10,2},{3,11},{11,3},{4,12},{12,4},... | collective-permute-start | bytes 147464 | tf_op jit(solution)/shard_map/ppermute | solution.py:415
  44.4 6.4 %collective-permute-start.9 = (f32[8,32,128]{2,1,0:T(8,128)S(1)}, f32[8,32,128]{2,1,0:T(8,128)S(1)}, u32[]{:S(2)}, u32[]{:S(2)}) collective-permute-start(f32[8,32,128]{2,1,0:T(8,128)S(1)} %constant_dynamic-slice_fusion.2), channel_id=1, source_target_pairs={{0,16},{16,32},{32,48},{48,0},{1,17},{17,33},{33,49},{49,1},{2,18}... | collective-permute-start | bytes 393224 | tf_op jit(solution)/shard_map/ppermute | solution.py:419
  45.8 8.7 %collective-permute-start.10 = (f32[8,32,128]{2,1,0:T(8,128)S(1)}, f32[8,32,128]{2,1,0:T(8,128)S(1)}, u32[]{:S(2)}, u32[]{:S(2)}) collective-permute-start(f32[8,32,128]{2,1,0:T(8,128)S(1)} %constant_dynamic-slice_fusion.2), channel_id=1, source_target_pairs={{0,32},{16,48},{32,0},{48,16},{1,33},{17,49},{33,1},{49,17},{2,34}... | collective-permute-start | bytes 393224 | tf_op jit(solution)/shard_map/ppermute | solution.py:419
  48.5 6.1 %collective-permute-start.11 = (f32[8,32,128]{2,1,0:T(8,128)S(1)}, f32[8,32,128]{2,1,0:T(8,128)S(1)}, u32[]{:S(2)}, u32[]{:S(2)}) collective-permute-start(f32[8,32,128]{2,1,0:T(8,128)S(1)} %constant_dynamic-slice_fusion.2), channel_id=1, source_target_pairs={{0,48},{16,0},{32,16},{48,32},{1,49},{17,1},{33,17},{49,33},{2,50}... | collective-permute-start | bytes 393224 | tf_op jit(solution)/shard_map/ppermute | solution.py:419
  54.6 5.1 %collective-permute-start.12 = (f32[2,4,32,128]{3,2,1,0:T(8,128)S(1)}, f32[2,4,32,128]{3,2,1,0:T(8,128)S(1)}, u32[]{:S(2)}, u32[]{:S(2)}) collective-permute-start(f32[2,4,32,128]{3,2,1,0:T(8,128)S(1)} %get-tuple-element.46), channel_id=1, source_target_pairs={{0,64},{64,128},{128,192},{192,0},{1,65},{65,129},{129,193},{193,1... | collective-permute-start | bytes 393224 | tf_op jit(solution)/shard_map/ppermute | solution.py:419
  57.1 5.4 %collective-permute-start.13 = (f32[2,4,32,128]{3,2,1,0:T(8,128)S(1)}, f32[2,4,32,128]{3,2,1,0:T(8,128)S(1)}, u32[]{:S(2)}, u32[]{:S(2)}) collective-permute-start(f32[2,4,32,128]{3,2,1,0:T(8,128)S(1)} %get-tuple-element.46), channel_id=1, source_target_pairs={{0,128},{64,192},{128,0},{192,64},{1,129},{65,193},{129,1},{193,65... | collective-permute-start | bytes 393224 | tf_op jit(solution)/shard_map/ppermute | solution.py:419
  57.1 6.0 %collective-permute-start.14 = (f32[2,4,32,128]{3,2,1,0:T(8,128)S(1)}, f32[2,4,32,128]{3,2,1,0:T(8,128)S(1)}, u32[]{:S(2)}, u32[]{:S(2)}) collective-permute-start(f32[2,4,32,128]{3,2,1,0:T(8,128)S(1)} %get-tuple-element.46), channel_id=1, source_target_pairs={{0,192},{64,0},{128,64},{192,128},{1,193},{65,1},{129,65},{193,129... | collective-permute-start | bytes 393224 | tf_op jit(solution)/shard_map/ppermute | solution.py:419
  63.2 7.3 %collective-permute-start.15 = (f32[4,2,4,32,128]{4,3,2,1,0:T(8,128)S(1)}, f32[4,2,4,32,128]{4,3,2,1,0:T(8,128)S(1)}, u32[]{:S(2)}, u32[]{:S(2)}) collective-permute-start(f32[4,2,4,32,128]{4,3,2,1,0:T(8,128)S(1)} %pad_maximum_fusion.2.near_ref), channel_id=1, source_target_pairs={{0,8},{8,0},{1,9},{9,1},{2,10},{10,2},{3,11},{11,3},{4,12},{12,4},... | collective-permute-start | bytes 1572872 | tf_op jit(solution)/shard_map/ppermute | solution.py:415
  65.5 22.6 %copy-start.2 = (s32[5]{0:T(128)}, s32[5]{0:T(128)S(1)}, u32[]{:S(2)}) copy-start(s32[5]{0:T(128)S(1)} %stack.85.ids_ref) | copy-start | bytes 64
  65.5 22.6 %copy-start.3 = (f32[24,128,128]{2,1,0:T(8,128)S(1)}, f32[24,128,128]{2,1,0:T(8,128)}, u32[]{:S(2)}) copy-start(f32[24,128,128]{2,1,0:T(8,128)} %all-gather.5.cloned.1.call-done) | copy-start | bytes 4718596
  65.5 19.2 %collective-permute-start.16 = (f32[4,4,32,128]{3,2,1,0:T(8,128)S(1)}, f32[4,4,32,128]{3,2,1,0:T(8,128)S(1)}, u32[]{:S(2)}, u32[]{:S(2)}) collective-permute-start(f32[4,4,32,128]{3,2,1,0:T(8,128)S(1)} %slice.76), channel_id=1, source_target_pairs={{0,64},{64,128},{128,192},{192,0},{1,65},{65,129},{129,193},{193,1... | collective-permute-start | bytes 786440 | tf_op jit(solution)/shard_map/ppermute | solution.py:419
  67.3 17.4 %collective-permute-start.17 = (f32[4,4,32,128]{3,2,1,0:T(8,128)S(1)}, f32[4,4,32,128]{3,2,1,0:T(8,128)S(1)}, u32[]{:S(2)}, u32[]{:S(2)}) collective-permute-start(f32[4,4,32,128]{3,2,1,0:T(8,128)S(1)} %slice.76), channel_id=1, source_target_pairs={{0,128},{64,192},{128,0},{192,64},{1,129},{65,193},{129,1},{193,65... | collective-permute-start | bytes 786440 | tf_op jit(solution)/shard_map/ppermute | solution.py:419
  69.6 15.1 %collective-permute-start.18 = (f32[4,4,32,128]{3,2,1,0:T(8,128)S(1)}, f32[4,4,32,128]{3,2,1,0:T(8,128)S(1)}, u32[]{:S(2)}, u32[]{:S(2)}) collective-permute-start(f32[4,4,32,128]{3,2,1,0:T(8,128)S(1)} %slice.76), channel_id=1, source_target_pairs={{0,192},{64,0},{128,64},{192,128},{1,193},{65,1},{129,65},{193,129... | collective-permute-start | bytes 786440 | tf_op jit(solution)/shard_map/ppermute | solution.py:419
  84.8 3.2 %collective-permute-start.19 = (f32[4,4,4,32,128]{4,3,2,1,0:T(8,128)S(1)}, f32[4,4,4,32,128]{4,3,2,1,0:T(8,128)S(1)}, u32[]{:S(2)}, u32[]{:S(2)}) collective-permute-start(f32[4,4,4,32,128]{4,3,2,1,0:T(8,128)S(1)} %pad_maximum_fusion.near_ref), channel_id=1, source_target_pairs={{0,8},{8,0},{1,9},{9,1},{2,10},{10,2},{3,11},{11,3},{4,12},{12,4},... | collective-permute-start | bytes 3145736 | tf_op jit(solution)/shard_map/ppermute | solution.py:415
  110.1 1.2 copy-start
  111.2 0.7 copy-start.1
Sparse Core Ops, SparseCore 0:
  9.1 40.7 all-gather.4
  52.5 60.0 all-gather.6

commit v10 on v9

--- a/solution.py
+++ b/solution.py
@@ -391,7 +391,7 @@
 
 def update(ids, t, c, right, kernel):
     tiles, columns = kernel.shape[:2]
-    n = 4
+    n = 6
     block = pl.BlockSpec((tiles, n, TILE, TILE), lambda j: (0, j, 0, 0))
 
     def piece(i):

time: 128 us -> 128 us (level)
  no operation moved by 1% of the time
where the time goes in v10:
time: 128 us; the launch traced here: 127 us
  Pallas kernels  44.2 us (35%)
  starting transfers between devices  42.8 us (33%)
  waiting for transfers between devices  21 us (16%)
  between operations  13.7 us (11%)
  local copies, waits for them, and re-layouts  5.56 us (4%)
    ppermute x16, starting transfers between devices, send(): return lax.ppermute(x, axis, pairs)  34.9 us
    pallas_call x1, Pallas kernels, second(): pl.pallas_call(second_kernel, out_shape=[jax.ShapeDtypeStruct((2, rows, W...  22 us
    ppermute x16, waiting for transfers between devices, send(): return lax.ppermute(x, axis, pairs)  16.2 us
    pallas_call x1, Pallas kernels, first(): pl.pallas_call(first_kernel, out_shape=jax.ShapeDtypeStruct(FACTOR, jnp.f...  14.2 us
    pallas_call x1, Pallas kernels, update(): pl.pallas_call(update_kernel, grid=(columns // n,), out_shape=jax.ShapeDt...  8 us
    ppermute x4, starting transfers between devices, swap(): return lax.ppermute(x, 'k', [(0, 1), (1, 0)])  7.83 us
    ppermute x4, waiting for transfers between devices, swap(): return lax.ppermute(x, 'k', [(0, 1), (1, 0)])  4.01 us
  transfers between devices with their start and end apart: 22, of which 13 were waited for; matrix products, arithmetic and copies ran while one was open for 2% of the time, Pallas kernels for 28%

profile of v10, /device:TPU:1, one launch (start us, length us, event | category | flops | bytes accessed | tf_op | source)
XLA Modules:
  0.0 127.4 jit_solution(407587866212887914)
XLA Ops:
  6.5 1.6 %slice_bitcast_fusion.4 = f32[3,128,128]{2,1,0:T(8,128)} fusion(f32[3,12,128,128]{3,2,1,0:T(8,128)} %bitcast.61), kind=kLoop, calls=%fused_computation.10 | loop fusion | bytes 393216 | tf_op jit(solution)/shard_map/squeeze | solution.py:452
  8.2 1.2 slice.54
  9.5 5.5 %collective-permute-start = (f32[12,32,128]{2,1,0:T(8,128)S(1)}, f32[12,32,128]{2,1,0:T(8,128)S(1)}, u32[]{:S(2)}, u32[]{:S(2)}) collective-permute-start(f32[12,32,128]{2,1,0:T(8,128)S(1)} %get-tuple-element.39), channel_id=1, source_target_pairs={{0,128},{1,129},{2,130},{3,131},{4,132},{5,133},{6,134},{7,135},{8... | collective-permute-start | bytes 589832 | tf_op jit(solution)/shard_map/ppermute | solution.py:419
  15.0 1.3 %collective-permute-start.1 = (f32[12,32,128]{2,1,0:T(8,128)S(1)}, f32[12,32,128]{2,1,0:T(8,128)S(1)}, u32[]{:S(2)}, u32[]{:S(2)}) collective-permute-start(f32[12,32,128]{2,1,0:T(8,128)S(1)} %get-tuple-element.38), channel_id=1, source_target_pairs={{0,192},{1,193},{2,194},{3,195},{4,196},{5,197},{6,198},{7,199},{8... | collective-permute-start | bytes 589832 | tf_op jit(solution)/shard_map/ppermute | solution.py:419
  16.3 1.3 %collective-permute-start.2 = (f32[12,32,128]{2,1,0:T(8,128)S(1)}, f32[12,32,128]{2,1,0:T(8,128)S(1)}, u32[]{:S(2)}, u32[]{:S(2)}) collective-permute-start(f32[12,32,128]{2,1,0:T(8,128)S(1)} %get-tuple-element.37), channel_id=1, source_target_pairs={{0,64},{1,65},{2,66},{3,67},{4,68},{5,69},{6,70},{7,71},{8,72},{9,... | collective-permute-start | bytes 589832 | tf_op jit(solution)/shard_map/ppermute | solution.py:419
  17.6 0.9 collective-permute-done
  18.5 1.3 %collective-permute-done.1 = f32[12,32,128]{2,1,0:T(8,128)S(1)} collective-permute-done((f32[12,32,128]{2,1,0:T(8,128)S(1)}, f32[12,32,128]{2,1,0:T(8,128)S(1)}, u32[]{:S(2)}, u32[]{:S(2)}) %collective-permute-start.1) | collective-permute-done | bytes 196640 | tf_op jit(solution)/shard_map/ppermute | solution.py:419
  19.8 2.9 %collective-permute-done.2 = f32[12,32,128]{2,1,0:T(8,128)S(1)} collective-permute-done((f32[12,32,128]{2,1,0:T(8,128)S(1)}, f32[12,32,128]{2,1,0:T(8,128)S(1)}, u32[]{:S(2)}, u32[]{:S(2)}) %collective-permute-start.2) | collective-permute-done | bytes 196640 | tf_op jit(solution)/shard_map/ppermute | solution.py:419
  23.5 1.6 %collective-permute-start.3 = (f32[32,128]{1,0:T(8,128)S(1)}, f32[32,128]{1,0:T(8,128)S(1)}, u32[]{:S(2)}, u32[]{:S(2)}) collective-permute-start(f32[32,128]{1,0:T(8,128)S(1)} %get-tuple-element.43), channel_id=1, source_target_pairs={{0,8},{8,0},{1,9},{9,1},{2,10},{10,2},{3,11},{11,3},{4,12},{12,4},... | collective-permute-start | bytes 49160 | tf_op jit(solution)/shard_map/ppermute | solution.py:415
  26.0 5.6 %collective-permute-start.4 = (f32[2,32,128]{2,1,0:T(8,128)S(1)}, f32[2,32,128]{2,1,0:T(8,128)S(1)}, u32[]{:S(2)}, u32[]{:S(2)}) collective-permute-start(f32[2,32,128]{2,1,0:T(8,128)S(1)} %pad_maximum_fusion.6), channel_id=1, source_target_pairs={{0,1},{1,2},{2,3},{3,4},{4,5},{5,6},{6,7},{7,0},{8,15},{9,8},{10,9... | collective-permute-start | bytes 98312 | tf_op jit(solution)/shard_map/ppermute | solution.py:419
  31.6 1.2 collective-permute-start.5
  33.2 4.5 %collective-permute-start.7 = (f32[32,128]{1,0:T(8,128)S(1)}, f32[32,128]{1,0:T(8,128)S(1)}, u32[]{:S(2)}, u32[]{:S(2)}) collective-permute-start(f32[32,128]{1,0:T(8,128)S(1)} %get-tuple-element.43), channel_id=1, source_target_pairs={{0,4},{1,5},{2,6},{3,7},{4,0},{5,1},{6,2},{7,3},{8,12},{9,13},{10,... | collective-permute-start | bytes 49160 | tf_op jit(solution)/shard_map/ppermute | solution.py:419
  37.7 2.6 %collective-permute-done.7 = f32[32,128]{1,0:T(8,128)S(1)} collective-permute-done((f32[32,128]{1,0:T(8,128)S(1)}, f32[32,128]{1,0:T(8,128)S(1)}, u32[]{:S(2)}, u32[]{:S(2)}) %collective-permute-start.7) | collective-permute-done | bytes 16416 | tf_op jit(solution)/shard_map/ppermute | solution.py:419
  40.3 3.0 %collective-permute-start.8 = (f32[3,32,128]{2,1,0:T(8,128)S(1)}, f32[3,32,128]{2,1,0:T(8,128)S(1)}, u32[]{:S(2)}, u32[]{:S(2)}) collective-permute-start(f32[3,32,128]{2,1,0:T(8,128)S(1)} %pad_maximum_fusion.4), channel_id=1, source_target_pairs={{0,8},{8,0},{1,9},{9,1},{2,10},{10,2},{3,11},{11,3},{4,12},{12,4},... | collective-permute-start | bytes 147464 | tf_op jit(solution)/shard_map/ppermute | solution.py:415
  43.4 0.9 collective-permute-done.8
  44.4 1.5 %collective-permute-start.9 = (f32[8,32,128]{2,1,0:T(8,128)S(1)}, f32[8,32,128]{2,1,0:T(8,128)S(1)}, u32[]{:S(2)}, u32[]{:S(2)}) collective-permute-start(f32[8,32,128]{2,1,0:T(8,128)S(1)} %constant_dynamic-slice_fusion.2), channel_id=1, source_target_pairs={{0,16},{16,32},{32,48},{48,0},{1,17},{17,33},{33,49},{49,1},{2,18}... | collective-permute-start | bytes 393224 | tf_op jit(solution)/shard_map/ppermute | solution.py:419
  45.8 2.6 %collective-permute-start.10 = (f32[8,32,128]{2,1,0:T(8,128)S(1)}, f32[8,32,128]{2,1,0:T(8,128)S(1)}, u32[]{:S(2)}, u32[]{:S(2)}) collective-permute-start(f32[8,32,128]{2,1,0:T(8,128)S(1)} %constant_dynamic-slice_fusion.2), channel_id=1, source_target_pairs={{0,32},{16,48},{32,0},{48,16},{1,33},{17,49},{33,1},{49,17},{2,34}... | collective-permute-start | bytes 393224 | tf_op jit(solution)/shard_map/ppermute | solution.py:419
  48.5 1.1 collective-permute-start.11
  49.5 1.2 collective-permute-done.9
  50.7 3.8 %collective-permute-done.10 = f32[8,32,128]{2,1,0:T(8,128)S(1)} collective-permute-done((f32[8,32,128]{2,1,0:T(8,128)S(1)}, f32[8,32,128]{2,1,0:T(8,128)S(1)}, u32[]{:S(2)}, u32[]{:S(2)}) %collective-permute-start.10) | collective-permute-done | bytes 131104 | tf_op jit(solution)/shard_map/ppermute | solution.py:419
  54.6 2.5 %collective-permute-start.12 = (f32[2,4,32,128]{3,2,1,0:T(8,128)S(1)}, f32[2,4,32,128]{3,2,1,0:T(8,128)S(1)}, u32[]{:S(2)}, u32[]{:S(2)}) collective-permute-start(f32[2,4,32,128]{3,2,1,0:T(8,128)S(1)} %get-tuple-element.46), channel_id=1, source_target_pairs={{0,64},{64,128},{128,192},{192,0},{1,65},{65,129},{129,193},{193,1... | collective-permute-start | bytes 393224 | tf_op jit(solution)/shard_map/ppermute | solution.py:419
  57.1 2.5 %collective-permute-start.14 = (f32[2,4,32,128]{3,2,1,0:T(8,128)S(1)}, f32[2,4,32,128]{3,2,1,0:T(8,128)S(1)}, u32[]{:S(2)}, u32[]{:S(2)}) collective-permute-start(f32[2,4,32,128]{3,2,1,0:T(8,128)S(1)} %get-tuple-element.46), channel_id=1, source_target_pairs={{0,192},{64,0},{128,64},{192,128},{1,193},{65,1},{129,65},{193,129... | collective-permute-start | bytes 393224 | tf_op jit(solution)/shard_map/ppermute | solution.py:419
  59.7 2.8 %collective-permute-done.13 = f32[2,4,32,128]{3,2,1,0:T(8,128)S(1)} collective-permute-done((f32[2,4,32,128]{3,2,1,0:T(8,128)S(1)}, f32[2,4,32,128]{3,2,1,0:T(8,128)S(1)}, u32[]{:S(2)}, u32[]{:S(2)}) %collective-permute-start.13) | collective-permute-done | bytes 131104 | tf_op jit(solution)/shard_map/ppermute | solution.py:419
  63.2 2.2 %collective-permute-start.15 = (f32[4,2,4,32,128]{4,3,2,1,0:T(8,128)S(1)}, f32[4,2,4,32,128]{4,3,2,1,0:T(8,128)S(1)}, u32[]{:S(2)}, u32[]{:S(2)}) collective-permute-start(f32[4,2,4,32,128]{4,3,2,1,0:T(8,128)S(1)} %pad_maximum_fusion.2.near_ref), channel_id=1, source_target_pairs={{0,8},{8,0},{1,9},{9,1},{2,10},{10,2},{3,11},{11,3},{4,12},{12,4},... | collective-permute-start | bytes 1572872 | tf_op jit(solution)/shard_map/ppermute | solution.py:415
  65.5 1.8 %collective-permute-start.16 = (f32[4,4,32,128]{3,2,1,0:T(8,128)S(1)}, f32[4,4,32,128]{3,2,1,0:T(8,128)S(1)}, u32[]{:S(2)}, u32[]{:S(2)}) collective-permute-start(f32[4,4,32,128]{3,2,1,0:T(8,128)S(1)} %slice.76), channel_id=1, source_target_pairs={{0,64},{64,128},{128,192},{192,0},{1,65},{65,129},{129,193},{193,1... | collective-permute-start | bytes 786440 | tf_op jit(solution)/shard_map/ppermute | solution.py:419
  67.3 2.3 %collective-permute-start.17 = (f32[4,4,32,128]{3,2,1,0:T(8,128)S(1)}, f32[4,4,32,128]{3,2,1,0:T(8,128)S(1)}, u32[]{:S(2)}, u32[]{:S(2)}) collective-permute-start(f32[4,4,32,128]{3,2,1,0:T(8,128)S(1)} %slice.76), channel_id=1, source_target_pairs={{0,128},{64,192},{128,0},{192,64},{1,129},{65,193},{129,1},{193,65... | collective-permute-start | bytes 786440 | tf_op jit(solution)/shard_map/ppermute | solution.py:419
  70.4 14.2 %first.1.w0_ref = f32[768,512]{1,0:T(8,128)S(1)} custom-call(s32[5]{0:T(128)S(1)} %stack.85.ids_ref, f32[4,2,4,32,128]{4,3,2,1,0:T(8,128)S(1)} %pad_maximum_fusion.2.near_ref, f32[4,2,4,32,128]{4,3,2,1,0:T(8,128)S(1)} %collective-permute-done.15.far_ref), custom_call_target="tpu_custom_call" | custom-call | flops 8589934592 | bytes 4194304 | tf_op jit(solution)/shard_map/first/pallas_call | solution.py:209
  84.8 1.0 collective-permute-start.19
  85.7 2.3 %collective-permute-done.19.far_ref = f32[4,4,4,32,128]{4,3,2,1,0:T(8,128)S(1)} collective-permute-done((f32[4,4,4,32,128]{4,3,2,1,0:T(8,128)S(1)}, f32[4,4,4,32,128]{4,3,2,1,0:T(8,128)S(1)}, u32[]{:S(2)}, u32[]{:S(2)}) %collective-permute-start.19) | collective-permute-done | bytes 1048608 | tf_op jit(solution)/shard_map/ppermute | solution.py:415
  88.0 22.0 %second.1 = (bf16[2,384,1024]{2,1,0:T(8,128)(2,1)S(1)}, f32[3,128,128]{2,1,0:T(8,128)S(1)}) custom-call(s32[5]{0:T(128)S(1)} %stack.85.ids_ref, f32[768,512]{1,0:T(8,128)S(1)} %first.1.w0_ref, f32[4,4,4,32,128]{4,3,2,1,0:T(8,128)S(1)} %pad_maximum_fusion.near_ref, f32[4,4,4,32,128]{4,3,2,1,0:T(8,128)S(1)} %collective-permute-done.19.far_ref, ...), custom_call_target="tpu_custom_call" | custom-call | flops 17179869184 | bytes 8388608 | tf_op jit(solution)/shard_map/second/pallas_call | solution.py:340
  110.1 1.1 copy-done
  112.6 8.0 %update.1 = f32[3,12,128,128]{3,2,1,0:T(8,128)} custom-call(s32[5]{0:T(128)} %copy-done.2, bf16[2,384,1024]{2,1,0:T(8,128)(2,1)} %copy-done, f32[3,128,128]{2,1,0:T(8,128)} %copy-done.1, f32[4,8,11,32,128]{4,3,2,1,0:T(8,128)} %bitcast.55, f32[4,8,11,32,128]{4,3,2,1,0:T(8,128)} %bitcast.56, f32[4,8,11,32,128]{4,3,2,1,0:T(8,128)} %bitcast.57, ...), custom_call_target="tpu_custom_call" | custom-call | tf_op jit(solution)/shard_map/update/pallas_call | solution.py:403
  (51 shorter events, 5.5 us)
Async XLA Ops:
  6.5 56.6 %all-gather.5.cloned.1.call-start = ((), (), s32[]{:S(2)}) async-start(), calls=%async_computation | async-start | bytes 1769472 | tf_op jit(solution)/shard_map/all_gather | solution.py:453
  8.2 104.4 %all-gather.7.cloned.1.call-start = ((), (), s32[]{:S(2)}) async-start(), calls=%async_computation.1 | async-start | bytes 5947392 | tf_op jit(solution)/shard_map/all_gather | solution.py:459
  9.5 9.0 %collective-permute-start = (f32[12,32,128]{2,1,0:T(8,128)S(1)}, f32[12,32,128]{2,1,0:T(8,128)S(1)}, u32[]{:S(2)}, u32[]{:S(2)}) collective-permute-start(f32[12,32,128]{2,1,0:T(8,128)S(1)} %get-tuple-element.39), channel_id=1, source_target_pairs={{0,128},{1,129},{2,130},{3,131},{4,132},{5,133},{6,134},{7,135},{8... | collective-permute-start | bytes 589832 | tf_op jit(solution)/shard_map/ppermute | solution.py:419
  15.0 4.8 %collective-permute-start.1 = (f32[12,32,128]{2,1,0:T(8,128)S(1)}, f32[12,32,128]{2,1,0:T(8,128)S(1)}, u32[]{:S(2)}, u32[]{:S(2)}) collective-permute-start(f32[12,32,128]{2,1,0:T(8,128)S(1)} %get-tuple-element.38), channel_id=1, source_target_pairs={{0,192},{1,193},{2,194},{3,195},{4,196},{5,197},{6,198},{7,199},{8... | collective-permute-start | bytes 589832 | tf_op jit(solution)/shard_map/ppermute | solution.py:419
  16.3 6.4 %collective-permute-start.2 = (f32[12,32,128]{2,1,0:T(8,128)S(1)}, f32[12,32,128]{2,1,0:T(8,128)S(1)}, u32[]{:S(2)}, u32[]{:S(2)}) collective-permute-start(f32[12,32,128]{2,1,0:T(8,128)S(1)} %get-tuple-element.37), channel_id=1, source_target_pairs={{0,64},{1,65},{2,66},{3,67},{4,68},{5,69},{6,70},{7,71},{8,72},{9,... | collective-permute-start | bytes 589832 | tf_op jit(solution)/shard_map/ppermute | solution.py:419
  23.5 2.5 %collective-permute-start.3 = (f32[32,128]{1,0:T(8,128)S(1)}, f32[32,128]{1,0:T(8,128)S(1)}, u32[]{:S(2)}, u32[]{:S(2)}) collective-permute-start(f32[32,128]{1,0:T(8,128)S(1)} %get-tuple-element.43), channel_id=1, source_target_pairs={{0,8},{8,0},{1,9},{9,1},{2,10},{10,2},{3,11},{11,3},{4,12},{12,4},... | collective-permute-start | bytes 49160 | tf_op jit(solution)/shard_map/ppermute | solution.py:415
  26.0 14.3 %collective-permute-start.4 = (f32[2,32,128]{2,1,0:T(8,128)S(1)}, f32[2,32,128]{2,1,0:T(8,128)S(1)}, u32[]{:S(2)}, u32[]{:S(2)}) collective-permute-start(f32[2,32,128]{2,1,0:T(8,128)S(1)} %pad_maximum_fusion.6), channel_id=1, source_target_pairs={{0,1},{1,2},{2,3},{3,4},{4,5},{5,6},{6,7},{7,0},{8,15},{9,8},{10,9... | collective-permute-start | bytes 98312 | tf_op jit(solution)/shard_map/ppermute | solution.py:419
  31.6 8.7 %collective-permute-start.5 = (f32[2,32,128]{2,1,0:T(8,128)S(1)}, f32[2,32,128]{2,1,0:T(8,128)S(1)}, u32[]{:S(2)}, u32[]{:S(2)}) collective-permute-start(f32[2,32,128]{2,1,0:T(8,128)S(1)} %pad_maximum_fusion.6), channel_id=1, source_target_pairs={{0,2},{1,3},{2,4},{3,5},{4,6},{5,7},{6,0},{7,1},{8,14},{9,15},{10,... | collective-permute-start | bytes 98312 | tf_op jit(solution)/shard_map/ppermute | solution.py:419
  32.7 7.5 %collective-permute-start.6 = (f32[2,32,128]{2,1,0:T(8,128)S(1)}, f32[2,32,128]{2,1,0:T(8,128)S(1)}, u32[]{:S(2)}, u32[]{:S(2)}) collective-permute-start(f32[2,32,128]{2,1,0:T(8,128)S(1)} %pad_maximum_fusion.6), channel_id=1, source_target_pairs={{0,3},{1,4},{2,5},{3,6},{4,7},{5,0},{6,1},{7,2},{8,13},{9,14},{10,... | collective-permute-start | bytes 98312 | tf_op jit(solution)/shard_map/ppermute | solution.py:419
  33.2 7.1 %collective-permute-start.7 = (f32[32,128]{1,0:T(8,128)S(1)}, f32[32,128]{1,0:T(8,128)S(1)}, u32[]{:S(2)}, u32[]{:S(2)}) collective-permute-start(f32[32,128]{1,0:T(8,128)S(1)} %get-tuple-element.43), channel_id=1, source_target_pairs={{0,4},{1,5},{2,6},{3,7},{4,0},{5,1},{6,2},{7,3},{8,12},{9,13},{10,... | collective-permute-start | bytes 49160 | tf_op jit(solution)/shard_map/ppermute | solution.py:419
  40.3 3.9 %collective-permute-start.8 = (f32[3,32,128]{2,1,0:T(8,128)S(1)}, f32[3,32,128]{2,1,0:T(8,128)S(1)}, u32[]{:S(2)}, u32[]{:S(2)}) collective-permute-start(f32[3,32,128]{2,1,0:T(8,128)S(1)} %pad_maximum_fusion.4), channel_id=1, source_target_pairs={{0,8},{8,0},{1,9},{9,1},{2,10},{10,2},{3,11},{11,3},{4,12},{12,4},... | collective-permute-start | bytes 147464 | tf_op jit(solution)/shard_map/ppermute | solution.py:415
  44.4 6.4 %collective-permute-start.9 = (f32[8,32,128]{2,1,0:T(8,128)S(1)}, f32[8,32,128]{2,1,0:T(8,128)S(1)}, u32[]{:S(2)}, u32[]{:S(2)}) collective-permute-start(f32[8,32,128]{2,1,0:T(8,128)S(1)} %constant_dynamic-slice_fusion.2), channel_id=1, source_target_pairs={{0,16},{16,32},{32,48},{48,0},{1,17},{17,33},{33,49},{49,1},{2,18}... | collective-permute-start | bytes 393224 | tf_op jit(solution)/shard_map/ppermute | solution.py:419
  45.8 8.7 %collective-permute-start.10 = (f32[8,32,128]{2,1,0:T(8,128)S(1)}, f32[8,32,128]{2,1,0:T(8,128)S(1)}, u32[]{:S(2)}, u32[]{:S(2)}) collective-permute-start(f32[8,32,128]{2,1,0:T(8,128)S(1)} %constant_dynamic-slice_fusion.2), channel_id=1, source_target_pairs={{0,32},{16,48},{32,0},{48,16},{1,33},{17,49},{33,1},{49,17},{2,34}... | collective-permute-start | bytes 393224 | tf_op jit(solution)/shard_map/ppermute | solution.py:419
  48.5 6.1 %collective-permute-start.11 = (f32[8,32,128]{2,1,0:T(8,128)S(1)}, f32[8,32,128]{2,1,0:T(8,128)S(1)}, u32[]{:S(2)}, u32[]{:S(2)}) collective-permute-start(f32[8,32,128]{2,1,0:T(8,128)S(1)} %constant_dynamic-slice_fusion.2), channel_id=1, source_target_pairs={{0,48},{16,0},{32,16},{48,32},{1,49},{17,1},{33,17},{49,33},{2,50}... | collective-permute-start | bytes 393224 | tf_op jit(solution)/shard_map/ppermute | solution.py:419
  54.6 5.1 %collective-permute-start.12 = (f32[2,4,32,128]{3,2,1,0:T(8,128)S(1)}, f32[2,4,32,128]{3,2,1,0:T(8,128)S(1)}, u32[]{:S(2)}, u32[]{:S(2)}) collective-permute-start(f32[2,4,32,128]{3,2,1,0:T(8,128)S(1)} %get-tuple-element.46), channel_id=1, source_target_pairs={{0,64},{64,128},{128,192},{192,0},{1,65},{65,129},{129,193},{193,1... | collective-permute-start | bytes 393224 | tf_op jit(solution)/shard_map/ppermute | solution.py:419
  57.1 5.4 %collective-permute-start.13 = (f32[2,4,32,128]{3,2,1,0:T(8,128)S(1)}, f32[2,4,32,128]{3,2,1,0:T(8,128)S(1)}, u32[]{:S(2)}, u32[]{:S(2)}) collective-permute-start(f32[2,4,32,128]{3,2,1,0:T(8,128)S(1)} %get-tuple-element.46), channel_id=1, source_target_pairs={{0,128},{64,192},{128,0},{192,64},{1,129},{65,193},{129,1},{193,65... | collective-permute-start | bytes 393224 | tf_op jit(solution)/shard_map/ppermute | solution.py:419
  57.1 6.0 %collective-permute-start.14 = (f32[2,4,32,128]{3,2,1,0:T(8,128)S(1)}, f32[2,4,32,128]{3,2,1,0:T(8,128)S(1)}, u32[]{:S(2)}, u32[]{:S(2)}) collective-permute-start(f32[2,4,32,128]{3,2,1,0:T(8,128)S(1)} %get-tuple-element.46), channel_id=1, source_target_pairs={{0,192},{64,0},{128,64},{192,128},{1,193},{65,1},{129,65},{193,129... | collective-permute-start | bytes 393224 | tf_op jit(solution)/shard_map/ppermute | solution.py:419
  63.2 7.3 %collective-permute-start.15 = (f32[4,2,4,32,128]{4,3,2,1,0:T(8,128)S(1)}, f32[4,2,4,32,128]{4,3,2,1,0:T(8,128)S(1)}, u32[]{:S(2)}, u32[]{:S(2)}) collective-permute-start(f32[4,2,4,32,128]{4,3,2,1,0:T(8,128)S(1)} %pad_maximum_fusion.2.near_ref), channel_id=1, source_target_pairs={{0,8},{8,0},{1,9},{9,1},{2,10},{10,2},{3,11},{11,3},{4,12},{12,4},... | collective-permute-start | bytes 1572872 | tf_op jit(solution)/shard_map/ppermute | solution.py:415
  65.5 22.6 %copy-start.2 = (s32[5]{0:T(128)}, s32[5]{0:T(128)S(1)}, u32[]{:S(2)}) copy-start(s32[5]{0:T(128)S(1)} %stack.85.ids_ref) | copy-start | bytes 64
  65.5 22.6 %copy-start.3 = (f32[24,128,128]{2,1,0:T(8,128)S(1)}, f32[24,128,128]{2,1,0:T(8,128)}, u32[]{:S(2)}) copy-start(f32[24,128,128]{2,1,0:T(8,128)} %all-gather.5.cloned.1.call-done) | copy-start | bytes 4718596
  65.5 19.2 %collective-permute-start.16 = (f32[4,4,32,128]{3,2,1,0:T(8,128)S(1)}, f32[4,4,32,128]{3,2,1,0:T(8,128)S(1)}, u32[]{:S(2)}, u32[]{:S(2)}) collective-permute-start(f32[4,4,32,128]{3,2,1,0:T(8,128)S(1)} %slice.76), channel_id=1, source_target_pairs={{0,64},{64,128},{128,192},{192,0},{1,65},{65,129},{129,193},{193,1... | collective-permute-start | bytes 786440 | tf_op jit(solution)/shard_map/ppermute | solution.py:419
  67.3 17.4 %collective-permute-start.17 = (f32[4,4,32,128]{3,2,1,0:T(8,128)S(1)}, f32[4,4,32,128]{3,2,1,0:T(8,128)S(1)}, u32[]{:S(2)}, u32[]{:S(2)}) collective-permute-start(f32[4,4,32,128]{3,2,1,0:T(8,128)S(1)} %slice.76), channel_id=1, source_target_pairs={{0,128},{64,192},{128,0},{192,64},{1,129},{65,193},{129,1},{193,65... | collective-permute-start | bytes 786440 | tf_op jit(solution)/shard_map/ppermute | solution.py:419
  69.6 15.1 %collective-permute-start.18 = (f32[4,4,32,128]{3,2,1,0:T(8,128)S(1)}, f32[4,4,32,128]{3,2,1,0:T(8,128)S(1)}, u32[]{:S(2)}, u32[]{:S(2)}) collective-permute-start(f32[4,4,32,128]{3,2,1,0:T(8,128)S(1)} %slice.76), channel_id=1, source_target_pairs={{0,192},{64,0},{128,64},{192,128},{1,193},{65,1},{129,65},{193,129... | collective-permute-start | bytes 786440 | tf_op jit(solution)/shard_map/ppermute | solution.py:419
  84.8 3.2 %collective-permute-start.19 = (f32[4,4,4,32,128]{4,3,2,1,0:T(8,128)S(1)}, f32[4,4,4,32,128]{4,3,2,1,0:T(8,128)S(1)}, u32[]{:S(2)}, u32[]{:S(2)}) collective-permute-start(f32[4,4,4,32,128]{4,3,2,1,0:T(8,128)S(1)} %pad_maximum_fusion.near_ref), channel_id=1, source_target_pairs={{0,8},{8,0},{1,9},{9,1},{2,10},{10,2},{3,11},{11,3},{4,12},{12,4},... | collective-permute-start | bytes 3145736 | tf_op jit(solution)/shard_map/ppermute | solution.py:415
  110.1 1.2 copy-start
  111.2 0.7 copy-start.1
Sparse Core Ops, SparseCore 0:
  9.1 40.7 all-gather.4
  52.5 60.0 all-gather.6
